TPU v7x, 256 devices: a whole 4x4x8 slice. The times are simulated.
256 devices in a mesh: dp: 8 (over x, core), expert: 32 (over y, z).
Axes of the slice: x: 4, y: 4, z: 8, core: 2. Of those that a mesh axis runs over, the one named last changes fastest.
Arguments:
- frames: bfloat16 [32768, 1024], P(('dp', 'expert')), may hold values from -6 to 6
- lengths: int32 [256, 4], P(('dp', 'expert')), may hold values from 1 to 80, 128 in all within a row
- w_qkv: bfloat16 [1024, 3072], P('expert'), may hold values from -4 to 4
- w_out: bfloat16 [1024, 1024], P('expert'), may hold values from -0.1875 to 0.1875
- conv_w: float32 [31, 1024], replicated, may hold values from -1 to 1
- w_router: bfloat16 [1024, 64], replicated, may hold values from -0.1875 to 0.1875
- expert_ids: int32 [32768, 2], P(('dp', 'expert')), may hold values from 0 to 63, all different within a row; in each aligned block of 128 rows (0 to 127, 128 to 255, ...) at most 5 rows name the same one
- w_up: bfloat16 [64, 1024, 4096], P('expert', None, 'dp'), may hold values from -0.1875 to 0.1875
- w_down: bfloat16 [64, 4096, 1024], P('expert', 'dp'), may hold values from -0.09375 to 0.09375
Outputs:
- block_out: bfloat16 [32768, 1024], P(('dp', 'expert'))
Inputs may be any that keep to these rules, and one draw needn't show every extreme that they name: `expert_ids`: among the rows of one device no expert is named by more than 5 rows. `lengths`: each row sums to 128.
All inputs are finite; a program needn't handle non-finite values.
Results may differ from a plain program's by a relative error of at most 0.017.
Values may be sent and summed in bfloat16 or wider, within the bound.
A program may use at most 128 MiB of HBM per device.

v0:
```python
import jax
import jax.numpy as jnp
from jax import lax
from jax.sharding import PartitionSpec as P

HEADS = 16
HEAD_DIM = 64
BLK = 128
TOP = 2
EXP_DEV = 2


def normalize(values):
    mean_value = jnp.mean(values, axis=-1, keepdims=True)
    centred = values - mean_value
    variance = jnp.mean(centred * centred, axis=-1, keepdims=True)
    return centred * lax.rsqrt(variance + 1e-05)


def segment_rows(row_lengths, count_rows):
    ends = jnp.cumsum(row_lengths)
    offsets = jnp.arange(count_rows, dtype=jnp.int32)
    return jnp.sum((offsets[:, None] >= ends[None, :]).astype(jnp.int32), axis=1)


def depthwise(normed, kernel, segments):
    half_width = (kernel.shape[0] - 1) // 2
    count_rows = normed.shape[0]
    padded = jnp.pad(normed, ((half_width, half_width), (0, 0)))
    seg_padded = jnp.pad(segments, (half_width, half_width), constant_values=-1)
    total = jnp.zeros_like(normed)
    for offset in range(kernel.shape[0]):
        window = padded[offset : offset + count_rows]
        same = (seg_padded[offset : offset + count_rows] == segments).astype(normed.dtype)
        total = total + kernel[offset][None, :] * window * same[:, None]
    return total


def block_attention(qkv, segments):
    count_rows = qkv.shape[0]
    blocks = count_rows // BLK
    pieces = qkv.reshape(blocks, BLK, 3, HEADS, HEAD_DIM)
    scores = jnp.einsum(
        "cqhd,ckhd->chqk", pieces[:, :, 0], pieces[:, :, 1], preferred_element_type=jnp.float32
    ) * HEAD_DIM ** (-0.5)
    seg_blocks = segments.reshape(blocks, BLK)
    allowed = seg_blocks[:, :, None] == seg_blocks[:, None, :]
    scores = jnp.where(allowed[:, None], scores, -1e30)
    highest = jnp.max(scores, axis=-1, keepdims=True)
    expo = jnp.exp(scores - highest)
    probs = (expo / jnp.sum(expo, axis=-1, keepdims=True)).astype(jnp.bfloat16)
    mixed = jnp.einsum(
        "chqk,ckhd->cqhd", probs, pieces[:, :, 2], preferred_element_type=jnp.float32
    )
    return mixed.astype(jnp.bfloat16).reshape(count_rows, HEADS * HEAD_DIM)


def local(frames, lengths, w_qkv, w_out, conv_w, w_router, expert_ids, w_up, w_down):
    full_qkv, full_out = (
        lax.all_gather(w_qkv, "expert", axis=0, tiled=True),
        lax.all_gather(w_out, "expert", axis=0, tiled=True),
    )
    count_rows = frames.shape[0]
    feature_count = frames.shape[1]
    segments = segment_rows(lengths[0], count_rows)
    normed_in = normalize(frames.astype(jnp.float32)).astype(jnp.bfloat16)
    qkv = jnp.dot(normed_in, full_qkv, preferred_element_type=jnp.float32).astype(jnp.bfloat16)
    mixed = block_attention(qkv, segments)
    first = (
        frames.astype(jnp.float32) + jnp.dot(mixed, full_out, preferred_element_type=jnp.float32)
    ).astype(jnp.bfloat16)
    conv_in = normalize(first.astype(jnp.float32))
    conv_out = depthwise(conv_in, conv_w, segments)
    second = (first.astype(jnp.float32) + jax.nn.silu(conv_out)).astype(jnp.bfloat16)
    hidden = normalize(second.astype(jnp.float32)).astype(jnp.bfloat16)
    logits = jnp.dot(hidden, w_router, preferred_element_type=jnp.float32)
    gates = jax.nn.sigmoid(jnp.take_along_axis(logits, expert_ids, axis=1))
    group_size = lax.axis_size("expert")
    experts_all = EXP_DEV * group_size
    capacity = max(2, count_rows * TOP * 5 // (4 * experts_all))
    flat_ids = expert_ids.reshape(-1)
    onehot = (flat_ids[:, None] == jnp.arange(experts_all, dtype=jnp.int32)[None, :]).astype(
        jnp.int32
    )
    slots = jnp.sum(jnp.cumsum(onehot, axis=0) * onehot, axis=1) - 1
    target = flat_ids // EXP_DEV
    local_expert = flat_ids % EXP_DEV
    position = target * capacity + slots
    source_row = jnp.arange(flat_ids.shape[0], dtype=jnp.int32) // TOP
    table = (
        jnp.full((group_size * capacity, EXP_DEV), count_rows, jnp.int32)
        .at[position, local_expert]
        .set(source_row)
    )
    padded = jnp.concatenate([hidden, jnp.zeros((1, feature_count), jnp.bfloat16)], axis=0)
    outgoing = padded[table]
    incoming = lax.all_to_all(outgoing, "expert", split_axis=0, concat_axis=0, tiled=True)
    upward = jnp.einsum(
        "ned,edf->nef",
        lax.all_gather(incoming, "dp", axis=0, tiled=True),
        w_up,
        preferred_element_type=jnp.float32,
    )
    activated = jax.nn.silu(upward).astype(jnp.bfloat16)
    summed = lax.psum_scatter(
        jnp.einsum("nef,efd->ned", activated, w_down, preferred_element_type=jnp.float32).astype(
            jnp.bfloat16
        ),
        "dp",
        scatter_dimension=0,
        tiled=True,
    )
    returned = lax.all_to_all(summed, "expert", split_axis=0, concat_axis=0, tiled=True)
    picked = returned[position, local_expert].reshape(count_rows, TOP, feature_count)
    combined = second.astype(jnp.float32) + jnp.sum(
        gates[:, :, None] * picked.astype(jnp.float32), axis=1
    )
    return combined.astype(jnp.bfloat16)


def solution(mesh):
    in_specs = (
        P(("dp", "expert"), None),
        P(("dp", "expert"), None),
        P("expert", None),
        P("expert", None),
        P(),
        P(),
        P(("dp", "expert"), None),
        P("expert", None, "dp"),
        P("expert", "dp", None),
    )
    out_specs = P(("dp", "expert"), None)
    return jax.shard_map(local, mesh=mesh, in_specs=in_specs, out_specs=out_specs, check_vma=False)
```

profile of v0, /device:TPU:7, one launch (start us, length us, event | category | flops | bytes accessed | tf_op | source)
XLA Modules:
  0.0 344.7 jit_solution(10503105305009549774)
XLA Ops:
  6.5 0.7 all-gather.4.cloned.1.call-update
  7.3 0.7 all-gather.6.cloned.1.call-update
  8.1 0.8 copy.63
  8.9 0.1 eq.174
  9.0 0.1 eq.170
  9.1 0.1 reshape.349
  9.3 0.8 reduce-window.18
  10.1 0.6 reduce-window.19
  10.7 0.2 slice_reduce_fusion
  11.1 12.2 %scatter_fusion = s32[160,2]{0,1:T(2,128)S(1)} fusion(s32[160,2]{0,1:T(2,128)S(1)} %broadcast_in_dim.22, s32[256]{0:T(256)S(1)} %bitcast.106, s32[256]{0:T(256)S(1)} %and_select_fusion.2), kind=kCustom, calls=%fused_computation.3 | custom fusion | bytes 5120 | tf_op jit(solution)/shard_map/scatter | solution.py:93
  23.5 0.1 reshape.354
  23.7 1.1 convert_reduce_fusion.1
  24.8 1.2 fusion.18
  26.3 1.1 fusion.124
  27.4 1.4 fusion.123
  28.8 72.4 %all-gather.4.cloned.1.call-done = bf16[1024,3072]{1,0:T(8,128)(2,1)} async-done(((bf16[32,3072]{1,0:T(8,128)(2,1)}), bf16[1024,3072]{1,0:T(8,128)(2,1)}) %all-gather.4.cloned.1.call-update) | async-done | bytes 6291472 | tf_op jit(solution)/shard_map/all_gather | solution.py:60
  101.2 3.9 %convolution_convert_fusion.1 = bf16[128,3072]{1,0:T(8,128)(2,1)S(1)} fusion(bf16[1024,3072]{1,0:T(8,128)(2,1)} %all-gather.4.cloned.1.call-done, bf16[128,1024]{1,0:T(8,128)(2,1)} %param.9, f32[128]{0:T(128)S(1)} %add_rsqrt_fusion.2, f32[128]{0:T(128)S(1)} %broadcast_multiply_fusion.2), kind=kOutput, calls=%fused_computation.13 | convolution fusion | flops 806223872 | bytes 7341056 | tf_op jit(solution)/shard_map/dot_general | solution.py:67
  105.2 1.2 copy.58
  106.4 1.5 fusion.125
  107.9 2.4 fusion.9
  110.3 2.0 convolution_convert_fusion.2
  112.3 62.8 %all-gather.6.cloned.1.call-done = bf16[1024,1024]{1,0:T(8,128)(2,1)} async-done(((bf16[32,1024]{1,0:T(8,128)(2,1)}), bf16[1024,1024]{1,0:T(8,128)(2,1)}) %all-gather.6.cloned.1.call-update) | async-done | bytes 2097168 | tf_op jit(solution)/shard_map/all_gather | solution.py:61
  175.2 2.1 fusion.126
  177.3 0.2 multiply_reduce_fusion.1
  177.6 0.1 subtract_multiply_fusion
  177.7 4.2 %convert_reduce_fusion = (f32[128]{0:T(128)S(1)}, bf16[128,1024]{1,0:T(8,128)(2,1)S(1)}) fusion(f32[128,1024]{1,0:T(8,128)S(1)} %get-tuple-element.72, f32[128]{0:T(128)S(1)} %get-tuple-element.70, f32[1024]{0:T(1024)S(1)} %bitcast.121, f32[128]{0:T(128)S(1)} %get-tuple-element.69, f32[1024]{0:T(1024)S(1)} %bitcast.122, f32[128]{0:T(128)S(1)} %get-tuple-element.42, ...), kind=kLoop, calls=%fused_computation.57 | loop fusion | flops 12976000 | bytes 1453568 | tf_op jit(solution)/shard_map/reduce_sum | solution.py:14
  181.9 0.2 fusion.16
  182.1 0.2 fusion.17
  182.4 0.7 copy-done.2
  183.1 2.1 gather_fusion
  185.2 1.1 reshape.353
  186.3 18.3 %all_to_all.10 = bf16[160,2,1024]{2,1,0:T(2,128)(2,1)S(1)} all-to-all(bf16[160,2,1024]{2,1,0:T(2,128)(2,1)} %reshape.353), channel_id=1, replica_groups=mesh['dp'=8,'expert'=32] {'expert'}, dimensions={0} | all-to-all | bytes 1310720 | tf_op jit(solution)/shard_map/all_to_all | solution.py:97
  204.6 1.0 copy.68
  205.7 0.2 reduce-scatter.2.cloned.1.call-start
  205.9 41.2 %all-gather.8.cloned.1.call-done = bf16[1280,2,1024]{2,0,1:T(8,128)(2,1)} async-done(((bf16[160,2,1024]{2,0,1:T(8,128)(2,1)}), bf16[1280,2,1024]{2,0,1:T(8,128)(2,1)}) %all-gather.8.cloned.1.call-update) | async-done | bytes 5242896 | tf_op jit(solution)/shard_map/all_gather | solution.py:100
  247.1 9.7 %fusion.5 = bf16[1280,2,1024]{2,0,1:T(8,128)(2,1)} fusion(bf16[2,512,1024]{2,1,0:T(8,128)(2,1)S(1)} %copy-done, bf16[1280,2,1024]{2,0,1:T(8,128)(2,1)} %all-gather.8.cloned.1.call-done, bf16[2,1024,512]{2,1,0:T(8,128)(2,1)} %param.16), kind=kOutput, calls=%fused_computation.12 | convolution fusion | flops 5377884160 | bytes 14680064 | tf_op jit(solution)/shard_map/nef,efd->ned/dot_general | solution.py:106
  256.9 43.2 %reduce-scatter.2.cloned.1.call-done = bf16[160,2,1024]{2,0,1:T(8,128)(2,1)} async-done(((bf16[1280,2,1024]{2,0,1:T(8,128)(2,1)}), bf16[160,2,1024]{2,0,1:T(8,128)(2,1)}) %reduce-scatter.2.cloned.1.call-update) | async-done | bytes 655376 | tf_op jit(solution)/shard_map/reduce_scatter | solution.py:105
  300.1 2.6 copy.69
  302.7 9.6 %all-to-all-start.1 = ((bf16[160,2,1024]{2,1,0:T(2,128)(2,1)}), bf16[160,2,1024]{2,1,0:T(2,128)(2,1)S(1)}, u32[]{:S(2)}, u32[]{:S(2)}) async-start(bf16[160,2,1024]{2,1,0:T(2,128)(2,1)} %copy.69), calls=%async_computation.2 | async-start | bytes 1310720 | tf_op jit(solution)/shard_map/all_to_all | solution.py:113
  312.4 0.1 reshape.366
  312.6 0.2 fusion.127
  312.8 2.0 gather_fusion.2
  314.8 0.1 reshape.369
  315.1 16.3 %all-to-all-done.1 = bf16[160,2,1024]{2,1,0:T(2,128)(2,1)S(1)} async-done(((bf16[160,2,1024]{2,1,0:T(2,128)(2,1)}), bf16[160,2,1024]{2,1,0:T(2,128)(2,1)S(1)}, u32[]{:S(2)}, u32[]{:S(2)}) %all-to-all-start.1) | async-done | bytes 655392 | tf_op jit(solution)/shard_map/all_to_all | solution.py:113
  331.4 3.0 gather_fusion.1
  334.4 1.7 reshape.351
  336.1 1.3 multiply_reduce_fusion
  337.4 0.8 fusion.20
  (44 shorter events, 1.2 us)
Async XLA Ops:
  6.5 240.6 %copy-start = (bf16[2,512,1024]{2,1,0:T(8,128)(2,1)S(1)}, bf16[2,512,1024]{2,1,0:T(8,128)(2,1)}, u32[]{:S(2)}) copy-start(bf16[2,512,1024]{2,1,0:T(8,128)(2,1)} %param.17) | copy-start | bytes 6291460
  6.5 94.7 %all-gather.4.cloned.1.call-start = ((), (), s32[]{:S(2)}) async-start(), calls=%async_computation.3 | async-start | bytes 6488064 | tf_op jit(solution)/shard_map/all_gather | solution.py:60
  7.3 167.9 %all-gather.6.cloned.1.call-start = ((), (), s32[]{:S(2)}) async-start(), calls=%async_computation.4 | async-start | bytes 2162688 | tf_op jit(solution)/shard_map/all_gather | solution.py:61
  8.0 239.1 %all-gather.8.cloned.1.call-start = ((), (), s32[]{:S(2)}) async-start(), calls=%async_computation.5 | async-start | bytes 5898240 | tf_op jit(solution)/shard_map/all_gather | solution.py:100
  105.2 70.0 %copy-start.1 = (bf16[128,1024]{1,0:T(8,128)(2,1)S(1)}, bf16[128,1024]{1,0:T(8,128)(2,1)}, u32[]{:S(2)}) copy-start(bf16[128,1024]{1,0:T(8,128)(2,1)} %param.9) | copy-start | bytes 786436
  182.4 0.7 copy-start.2
  205.7 94.4 %reduce-scatter.2.cloned.1.call-start = ((), (), s32[]{:S(2)}) async-start(), calls=%async_computation.6 | async-start | bytes 5898240 | tf_op jit(solution)/shard_map/reduce_scatter | solution.py:105
  256.9 55.4 %copy-start.5 = (s32[128,2]{0,1:T(2,128)S(1)}, s32[128,2]{0,1:T(2,128)}, u32[]{:S(2)}) copy-start(s32[128,2]{0,1:T(2,128)} %param.15) | copy-start | bytes 3076
  256.9 55.7 %copy-start.3 = (bf16[128,1024]{1,0:T(8,128)(2,1)S(1)}, bf16[128,1024]{1,0:T(8,128)(2,1)}, u32[]{:S(2)}) copy-start(bf16[128,1024]{1,0:T(8,128)(2,1)} %copy-done.2) | copy-start | bytes 786436
  256.9 55.7 %copy-start.4 = (bf16[1024,64]{0,1:T(8,128)(2,1)S(1)}, bf16[1024,64]{0,1:T(8,128)(2,1)}, u32[]{:S(2)}) copy-start(bf16[1024,64]{0,1:T(8,128)(2,1)} %param.14) | copy-start | bytes 393220
  302.7 28.7 %all-to-all-start.1 = ((bf16[160,2,1024]{2,1,0:T(2,128)(2,1)}), bf16[160,2,1024]{2,1,0:T(2,128)(2,1)S(1)}, u32[]{:S(2)}, u32[]{:S(2)}) async-start(bf16[160,2,1024]{2,1,0:T(2,128)(2,1)} %copy.69), calls=%async_computation.2 | async-start | bytes 1310720 | tf_op jit(solution)/shard_map/all_to_all | solution.py:113
Sparse Core Ops, SparseCore 0:
  9.9 91.2 all-gather.3
  103.8 71.3 all-gather.5
  205.8 41.3 all-gather.7
  257.0 43.0 reduce-scatter.1
where the time goes:
time: 346 us; the launch traced here: 345 us
  waiting for transfers between devices  237 us (68%)
  local copies, waits for them, and re-layouts  32.4 us (9%)
  matrix products  22 us (6%)
  blocking collectives  18.3 us (5%)
  between operations  13.4 us (4%)
  other arithmetic  11.4 us (3%)
  starting transfers between devices  9.87 us (3%)
    all_gather x1, waiting for transfers between devices, local(): lax.all_gather(w_qkv, 'expert', axis=0, tiled=True)  72.4 us
    all_gather x1, waiting for transfers between devices, local(): lax.all_gather(w_out, 'expert', axis=0, tiled=True)  62.8 us
    reduce_scatter x1, waiting for transfers between devices, local(): lax.psum_scatter(jnp.einsum('nef,efd->ned', activated, w_down, preferred_...  43.2 us
    all_gather x1, waiting for transfers between devices, local(): lax.all_gather(incoming, 'dp', axis=0, tiled=True)  41.2 us
    all_to_all x1, blocking collectives, local(): lax.all_to_all(outgoing, 'expert', split_axis=0, concat_axis=0, tiled=True)  18.3 us
    all_to_all x1, waiting for transfers between devices, local(): lax.all_to_all(summed, 'expert', split_axis=0, concat_axis=0, tiled=True)  16.3 us
    scatter x1, local copies, waits for them, and re-layouts, local(): table = jnp.full((group_size * capacity, EXP_DEV), count_rows, jnp.int32)...  12.2 us
    dot_general x1, matrix products, local(): jnp.einsum('nef,efd->ned', activated, w_down, preferred_element_type=jnp....  9.73 us
  transfers between devices with their start and end apart: 5, of which 5 were waited for; matrix products, arithmetic and copies ran while one was open for 10% of the time, Pallas kernels for 0%

commit v1 on v0

v1 whole, which is shorter than its diff:
```python
import functools

import jax
import jax.numpy as jnp
from jax import lax
from jax.experimental import pallas as pl
from jax.experimental.pallas import tpu as pltpu
from jax.sharding import PartitionSpec as P

HEADS = 16
HEAD_DIM = 64
ROWS = 128
D = 1024
TOP = 2
NX, NY, NZ = 4, 4, 8
EXPERT_DEVS = NY * NZ
CAP = 5
CELL = 2 * CAP
SUB = CELL * D // 128
QCOLS = 384
OCOLS = 512
WCOLS = QCOLS + OCOLS
XROWS = ROWS + 16
MESH = pl.DeviceIdType.MESH
ANY = pl.BlockSpec(memory_space=pl.ANY)
VMEM = pl.BlockSpec(memory_space=pltpu.VMEM)
BF = jnp.bfloat16
F32 = jnp.float32


def normalize(values):
    mean_value = jnp.mean(values, axis=-1, keepdims=True)
    centred = values - mean_value
    variance = jnp.mean(centred * centred, axis=-1, keepdims=True)
    return centred * lax.rsqrt(variance + 1e-05)


class Place:
    def __init__(self):
        dp, ex = lax.axis_index("dp"), lax.axis_index("expert")
        self.dp, self.ex = dp, ex
        self.x, self.c = dp // 2, dp % 2
        self.y, self.z = ex // NZ, ex % NZ

    def at(self, dx=0, dy=0, dz=0, other=False):
        x, y, z = (self.x + dx + NX) % NX, (self.y + dy + NY) % NY, (self.z + dz + NZ) % NZ
        c = 1 - self.c if other else self.c
        return (x * 2 + c, y * NZ + z)


class Sends:
    def __init__(self, send_sem, recv_sem):
        self.send_sem, self.recv_sem, self.copies = send_sem, recv_sem, []

    def start(self, src, dst, device):
        at = len(self.copies)
        copy = pltpu.make_async_remote_copy(
            src_ref=src,
            dst_ref=dst,
            send_sem=self.send_sem.at[at],
            recv_sem=self.recv_sem.at[at],
            device_id=device,
            device_id_type=MESH,
        )
        copy.start()
        self.copies.append(copy)
        return copy

    def finish(self):
        for copy in self.copies:
            copy.wait_send()


def greet(devices):
    barrier = pltpu.get_barrier_semaphore()
    for device in devices:
        pl.semaphore_signal(barrier, inc=1, device_id=device, device_id_type=MESH)
    pl.semaphore_wait(barrier, len(devices))


def run_tasks(tasks):
    waiting = [(task, next(task, None)) for task in tasks]
    while waiting:
        later = []
        for task, copy in waiting:
            if copy is None:
                continue
            copy.wait_recv()
            later.append((task, next(task, None)))
        waiting = later


GATHER_SENDS = 64


def gather_kernel(
    xc, wqkv, wout, wup, wdn, xg, wg, up2, dn2, send_sem, recv_sem, local_sem
):
    me = Place()
    x, c, y, z, dp = me.x, me.c, me.y, me.z, me.dp
    sib = me.at(other=True)
    xr, xl = me.at(dx=1), me.at(dx=-1)
    yu, yd = me.at(dy=1), me.at(dy=-1)
    zu, zd = me.at(dz=1), me.at(dz=-1)
    locals_ = []

    def local(src, dst):
        copy = pltpu.make_async_copy(src, dst, local_sem.at[len(locals_)])
        copy.start()
        locals_.append(copy)

    for part in range(3):
        columns = pl.ds(pl.multiple_of(part * D + dp * 128, 128), 128)
        local(wqkv.at[:, columns], wg.at[y, z, :, pl.ds(part * 128, 128)])
    local(
        wout.at[:, pl.ds(pl.multiple_of(c * OCOLS, 128), OCOLS)],
        wg.at[y, z, :, pl.ds(QCOLS, OCOLS)],
    )
    local(xc, xg.at[dp])
    local(wup.at[c], up2.at[c])
    local(wdn.at[c], dn2.at[c])

    greet([sib, xr, xl, yu, yd, zu, zd])
    sends = Sends(send_sem, recv_sem)
    start = sends.start
    first_sib = start(xc, xg.at[dp], sib)
    to_r = start(xc, xg.at[dp], xr)
    to_l = start(xc, xg.at[dp], xl)
    for copy in locals_[:4]:
        copy.wait()

    def yy(d):
        return (y + d + NY) % NY

    def zz(d):
        return (z + d + NZ) % NZ

    def x_chain():
        left = xg.at[((x + NX - 1) % NX) * 2 + c]
        right = xg.at[((x + 1) % NX) * 2 + c]
        across = xg.at[((x + 2) % NX) * 2 + c]
        yield to_r
        low = left.at[pl.ds(0, 80)]
        relay_r = start(low, low, xr)
        sib1 = start(left, left, sib)
        yield to_l
        high = right.at[pl.ds(80, 64)]
        relay_l = start(high, high, xl)
        sib2 = start(right, right, sib)
        yield relay_r
        yield relay_l
        sib3 = start(across, across, sib)
        for copy in (first_sib, sib1, sib2, sib3):
            yield copy

    def z_first():
        def block(dy, dz):
            return wg.at[yy(dy), zz(dz), pl.ds(0, 16)]

        spread = []

        def available(dz):
            spread.append(
                (dz, start(block(0, dz), block(0, dz), yu), start(block(0, dz), block(0, dz), yd))
            )

        up = start(block(0, 0), block(0, 0), zu)
        down = start(block(0, 0), block(0, 0), zd)
        available(0)
        for s in range(1, 4):
            yield up
            up = start(block(0, -s), block(0, -s), zu)
            available(-s)
            yield down
            if s < 3:
                down = start(block(0, s), block(0, s), zd)
            available(s)
        yield up
        available(4)
        last = []
        for dz, to_u, to_d in spread:
            yield to_u
            yield to_d
            if dz in (0, 1, 2, 3):
                last.append(start(block(-1, dz), block(-1, dz), yu))
            else:
                last.append(start(block(1, dz), block(1, dz), yd))
        for copy in last:
            yield copy

    def y_first():
        def block(dy):
            return wg.at[yy(dy), z, pl.ds(16, 16)]

        def bundle(dz, first=0, count=NY):
            return wg.at[pl.ds(first, count), zz(dz), pl.ds(16, 16)]

        to_u = start(block(0), block(0), yu)
        to_d = start(block(0), block(0), yd)
        yield to_u
        relay = start(block(-1), block(-1), yu)
        yield to_d
        yield relay
        up = start(bundle(0), bundle(0), zu)
        down = start(bundle(0), bundle(0), zd)
        for s in range(1, 4):
            yield up
            if s < 3:
                up = start(bundle(-s), bundle(-s), zu)
            else:
                up = start(bundle(-s, 0, 2), bundle(-s, 0, 2), zu)
            yield down
            if s < 3:
                down = start(bundle(s), bundle(s), zd)
            else:
                down = start(bundle(s, 2, 2), bundle(s, 2, 2), zd)
        yield up
        yield down

    def swap():
        one = start(wup.at[1 - c], up2.at[c], sib)
        two = start(wdn.at[1 - c], dn2.at[c], sib)
        yield from ()
        swaps.extend((one, two))

    swaps = []
    run_tasks([y_first(), z_first(), x_chain(), swap()])
    for copy in swaps:
        copy.wait_recv()
    for copy in locals_[4:]:
        copy.wait()
    sends.finish()


def gather_all(xc, w_qkv, w_out, w_up, w_down):
    return pl.pallas_call(
        gather_kernel,
        out_shape=(
            jax.ShapeDtypeStruct((8, XROWS, D), BF),
            jax.ShapeDtypeStruct((NY, NZ, 32, WCOLS), BF),
            jax.ShapeDtypeStruct(w_up.shape, BF),
            jax.ShapeDtypeStruct(w_down.shape, BF),
        ),
        in_specs=[ANY] * 5,
        out_specs=[ANY] * 4,
        scratch_shapes=[
            pltpu.SemaphoreType.DMA((GATHER_SENDS,)),
            pltpu.SemaphoreType.DMA((GATHER_SENDS,)),
            pltpu.SemaphoreType.DMA((8,)),
        ],
        compiler_params=pltpu.CompilerParams(collective_id=0, has_side_effects=True),
        name="gather",
    )(xc, w_qkv, w_out, w_up, w_down)


def attention_kernel(x_ref, w_ref, out_ref):
    block = x_ref[0]
    qkv = jnp.dot(block[:ROWS], w_ref[...], preferred_element_type=F32).astype(BF)
    marks = block[ROWS : ROWS + 4, :ROWS].astype(F32)
    same = lax.dot_general(marks, marks, (((0,), (0,)), ((), ())), preferred_element_type=F32)
    allowed = same > 0.5
    for h in range(2):
        q = qkv[:, h * 64 : h * 64 + 64]
        k = qkv[:, 128 + h * 64 : 128 + h * 64 + 64]
        v = qkv[:, 256 + h * 64 : 256 + h * 64 + 64]
        scores = lax.dot_general(q, k, (((1,), (1,)), ((), ())), preferred_element_type=F32)
        scores = jnp.where(allowed, scores * HEAD_DIM ** (-0.5), -1e30)
        highest = jnp.max(scores, axis=-1, keepdims=True)
        expo = jnp.exp(scores - highest)
        probs = (expo / jnp.sum(expo, axis=-1, keepdims=True)).astype(BF)
        mixed = jnp.dot(probs, v, preferred_element_type=F32).astype(BF)
        out_ref[0, :, h * 64 : h * 64 + 64] = mixed


def attention(xg, wg):
    return pl.pallas_call(
        attention_kernel,
        grid=(8,),
        out_shape=jax.ShapeDtypeStruct((8, ROWS, 128), BF),
        in_specs=[
            pl.BlockSpec((1, XROWS, D), lambda i: (i, 0, 0)),
            pl.BlockSpec((D, QCOLS), lambda i: (0, 0)),
        ],
        out_specs=pl.BlockSpec((1, ROWS, 128), lambda i: (i, 0, 0)),
        compiler_params=pltpu.CompilerParams(vmem_limit_bytes=24 << 20),
        name="attention",
    )(xg, wg.reshape(D, WCOLS))


def heads_kernel(mixed, wg, out, wo, send_sem, recv_sem, local_sem):
    me = Place()
    dp, c = me.dp, me.c
    peers = [((dp + o) % 8, me.ex) for o in range(1, 8)]
    sib = me.at(other=True)
    half = pl.ds(pl.multiple_of(c * OCOLS, 128), OCOLS)
    mine = wg.at[:, :, :, pl.ds(QCOLS, OCOLS)]
    keep = pltpu.make_async_copy(mixed.at[dp], out.at[dp], local_sem.at[0])
    keep.start()
    keep_w = pltpu.make_async_copy(mine, wo.at[:, :, :, half], local_sem.at[1])
    keep_w.start()
    greet(peers)
    sends = Sends(send_sem, recv_sem)
    for o in range(1, 8):
        sends.start(mixed.at[(dp + o) % 8], out.at[dp], peers[o - 1])
    sends.start(mine, wo.at[:, :, :, half], sib)
    for copy in sends.copies:
        copy.wait_recv()
    keep.wait()
    keep_w.wait()
    sends.finish()


def heads_back(mixed, wg):
    return pl.pallas_call(
        heads_kernel,
        out_shape=(
            jax.ShapeDtypeStruct((8, ROWS, 128), BF),
            jax.ShapeDtypeStruct((NY, NZ, 32, D), BF),
        ),
        in_specs=[ANY] * 2,
        out_specs=[ANY] * 2,
        scratch_shapes=[
            pltpu.SemaphoreType.DMA((8,)),
            pltpu.SemaphoreType.DMA((8,)),
            pltpu.SemaphoreType.DMA((2,)),
        ],
        compiler_params=pltpu.CompilerParams(collective_id=1, has_side_effects=True),
        name="heads_back",
    )(mixed, wg)


PLANE = [(dy, dz) for dz in range(NZ) for dy in range(NY) if (dy, dz) != (0, 0)]


def plane_peers(me):
    return [me.at(dy=dy, dz=dz) for dy, dz in PLANE]


def dispatch_kernel(cells, out, send_sem, recv_sem, local_sem):
    me = Place()
    x, y, z = me.x, me.y, me.z
    xr, xl = me.at(dx=1), me.at(dx=-1)
    keep = pltpu.make_async_copy(cells.at[y, z], out.at[x, z, y], local_sem.at[0])
    keep.start()
    greet(plane_peers(me) + [xr, xl])
    sends = Sends(send_sem, recv_sem)
    start = sends.start
    order = (0, 1, 7, 2, 6, 3, 5, 4)
    direct = {}
    for dz in order:
        for dy in range(NY):
            if (dy, dz) != (0, 0):
                src = cells.at[(y + dy) % NY, (z + dz) % NZ]
                direct[dy, dz] = start(src, out.at[x, z, y], me.at(dy=dy, dz=dz))
    keep.wait()
    right, left = (x + 1) % NX, (x + NX - 1) % NX
    sideways, last = [], []

    def relay(i):
        group = (z - order[i] + NZ) % NZ
        to_r, to_l = sideways[i]
        to_r.wait_recv()
        low = out.at[left, group, pl.ds(0, 2)]
        last.append(start(low, low, xr))
        to_l.wait_recv()
        high = out.at[right, group, pl.ds(2, 2)]
        last.append(start(high, high, xl))

    for i, dz in enumerate(order):
        for dy in range(NY):
            if (dy, dz) != (0, 0):
                direct[dy, dz].wait_recv()
        block = out.at[x, (z - dz + NZ) % NZ]
        sideways.append((start(block, block, xr), start(block, block, xl)))
        if i >= 1:
            relay(i - 1)
    relay(NZ - 1)
    for copy in last:
        copy.wait_recv()
    sends.finish()


def dispatch(cells):
    count = 31 + 4 * NZ
    return pl.pallas_call(
        dispatch_kernel,
        out_shape=jax.ShapeDtypeStruct((NX, NZ, NY, SUB, 128), BF),
        in_specs=[ANY],
        out_specs=ANY,
        scratch_shapes=[
            pltpu.SemaphoreType.DMA((count,)),
            pltpu.SemaphoreType.DMA((count,)),
            pltpu.SemaphoreType.DMA((1,)),
        ],
        compiler_params=pltpu.CompilerParams(collective_id=2, has_side_effects=True),
        name="dispatch",
    )(cells)


def combine_kernel(
    part, out, rel_r, rel_l, in_l, in_r, sum_r, sum_l, total, send_sem, recv_sem, local_sem
):
    me = Place()
    x, y, z = me.x, me.y, me.z
    xr, xl = me.at(dx=1), me.at(dx=-1)
    right, left, across = (x + 1) % NX, (x + NX - 1) % NX, (x + 2) % NX
    greet(plane_peers(me) + [xr, xl])
    sends = Sends(send_sem, recv_sem)
    start = sends.start
    order = (4, 3, 5, 2, 6, 1, 7, 0)
    low, high = pl.ds(0, 2), pl.ds(2, 2)
    begun, second, final = [], [], []

    def begin(i):
        g = (z + order[i]) % NZ
        begun.append(
            (
                start(part.at[across, g, low], rel_r.at[g], xr),
                start(part.at[across, g, high], rel_l.at[g], xl),
                start(part.at[right, g, high], in_l.at[g, high], xr),
                start(part.at[left, g, low], in_r.at[g, low], xl),
            )
        )

    def add(i):
        g = (z + order[i]) % NZ
        begun[i][0].wait_recv()
        sum_r[g] = (part[right, g, low].astype(F32) + rel_r[g].astype(F32)).astype(BF)
        one = start(sum_r.at[g], in_l.at[g, low], xr)
        begun[i][1].wait_recv()
        sum_l[g] = (part[left, g, high].astype(F32) + rel_l[g].astype(F32)).astype(BF)
        two = start(sum_l.at[g], in_r.at[g, high], xl)
        second.append((one, two))

    def close(i):
        g = (z + order[i]) % NZ
        begun[i][2].wait_recv()
        begun[i][3].wait_recv()
        second[i][0].wait_recv()
        second[i][1].wait_recv()
        total[g] = (
            part[x, g].astype(F32) + in_l[g].astype(F32) + in_r[g].astype(F32)
        ).astype(BF)
        for dy in range(NY):
            src = total.at[g, (y + dy) % NY]
            if (dy, order[i]) == (0, 0):
                keep = pltpu.make_async_copy(src, out.at[z, y], local_sem.at[0])
                keep.start()
                final.append(keep)
            else:
                start(src, out.at[z, y], me.at(dy=dy, dz=order[i]))
                final.append(sends.copies[-1])

    ahead = 3
    for i in range(ahead):
        begin(i)
    for i in range(NZ):
        if i + ahead < NZ:
            begin(i + ahead)
        add(i)
        if i >= 1:
            close(i - 1)
    close(NZ - 1)
    for copy in final[:-NY]:
        copy.wait_recv()
    final[-NY].wait()
    for copy in final[-NY + 1 :]:
        copy.wait_recv()
    sends.finish()


def combine(part):
    count = 31 + 6 * NZ
    cell = (SUB, 128)
    return pl.pallas_call(
        combine_kernel,
        out_shape=jax.ShapeDtypeStruct((NZ, NY) + cell, BF),
        in_specs=[VMEM],
        out_specs=ANY,
        scratch_shapes=[
            pltpu.VMEM((NZ, 2) + cell, BF),
            pltpu.VMEM((NZ, 2) + cell, BF),
            pltpu.VMEM((NZ, NY) + cell, BF),
            pltpu.VMEM((NZ, NY) + cell, BF),
            pltpu.VMEM((NZ, 2) + cell, BF),
            pltpu.VMEM((NZ, 2) + cell, BF),
            pltpu.VMEM((NZ, NY) + cell, BF),
            pltpu.SemaphoreType.DMA((count,)),
            pltpu.SemaphoreType.DMA((count,)),
            pltpu.SemaphoreType.DMA((1,)),
        ],
        compiler_params=pltpu.CompilerParams(
            collective_id=3, has_side_effects=True, vmem_limit_bytes=24 << 20
        ),
        name="combine",
    )(part)


def depthwise(normed, kernel, segments):
    half_width = (kernel.shape[0] - 1) // 2
    count_rows = normed.shape[0]
    padded = jnp.pad(normed, ((half_width, half_width), (0, 0)))
    seg_padded = jnp.pad(segments, (half_width, half_width), constant_values=-1)
    total = jnp.zeros_like(normed)
    for offset in range(kernel.shape[0]):
        window = padded[offset : offset + count_rows]
        same = (seg_padded[offset : offset + count_rows] == segments).astype(normed.dtype)
        total = total + kernel[offset][None, :] * window * same[:, None]
    return total


def swap_cores(values):
    return lax.ppermute(values, "dp", [(d, d ^ 1) for d in range(8)])


def local(frames, lengths, w_qkv, w_out, conv_w, w_router, expert_ids, w_up, w_down):
    core = lax.axis_index("dp") % 2
    offsets = jnp.arange(ROWS, dtype=jnp.int32)
    steps = jnp.arange(4, dtype=jnp.int32)
    ends = jnp.sum(jnp.where(steps[:, None] <= steps[None, :], lengths[0][:, None], 0), axis=0)
    segments = jnp.sum((offsets[:, None] >= ends[None, :]).astype(jnp.int32), axis=1)
    marks = (steps[:, None] == segments[None, :]).astype(BF)
    notes = jnp.concatenate([marks, expert_ids.T.astype(BF)], axis=0)
    notes = jnp.pad(notes, ((0, 16 - 6), (0, D - ROWS)))
    normed_in = normalize(frames.astype(F32)).astype(BF)
    xc = jnp.concatenate([normed_in, notes], axis=0)

    xg, wg, up2, dn2 = gather_all(xc, w_qkv, w_out, w_up, w_down)
    mixed, wo = heads_back(attention(xg, wg), wg)
    mixed = mixed.transpose(1, 0, 2).reshape(ROWS, D)

    first = (
        frames.astype(F32) + jnp.dot(mixed, wo.reshape(D, D), preferred_element_type=F32)
    ).astype(BF)
    conv_in = normalize(first.astype(F32))
    conv_out = depthwise(conv_in, conv_w, segments)
    second = (first.astype(F32) + jax.nn.silu(conv_out)).astype(BF)
    hidden = normalize(second.astype(F32)).astype(BF)

    theirs = swap_cores(hidden)
    both = jnp.stack([jnp.where(core == 0, hidden, theirs), jnp.where(core == 0, theirs, hidden)])
    both = both.reshape(2 * ROWS, D)
    pair = lax.dynamic_slice_in_dim(xg, lax.axis_index("dp") // 2 * 2, 2, axis=0)
    ids = pair[:, ROWS + 4 : ROWS + 6, :ROWS].astype(jnp.int32)
    logits = jnp.dot(both, w_router, preferred_element_type=F32).reshape(2, ROWS, -1)
    experts = jnp.arange(2 * EXPERT_DEVS, dtype=jnp.int32)
    chosen = ids[..., None] == experts
    gates = jax.nn.sigmoid(jnp.sum(jnp.where(chosen, logits[:, None], 0.0), axis=-1))
    flat = chosen.reshape(2, TOP * ROWS, -1).astype(BF)
    order = jnp.arange(TOP * ROWS, dtype=jnp.int32)
    before = (order[None, :] < order[:, None]).astype(BF)
    counts = jnp.einsum("ij,sje->sie", before, flat, preferred_element_type=F32)
    ranks = jnp.sum(counts * flat.astype(F32), axis=-1).astype(jnp.int32)
    ranks = ranks.reshape(2, TOP, ROWS)
    source = jnp.arange(2, dtype=jnp.int32)[:, None, None]
    slots = jnp.where(ids % 2 == core, ids // 2 * CELL + source * CAP + ranks, -1)
    slots = slots.transpose(1, 0, 2).reshape(TOP, 2 * ROWS)
    places = jnp.arange(EXPERT_DEVS * CELL, dtype=jnp.int32)
    hits = slots[:, :, None] == places
    pick = (hits[0] | hits[1]).astype(BF)
    cells = lax.dot_general(
        pick, both, (((0,), (0,)), ((), ())), preferred_element_type=F32
    ).astype(BF)

    routed = dispatch(cells.reshape(NY, NZ, SUB, 128)).reshape(-1, D)
    result = jnp.zeros((routed.shape[0], D), F32)
    for piece in range(2):
        upward = jnp.dot(routed, up2[piece], preferred_element_type=F32)
        activated = jax.nn.silu(upward).astype(BF)
        result = result + jnp.dot(activated, dn2[piece], preferred_element_type=F32)
    part = result.astype(BF).reshape(NX, NZ, NY, SUB, 128)
    returned = combine(part).reshape(NZ, NY, CELL, D).transpose(1, 0, 2, 3).reshape(-1, D)

    given = jnp.zeros((2 * ROWS, D), F32)
    for k in range(TOP):
        picked = jnp.dot(hits[k].astype(BF), returned, preferred_element_type=F32)
        given = given + gates[:, k].reshape(-1, 1) * picked
    given = given.reshape(2, ROWS, D)
    mine = jnp.where(core == 0, given[0], given[1])
    yours = jnp.where(core == 0, given[1], given[0])
    other = swap_cores(yours.astype(BF))
    return (second.astype(F32) + (mine + other.astype(F32))).astype(BF)


def solution(mesh):
    in_specs = (
        P(("dp", "expert"), None),
        P(("dp", "expert"), None),
        P("expert", None),
        P("expert", None),
        P(),
        P(),
        P(("dp", "expert"), None),
        P("expert", None, "dp"),
        P("expert", "dp", None),
    )
    out_specs = P(("dp", "expert"), None)
    return jax.shard_map(local, mesh=mesh, in_specs=in_specs, out_specs=out_specs, check_vma=False)
```

time: 346 us -> 250 us (0.72)
  waiting for transfers between devices: 237 us -> 1.16 us
  Pallas kernels: 0 us -> 189 us
  blocking collectives: 18.3 us -> 0 us
  local copies, waits for them, and re-layouts: 32.4 us -> 17.2 us
  between operations: 13.4 us -> 0.34 us
    pallas_call x0 -> x5, Pallas kernels: none -> 189 us  [the longest x1 76.6 us: gather_all(): pl.pallas_call(gather_kernel, out_shape=(jax.ShapeDtypeStruct((8, XROWS,...]
    all_gather x3 -> x0, waiting for transfers between devices: 176 us -> none  [the longest x1 72.4 us: local(): lax.all_gather(w_qkv, 'expert', axis=0, tiled=True)]
    reduce_scatter x1 -> x0, waiting for transfers between devices: 43.2 us -> none  [local(): lax.psum_scatter(jnp.einsum('nef,efd->ned', activated, w_down, preferred_...]
    all_to_all x1 -> x0, blocking collectives: 18.3 us -> none  [local(): lax.all_to_all(outgoing, 'expert', split_axis=0, concat_axis=0, tiled=True)]
    all_to_all x1 -> x0, waiting for transfers between devices: 16.3 us -> none  [local(): lax.all_to_all(summed, 'expert', split_axis=0, concat_axis=0, tiled=True)]
    scatter x1 -> x0, local copies, waits for them, and re-layouts: 12.2 us -> none  [local(): table = jnp.full((group_size * capacity, EXP_DEV), count_rows, jnp.int32)...]
    all_to_all x1 -> x0, starting transfers between devices: 9.57 us -> none  [local(): lax.all_to_all(summed, 'expert', split_axis=0, concat_axis=0, tiled=True)]
    reshape x1 -> x5, local copies, waits for them, and re-layouts: 0.14 us -> 9.38 us  [the longest x2 4.95 us: local(): routed = dispatch(cells.reshape(NY, NZ, SUB, 128)).reshape(-1, D)]
  transfers between devices with their start and end apart: 5 -> 2, of which waited for: 5 -> 1; matrix products, arithmetic and copies ran while one was open for 10% -> 1% of each run, Pallas kernels for 0% -> 0%
where the time goes in v1:
time: 250 us; the launch traced here: 248 us
  Pallas kernels  189 us (76%)
  matrix products  18.6 us (7%)
  local copies, waits for them, and re-layouts  17.2 us (7%)
  other arithmetic  13.7 us (5%)
  starting transfers between devices  8.05 us (3%)
    pallas_call x1, Pallas kernels, gather_all(): pl.pallas_call(gather_kernel, out_shape=(jax.ShapeDtypeStruct((8, XROWS,...  76.6 us
    pallas_call x1, Pallas kernels, dispatch(): pl.pallas_call(dispatch_kernel, out_shape=jax.ShapeDtypeStruct((NX, NZ, N...  39.7 us
    pallas_call x1, Pallas kernels, heads_back(): pl.pallas_call(heads_kernel, out_shape=(jax.ShapeDtypeStruct((8, ROWS, 12...  34 us
    pallas_call x1, Pallas kernels, combine(): pl.pallas_call(combine_kernel, out_shape=jax.ShapeDtypeStruct((NZ, NY) +...  30.8 us
    dot_general x2, matrix products, local(): result = result + jnp.dot(activated, dn2[piece], preferred_element_type=F32)  14.7 us
    ppermute x2, starting transfers between devices, swap_cores(): return lax.ppermute(values, 'dp', [(d, d ^ 1) for d in range(8)])  8.05 us
    pallas_call x1, Pallas kernels, attention(): pl.pallas_call(attention_kernel, grid=(8,), out_shape=jax.ShapeDtypeStruc...  7.5 us
    reduce_sum x2, other arithmetic, normalize(): mean_value = jnp.mean(values, axis=-1, keepdims=True)  5.27 us
  transfers between devices with their start and end apart: 2, of which 1 were waited for; matrix products, arithmetic and copies ran while one was open for 1% of the time, Pallas kernels for 0%

profile of v1, /device:TPU:7, one launch (start us, length us, event | category | flops | bytes accessed | tf_op | source)
XLA Modules:
  0.0 247.8 jit_solution(17884858987462579133)
XLA Ops:
  0.0 0.8 select_reduce_fusion.1
  0.8 0.1 convert_reduce_fusion.2
  0.9 0.1 compare_convert_fusion.28
  1.0 0.1 compare_convert_fusion.29
  1.1 1.1 fusion.153
  2.2 1.4 fusion.152
  3.6 0.7 convert_bitcast_fusion
  4.3 1.1 convert_reduce_fusion.1
  5.4 1.2 fusion.34
  6.6 1.2 fusion.35
  7.7 0.7 pad_maximum_fusion.1.xc
  8.5 76.6 %gather.1 = (bf16[8,144,1024]{2,1,0:T(8,128)(2,1)}, bf16[4,8,32,896]{3,2,1,0:T(8,128)(2,1)}, bf16[2,1024,512]{2,1,0:T(8,128)(2,1)}, bf16[2,512,1024]{2,1,0:T(8,128)(2,1)}) custom-call(bf16[144,1024]{1,0:T(8,128)(2,1)} %pad_maximum_fusion.1.xc, bf16[32,3072]{1,0:T(8,128)(2,1)} %wqkv.1, bf16[32,1024]{1,0:T(8,128)(2,1)} %wout.1, bf16[2,1024,512]{2,1,0:T(8,128)(2,1)} %wup.1, ...), custom_call_target="tpu_custom_call" | custom-call | tf_op jit(solution)/shard_map/gather/pallas_call | solution.py:236
  85.1 1.5 copy-done.1
  86.6 1.7 copy-done.2
  88.3 7.5 %attention.1.mixed = bf16[8,128,128]{2,1,0:T(8,128)(2,1)S(1)} custom-call(bf16[8,144,1024]{2,1,0:T(8,128)(2,1)S(1)} %copy-done.2, bf16[1024,896]{1,0:T(8,128)(2,1)S(1)} %bitcast.107), custom_call_target="tpu_custom_call" | custom-call | tf_op jit(solution)/shard_map/attention/pallas_call | solution.py:276
  95.8 0.7 copy-done.3
  96.5 34.0 %heads_back.1 = (bf16[8,128,128]{2,1,0:T(8,128)(2,1)}, bf16[4,8,32,1024]{3,2,1,0:T(8,128)(2,1)}) custom-call(bf16[8,128,128]{2,1,0:T(8,128)(2,1)} %copy-done.3, bf16[4,8,32,896]{3,2,1,0:T(8,128)(2,1)} %get-tuple-element.12.wg), custom_call_target="tpu_custom_call" | custom-call | tf_op jit(solution)/shard_map/heads_back/pallas_call | solution.py:314
  130.5 1.1 copy.14
  131.6 2.1 fusion.155
  133.8 0.2 multiply_reduce_fusion
  134.0 0.1 subtract_multiply_fusion
  134.2 4.2 %convert_reduce_fusion = (f32[128]{0:T(128)S(1)}, bf16[128,1024]{1,0:T(8,128)(2,1)S(1)}) fusion(f32[128,1024]{1,0:T(8,128)S(1)} %get-tuple-element.87, f32[128]{0:T(128)S(1)} %get-tuple-element.85, f32[1024]{0:T(1024)S(1)} %bitcast.123, f32[128]{0:T(128)S(1)} %get-tuple-element.57, f32[1024]{0:T(1024)S(1)} %bitcast.124, f32[128]{0:T(128)S(1)} %get-tuple-element.58, ...), kind=kLoop, calls=%fused_computation.59 | loop fusion | flops 12976000 | bytes 1453568 | tf_op jit(solution)/shard_map/reduce_sum | solution.py:32
  138.4 0.2 fusion.32
  138.6 0.2 fusion.33
  138.8 0.9 collective-permute-start
  139.8 0.7 dynamic-slice_convert_fusion
  140.5 0.2 fusion.7
  140.7 0.8 fusion.147
  141.5 0.2 iota_compare_fusion
  141.7 0.3 select_bitcast_fusion.1
  142.0 0.3 fusion.137
  142.4 0.4 convolution_convert_fusion
  142.8 1.1 reshape.126.cells
  143.9 39.7 %dispatch.1 = bf16[4,8,4,80,128]{4,3,2,1,0:T(8,128)(2,1)} custom-call(bf16[4,8,80,128]{3,2,1,0:T(8,128)(2,1)} %reshape.126.cells), custom_call_target="tpu_custom_call" | custom-call | tf_op jit(solution)/shard_map/dispatch/pallas_call | solution.py:385
  183.6 3.8 %reshape.127 = bf16[1280,1024]{1,0:T(8,128)(2,1)S(1)} reshape(bf16[4,8,4,80,128]{4,3,2,1,0:T(8,128)(2,1)} %dispatch.1) | data formatting | bytes 5242880 | tf_op jit(solution)/shard_map/reshape | solution.py:565
  187.5 6.9 %fusion.1 = f32[1280,1024]{1,0:T(8,128)} fusion(bf16[1280,1024]{1,0:T(8,128)(2,1)S(1)} %reshape.127, bf16[2,512,1024]{2,1,0:T(8,128)(2,1)} %get-tuple-element.16, bf16[2,1024,512]{2,1,0:T(8,128)(2,1)} %get-tuple-element.15), kind=kOutput, calls=%fused_computation.37 | convolution fusion | flops 2687631360 | bytes 9961472 | tf_op jit(solution)/shard_map/dot_general | solution.py:570
  194.4 7.7 %add_convert_fusion = bf16[1280,1024]{1,0:T(8,128)(2,1)} fusion(f32[1280,1024]{1,0:T(8,128)} %fusion.1, bf16[1280,1024]{1,0:T(8,128)(2,1)S(1)} %reshape.127, bf16[2,512,1024]{2,1,0:T(8,128)(2,1)} %get-tuple-element.16, bf16[2,1024,512]{2,1,0:T(8,128)(2,1)} %get-tuple-element.15), kind=kOutput, calls=%fused_computation | convolution fusion | flops 2690252800 | bytes 12582912 | tf_op jit(solution)/shard_map/dot_general | solution.py:570
  202.1 3.8 %reshape.128.part = bf16[4,8,4,80,128]{4,3,2,1,0:T(8,128)(2,1)S(1)} reshape(bf16[1280,1024]{1,0:T(8,128)(2,1)} %add_convert_fusion) | data formatting | bytes 5242880 | tf_op jit(solution)/shard_map/reshape | solution.py:571
  206.0 30.8 %combine.1 = bf16[8,4,80,128]{3,2,1,0:T(8,128)(2,1)S(1)} custom-call(bf16[4,8,4,80,128]{4,3,2,1,0:T(8,128)(2,1)S(1)} %reshape.128.part), custom_call_target="tpu_custom_call" | custom-call | tf_op jit(solution)/shard_map/combine/pallas_call | solution.py:475
  236.8 0.4 reshape.129
  237.2 0.1 copy.15
  237.3 0.2 reshape.130
  237.5 0.2 copy-done.8
  237.7 0.4 convolution_multiply_fusion.1
  238.2 0.4 fusion
  238.7 7.1 %collective-permute-start.1 = (bf16[128,1024]{1,0:T(8,128)(2,1)S(1)}, bf16[128,1024]{1,0:T(8,128)(2,1)S(1)}, u32[]{:S(2)}, u32[]{:S(2)}) collective-permute-start(bf16[128,1024]{1,0:T(8,128)(2,1)S(1)} %select_convert_fusion), channel_id=1, source_target_pairs={{0,32},{32,0},{64,96},{96,64},{128,160},{160,128},{192,224},{224,1... | collective-permute-start | bytes 786440 | tf_op jit(solution)/shard_map/ppermute | solution.py:513
  245.8 1.2 collective-permute-done.1
  246.9 0.8 fusion.36
  (32 shorter events, 0.3 us)
Async XLA Ops:
  0.0 142.0 %copy-start = (bf16[1024,64]{0,1:T(8,128)(2,1)S(1)}, bf16[1024,64]{0,1:T(8,128)(2,1)}, u32[]{:S(2)}) copy-start(bf16[1024,64]{0,1:T(8,128)(2,1)} %param.14) | copy-start | bytes 393220
  85.1 1.5 copy-start.1
  86.6 1.7 copy-start.2
  88.3 43.4 %copy-start.6 = (bf16[128,1024]{1,0:T(8,128)(2,1)S(1)}, bf16[128,1024]{1,0:T(8,128)(2,1)}, u32[]{:S(2)}) copy-start(bf16[128,1024]{1,0:T(8,128)(2,1)} %param.9) | copy-start | bytes 786436
  95.8 0.7 copy-start.3
  138.4 4.4 %copy-start.4 = (bf16[128,1024]{1,0:T(8,128)(2,1)}, bf16[128,1024]{1,0:T(8,128)(2,1)S(1)}, u32[]{:S(2)}) copy-start(bf16[128,1024]{1,0:T(8,128)(2,1)S(1)} %get-tuple-element.18) | copy-start | bytes 786436
  138.8 2.8 %collective-permute-start = (bf16[128,1024]{1,0:T(8,128)(2,1)S(1)}, bf16[128,1024]{1,0:T(8,128)(2,1)S(1)}, u32[]{:S(2)}, u32[]{:S(2)}) collective-permute-start(bf16[128,1024]{1,0:T(8,128)(2,1)S(1)} %fusion.33), channel_id=1, source_target_pairs={{0,32},{32,0},{64,96},{96,64},{128,160},{160,128},{192,224},{224,1... | collective-permute-start | bytes 786440 | tf_op jit(solution)/shard_map/ppermute | solution.py:513
  141.7 0.7 copy-start.7
  236.8 0.9 copy-start.8
  237.7 9.2 %copy-start.5 = (bf16[128,1024]{1,0:T(8,128)(2,1)S(1)}, bf16[128,1024]{1,0:T(8,128)(2,1)}, u32[]{:S(2)}) copy-start(bf16[128,1024]{1,0:T(8,128)(2,1)} %copy-done.4) | copy-start | bytes 786436
  238.7 8.3 %collective-permute-start.1 = (bf16[128,1024]{1,0:T(8,128)(2,1)S(1)}, bf16[128,1024]{1,0:T(8,128)(2,1)S(1)}, u32[]{:S(2)}, u32[]{:S(2)}) collective-permute-start(bf16[128,1024]{1,0:T(8,128)(2,1)S(1)} %select_convert_fusion), channel_id=1, source_target_pairs={{0,32},{32,0},{64,96},{96,64},{128,160},{160,128},{192,224},{224,1... | collective-permute-start | bytes 786440 | tf_op jit(solution)/shard_map/ppermute | solution.py:513

commit v2 on v1

v2 whole, which is shorter than its diff:
```python
import jax
import jax.numpy as jnp
from jax import lax
from jax.experimental import pallas as pl
from jax.experimental.pallas import tpu as pltpu
from jax.sharding import PartitionSpec as P

HEADS = 16
HEAD_DIM = 64
ROWS = 128
D = 1024
TOP = 2
NX, NY, NZ = 4, 4, 8
EXPERT_DEVS = NY * NZ
CAP = 5
CELL = 2 * CAP
SUB = CELL * D // 128
QCOLS = 384
OCOLS = 512
WCOLS = QCOLS + OCOLS
NOTES = 16
PLACES = EXPERT_DEVS * CELL
MESH = pl.DeviceIdType.MESH
ANY = pl.BlockSpec(memory_space=pl.ANY)
VMEM = pl.BlockSpec(memory_space=pltpu.VMEM)
SMEM = pl.BlockSpec(memory_space=pltpu.SMEM)
BF = jnp.bfloat16
F32 = jnp.float32


def normalize(values):
    mean_value = jnp.mean(values, axis=-1, keepdims=True)
    centred = values - mean_value
    variance = jnp.mean(centred * centred, axis=-1, keepdims=True)
    return centred * lax.rsqrt(variance + 1e-05)


class Place:
    def __init__(self):
        dp, ex = lax.axis_index("dp"), lax.axis_index("expert")
        self.dp, self.ex = dp, ex
        self.x, self.c = dp // 2, dp % 2
        self.y, self.z = ex // NZ, ex % NZ

    def at(self, dx=0, dy=0, dz=0, other=False):
        x, y, z = (self.x + dx + NX) % NX, (self.y + dy + NY) % NY, (self.z + dz + NZ) % NZ
        c = 1 - self.c if other else self.c
        return (x * 2 + c, y * NZ + z)


class Sends:
    def __init__(self, send_sem, recv_sem):
        self.send_sem, self.recv_sem, self.copies = send_sem, recv_sem, []

    def start(self, src, dst, device):
        at = len(self.copies)
        copy = pltpu.make_async_remote_copy(
            src_ref=src,
            dst_ref=dst,
            send_sem=self.send_sem.at[at],
            recv_sem=self.recv_sem.at[at],
            device_id=device,
            device_id_type=MESH,
        )
        copy.start()
        self.copies.append(copy)
        return copy

    def finish(self):
        for copy in self.copies:
            copy.wait_send()


def greet(devices):
    barrier = pltpu.get_barrier_semaphore()
    for device in devices:
        pl.semaphore_signal(barrier, inc=1, device_id=device, device_id_type=MESH)
    pl.semaphore_wait(barrier, len(devices))


def run_tasks(tasks):
    waiting = [(task, next(task, None)) for task in tasks]
    while waiting:
        later = []
        for task, copy in waiting:
            if copy is None:
                continue
            copy.wait_recv()
            later.append((task, next(task, None)))
        waiting = later


GATHER_SENDS = 80


def write_notes(lengths, ids, notes):
    rows = lax.broadcasted_iota(jnp.int32, (8, ROWS), 0)
    lanes = lax.broadcasted_iota(jnp.int32, (8, ROWS), 1)
    marks = jnp.zeros((8, ROWS), F32)
    begin = jnp.int32(0)
    for u in range(4):
        end = begin + lengths[0, u]
        inside = (rows == u) & (lanes >= begin) & (lanes < end)
        marks = jnp.where(inside, 1.0, marks)
        begin = end
    square = (ROWS, ROWS)
    eye = (
        lax.broadcasted_iota(jnp.int32, square, 0) == lax.broadcasted_iota(jnp.int32, square, 1)
    ).astype(BF)
    wide = jnp.zeros((ROWS, 8), jnp.int32)
    column = lax.broadcasted_iota(jnp.int32, (ROWS, 8), 1)
    for k in range(TOP):
        wide = jnp.where(column == 4 + k, ids[:, k : k + 1], wide)
    turned = lax.dot_general(
        wide.astype(F32).astype(BF), eye, (((0,), (0,)), ((), ())), preferred_element_type=F32
    )
    full = jnp.concatenate([marks + turned, jnp.zeros((NOTES - 8, ROWS), F32)], axis=0)
    notes[...] = full.astype(BF)


def gather_kernel(
    frames,
    lengths,
    ids,
    wqkv,
    wout,
    wup,
    wdn,
    xg,
    ng,
    wg,
    up_sib,
    dn_sib,
    xc,
    notes,
    send_sem,
    recv_sem,
    local_sem,
):
    me = Place()
    x, c, y, z, dp = me.x, me.c, me.y, me.z, me.dp
    sib = me.at(other=True)
    xr, xl = me.at(dx=1), me.at(dx=-1)
    yu, yd = me.at(dy=1), me.at(dy=-1)
    zu, zd = me.at(dz=1), me.at(dz=-1)
    locals_ = []

    def local(src, dst):
        copy = pltpu.make_async_copy(src, dst, local_sem.at[len(locals_)])
        copy.start()
        locals_.append(copy)

    for part in range(3):
        columns = pl.ds(pl.multiple_of(part * D + dp * 128, 128), 128)
        local(wqkv.at[:, columns], wg.at[y, z, :, pl.ds(part * 128, 128)])
    local(
        wout.at[:, pl.ds(pl.multiple_of(c * OCOLS, 128), OCOLS)],
        wg.at[y, z, :, pl.ds(QCOLS, OCOLS)],
    )
    others = [((dp + o) % 8, me.ex) for o in range(1, 8)]
    greet(others + [yu, yd, zu, zd])
    sends = Sends(send_sem, recv_sem)
    start = sends.start
    for copy in locals_:
        copy.wait()

    def yy(d):
        return (y + d + NY) % NY

    def zz(d):
        return (z + d + NZ) % NZ

    def x_chain():
        xc[...] = normalize(frames[...].astype(F32)).astype(BF)
        xg[dp] = xc[...]
        first_sib = start(xc, xg.at[dp], sib)
        to_r = start(xc, xg.at[dp], xr)
        to_l = start(xc, xg.at[dp], xl)
        write_notes(lengths, ids, notes)
        ng[dp] = notes[...]
        for device in others:
            noted.append(start(notes, ng.at[dp], device))
        left = xg.at[((x + NX - 1) % NX) * 2 + c]
        right = xg.at[((x + 1) % NX) * 2 + c]
        across = xg.at[((x + 2) % NX) * 2 + c]
        yield to_r
        low = left.at[pl.ds(0, 64)]
        relay_r = start(low, low, xr)
        sib1 = start(left, left, sib)
        yield to_l
        high = right.at[pl.ds(64, 64)]
        relay_l = start(high, high, xl)
        sib2 = start(right, right, sib)
        yield relay_r
        yield relay_l
        sib3 = start(across, across, sib)
        for copy in (first_sib, sib1, sib2, sib3):
            yield copy

    def z_first():
        def block(dy, dz):
            return wg.at[yy(dy), zz(dz), pl.ds(0, 16)]

        spread = []

        def available(dz):
            spread.append(
                (dz, start(block(0, dz), block(0, dz), yu), start(block(0, dz), block(0, dz), yd))
            )

        up = start(block(0, 0), block(0, 0), zu)
        down = start(block(0, 0), block(0, 0), zd)
        available(0)
        for s in range(1, 4):
            yield up
            up = start(block(0, -s), block(0, -s), zu)
            available(-s)
            yield down
            if s < 3:
                down = start(block(0, s), block(0, s), zd)
            available(s)
        yield up
        available(4)
        last = []
        for dz, to_u, to_d in spread:
            yield to_u
            yield to_d
            if dz in (0, 1, 2, 3):
                last.append(start(block(-1, dz), block(-1, dz), yu))
            else:
                last.append(start(block(1, dz), block(1, dz), yd))
        for copy in last:
            yield copy

    def y_first():
        def block(dy):
            return wg.at[yy(dy), z, pl.ds(16, 16)]

        def bundle(dz, first=0, count=NY):
            return wg.at[pl.ds(first, count), zz(dz), pl.ds(16, 16)]

        to_u = start(block(0), block(0), yu)
        to_d = start(block(0), block(0), yd)
        yield to_u
        relay = start(block(-1), block(-1), yu)
        yield to_d
        yield relay
        up = start(bundle(0), bundle(0), zu)
        down = start(bundle(0), bundle(0), zd)
        for s in range(1, 4):
            yield up
            if s < 3:
                up = start(bundle(-s), bundle(-s), zu)
            else:
                up = start(bundle(-s, 0, 2), bundle(-s, 0, 2), zu)
            yield down
            if s < 3:
                down = start(bundle(s), bundle(s), zd)
            else:
                down = start(bundle(s, 2, 2), bundle(s, 2, 2), zd)
        yield up
        yield down

    def swap():
        one = start(wup.at[1 - c], up_sib, sib)
        two = start(wdn.at[1 - c], dn_sib, sib)
        yield from ()
        swaps.extend((one, two))

    swaps, noted = [], []
    run_tasks([y_first(), z_first(), x_chain(), swap()])
    for copy in swaps + noted:
        copy.wait_recv()
    sends.finish()


def gather_all(frames, lengths, ids, w_qkv, w_out, w_up, w_down):
    return pl.pallas_call(
        gather_kernel,
        out_shape=(
            jax.ShapeDtypeStruct((8, ROWS, D), BF),
            jax.ShapeDtypeStruct((8, NOTES, ROWS), BF),
            jax.ShapeDtypeStruct((NY, NZ, 32, WCOLS), BF),
            jax.ShapeDtypeStruct(w_up.shape[1:], BF),
            jax.ShapeDtypeStruct(w_down.shape[1:], BF),
        ),
        in_specs=[VMEM, SMEM, VMEM] + [ANY] * 4,
        out_specs=[VMEM, VMEM, VMEM, ANY, ANY],
        scratch_shapes=[
            pltpu.VMEM((ROWS, D), BF),
            pltpu.VMEM((NOTES, ROWS), BF),
            pltpu.SemaphoreType.DMA((GATHER_SENDS,)),
            pltpu.SemaphoreType.DMA((GATHER_SENDS,)),
            pltpu.SemaphoreType.DMA((8,)),
        ],
        compiler_params=pltpu.CompilerParams(
            collective_id=0, has_side_effects=True, vmem_limit_bytes=24 << 20
        ),
        name="gather",
    )(frames, lengths, ids, w_qkv, w_out, w_up, w_down)


def attention_kernel(x_ref, notes_ref, w_ref, out_ref, qkv_ref):
    w = w_ref[...]
    for half in range(2):
        rows = x_ref[pl.ds(4 * half, 4)].reshape(4 * ROWS, D)
        qkv = jnp.dot(rows, w, preferred_element_type=F32).astype(BF)
        qkv_ref[pl.ds(4 * half, 4)] = qkv.reshape(4, ROWS, QCOLS)
    first_head = lax.broadcasted_iota(jnp.int32, (ROWS, 128), 1) < HEAD_DIM
    for b in range(8):
        marks = notes_ref[b, :4, :].astype(F32)
        same = lax.dot_general(marks, marks, (((0,), (0,)), ((), ())), preferred_element_type=F32)
        allowed = same > 0.5
        q, k, v = (qkv_ref[b, :, pl.ds(128 * i, 128)] for i in range(3))
        mixed = []
        for h in range(2):
            mine = jnp.where(first_head == (h == 0), q, jnp.zeros_like(q))
            scores = lax.dot_general(mine, k, (((1,), (1,)), ((), ())), preferred_element_type=F32)
            scores = jnp.where(allowed, scores * HEAD_DIM ** (-0.5), -1e30)
            highest = jnp.max(scores, axis=-1, keepdims=True)
            expo = jnp.exp(scores - highest)
            probs = (expo / jnp.sum(expo, axis=-1, keepdims=True)).astype(BF)
            mixed.append(jnp.dot(probs, v, preferred_element_type=F32))
        out_ref[b] = jnp.where(first_head, mixed[0], mixed[1]).astype(BF)


def attention(xg, ng, wg):
    return pl.pallas_call(
        attention_kernel,
        grid=(1,),
        out_shape=jax.ShapeDtypeStruct((8, ROWS, 128), BF),
        in_specs=[
            pl.BlockSpec((8, ROWS, D), lambda i: (0, 0, 0)),
            pl.BlockSpec((8, NOTES, ROWS), lambda i: (0, 0, 0)),
            pl.BlockSpec((D, QCOLS), lambda i: (0, 0)),
        ],
        out_specs=pl.BlockSpec((8, ROWS, 128), lambda i: (0, 0, 0)),
        scratch_shapes=[pltpu.VMEM((8, ROWS, QCOLS), BF)],
        compiler_params=pltpu.CompilerParams(vmem_limit_bytes=32 << 20),
        name="attention",
    )(xg, ng, wg.reshape(D, WCOLS))


def heads_kernel(mixed, wg, out, wo, send_sem, recv_sem, local_sem):
    me = Place()
    dp, c = me.dp, me.c
    peers = [((dp + o) % 8, me.ex) for o in range(1, 8)]
    sib = me.at(other=True)
    half = pl.ds(pl.multiple_of(c * OCOLS, 128), OCOLS)
    mine = wg.at[:, :, :, pl.ds(QCOLS, OCOLS)]
    keep = pltpu.make_async_copy(mixed.at[dp], out.at[dp], local_sem.at[0])
    keep.start()
    keep_w = pltpu.make_async_copy(mine, wo.at[:, :, :, half], local_sem.at[1])
    keep_w.start()
    greet(peers)
    sends = Sends(send_sem, recv_sem)
    for o in range(1, 8):
        sends.start(mixed.at[(dp + o) % 8], out.at[dp], peers[o - 1])
    sends.start(mine, wo.at[:, :, :, half], sib)
    for copy in sends.copies:
        copy.wait_recv()
    keep.wait()
    keep_w.wait()
    sends.finish()


def heads_back(mixed, wg):
    return pl.pallas_call(
        heads_kernel,
        out_shape=(
            jax.ShapeDtypeStruct((8, ROWS, 128), BF),
            jax.ShapeDtypeStruct((NY, NZ, 32, D), BF),
        ),
        in_specs=[ANY] * 2,
        out_specs=[VMEM] * 2,
        scratch_shapes=[
            pltpu.SemaphoreType.DMA((8,)),
            pltpu.SemaphoreType.DMA((8,)),
            pltpu.SemaphoreType.DMA((2,)),
        ],
        compiler_params=pltpu.CompilerParams(
            collective_id=1, has_side_effects=True, vmem_limit_bytes=16 << 20
        ),
        name="heads_back",
    )(mixed, wg)


def middle_kernel(
    frames, mixed, wo, notes, conv_w, w_router, ids, second, hidden, gates, hits, shifted, masks
):
    dp = lax.axis_index("dp")
    core = dp % 2
    rows = jnp.concatenate([mixed[b] for b in range(8)], axis=1)
    added = jnp.dot(rows, wo[...], preferred_element_type=F32)
    first = (frames[...].astype(F32) + added).astype(BF).astype(F32)
    conv_in = normalize(first)

    square = (ROWS, ROWS)
    at_row = lax.broadcasted_iota(jnp.int32, square, 0)
    at_lane = lax.broadcasted_iota(jnp.int32, square, 1)
    marks = notes[dp, :4, :].astype(F32)
    same = lax.dot_general(marks, marks, (((0,), (0,)), ((), ())), preferred_element_type=F32)
    begin = jnp.min(jnp.where(same > 0.5, at_lane, ROWS), axis=1, keepdims=True)
    end = jnp.max(jnp.where(same > 0.5, at_lane + 1, 0), axis=1, keepdims=True)
    low = jnp.broadcast_to(begin, square) - at_row + 15
    high = jnp.broadcast_to(end, square) - at_row + 15
    for j in range(31):
        masks[j] = jnp.where((low <= j) & (j < high), 1.0, 0.0)

    edge = jnp.zeros((16, D), F32)
    padded = jnp.concatenate([edge, conv_in, edge], axis=0)
    for s in range(8):
        shifted[s] = padded[s : s + 152]

    def columns(i, carry):
        lanes = pl.ds(pl.multiple_of(i * 128, 128), 128)
        total = jnp.zeros((ROWS, 128), F32)
        for j in range(31):
            window = shifted[(j + 1) % 8, pl.ds((j + 1) // 8 * 8, ROWS), lanes]
            total = total + (conv_w[pl.ds(j, 1), lanes] * window) * masks[j]
        shifted[0, pl.ds(0, ROWS), lanes] = total
        return carry

    lax.fori_loop(0, D // 128, columns, 0)
    conv_out = shifted[0, pl.ds(0, ROWS), :]
    after = (first + conv_out / (1.0 + jnp.exp(-conv_out))).astype(BF)
    second[...] = after
    normed = normalize(after.astype(F32)).astype(BF)
    hidden[...] = normed

    logits = jnp.dot(normed, w_router[...], preferred_element_type=F32)
    expert = lax.broadcasted_iota(jnp.int32, logits.shape, 1)
    for k in range(TOP):
        chosen = jnp.where(ids[:, k : k + 1] == expert, logits, 0.0)
        logit = jnp.sum(chosen, axis=1, keepdims=True)
        gates[:, k : k + 1] = 1.0 / (1.0 + jnp.exp(-logit))

    before = (at_row < at_lane).astype(BF)
    place = lax.broadcasted_iota(jnp.int32, (PLACES, ROWS), 0)
    each = lax.broadcasted_iota(jnp.int32, (2 * EXPERT_DEVS, ROWS), 0)
    for s in range(2):
        names = notes[dp // 2 * 2 + s, 4:8, :].astype(F32).astype(jnp.int32)
        held = jnp.zeros((2 * EXPERT_DEVS, 1), F32)
        for k in range(TOP):
            name = names[k : k + 1]
            one = name == each
            ones = jnp.where(one, 1.0, 0.0)
            earlier = jnp.dot(ones.astype(BF), before, preferred_element_type=F32) + held
            rank = jnp.sum(ones * earlier, axis=0, keepdims=True).astype(jnp.int32)
            held = held + jnp.sum(ones, axis=1, keepdims=True)
            slot = name // 2 * CELL + s * CAP + rank
            slot = jnp.where(name % 2 == core, slot, -1)
            hits[k, :, pl.ds(s * ROWS, ROWS)] = jnp.where(place == slot, 1.0, 0.0).astype(BF)


def middle(frames, mixed, wo, notes, conv_w, w_router, ids):
    return pl.pallas_call(
        middle_kernel,
        out_shape=(
            jax.ShapeDtypeStruct((ROWS, D), BF),
            jax.ShapeDtypeStruct((ROWS, D), BF),
            jax.ShapeDtypeStruct((ROWS, TOP), F32),
            jax.ShapeDtypeStruct((TOP, PLACES, 2 * ROWS), BF),
        ),
        in_specs=[VMEM] * 7,
        out_specs=[VMEM] * 4,
        scratch_shapes=[
            pltpu.VMEM((8, 152, D), F32),
            pltpu.VMEM((31, ROWS, ROWS), F32),
        ],
        compiler_params=pltpu.CompilerParams(vmem_limit_bytes=32 << 20),
        name="middle",
    )(frames, mixed, wo, notes, conv_w, w_router, ids)


PLANE = [(dy, dz) for dz in range(NZ) for dy in range(NY) if (dy, dz) != (0, 0)]


def plane_peers(me):
    return [me.at(dy=dy, dz=dz) for dy, dz in PLANE]


def dispatch_kernel(hidden, hits, out, both, cells, send_sem, recv_sem, local_sem):
    me = Place()
    x, y, z = me.x, me.y, me.z
    xr, xl, sib = me.at(dx=1), me.at(dx=-1), me.at(other=True)
    greet(plane_peers(me) + [xr, xl, sib])
    sends = Sends(send_sem, recv_sem)
    start = sends.start
    theirs = start(hidden, both.at[me.c], sib)
    both[me.c] = hidden[...]
    pick = hits[0] + hits[1]
    theirs.wait_recv()
    rows = jnp.dot(pick, both[...].reshape(2 * ROWS, D), preferred_element_type=F32)
    cells[...] = rows.astype(BF).reshape(PLACES, 8, 128).reshape(NY, NZ, SUB, 128)
    keep = pltpu.make_async_copy(cells.at[y, z], out.at[x, z, y], local_sem.at[0])
    keep.start()
    order = (0, 1, 7, 2, 6, 3, 5, 4)
    direct = {}

    def issue(dz):
        for dy in range(NY):
            if (dy, dz) != (0, 0):
                src = cells.at[(y + dy) % NY, (z + dz) % NZ]
                direct[dy, dz] = start(src, out.at[x, z, y], me.at(dy=dy, dz=dz))

    ahead = 2
    for dz in order[:ahead]:
        issue(dz)
    keep.wait()
    right, left = (x + 1) % NX, (x + NX - 1) % NX
    sideways, last = [], []

    def relay(i):
        group = (z - order[i] + NZ) % NZ
        to_r, to_l = sideways[i]
        to_r.wait_recv()
        low = out.at[left, group, pl.ds(0, 2)]
        last.append(start(low, low, xr))
        to_l.wait_recv()
        high = out.at[right, group, pl.ds(2, 2)]
        last.append(start(high, high, xl))

    for i, dz in enumerate(order):
        if i + ahead < NZ:
            issue(order[i + ahead])
        for dy in range(NY):
            if (dy, dz) != (0, 0):
                direct[dy, dz].wait_recv()
        block = out.at[x, (z - dz + NZ) % NZ]
        sideways.append((start(block, block, xr), start(block, block, xl)))
        if i >= 1:
            relay(i - 1)
    relay(NZ - 1)
    for copy in last:
        copy.wait_recv()
    sends.finish()


def dispatch(hidden, hits):
    count = 32 + 4 * NZ
    return pl.pallas_call(
        dispatch_kernel,
        out_shape=jax.ShapeDtypeStruct((NX, NZ, NY, SUB, 128), BF),
        in_specs=[VMEM, VMEM],
        out_specs=ANY,
        scratch_shapes=[
            pltpu.VMEM((2, ROWS, D), BF),
            pltpu.VMEM((NY, NZ, SUB, 128), BF),
            pltpu.SemaphoreType.DMA((count,)),
            pltpu.SemaphoreType.DMA((count,)),
            pltpu.SemaphoreType.DMA((1,)),
        ],
        compiler_params=pltpu.CompilerParams(
            collective_id=2, has_side_effects=True, vmem_limit_bytes=24 << 20
        ),
        name="dispatch",
    )(hidden, hits)


def expert_kernel(core_ref, x_ref, up_own, dn_own, up_sib, dn_sib, out_ref):
    rows = x_ref[0].reshape(PLACES, 8, 128).reshape(PLACES, D)
    result = None
    for up, down in ((up_own.at[0], dn_own.at[0]), (up_sib, dn_sib)):
        upward = jnp.dot(rows, up[...], preferred_element_type=F32)
        activated = (upward / (1.0 + jnp.exp(-upward))).astype(BF)
        term = jnp.dot(activated, down[...], preferred_element_type=F32)
        result = term if result is None else result + term
    out_ref[0] = result.astype(BF).reshape(PLACES, 8, 128).reshape(PLACES * 8, 128)


def expert(core, routed, w_up, w_down, up_sib, dn_sib):
    block = pl.BlockSpec((1, PLACES * 8, 128), lambda i, c: (i, 0, 0))
    return pl.pallas_call(
        expert_kernel,
        out_shape=jax.ShapeDtypeStruct(routed.shape, BF),
        grid_spec=pltpu.PrefetchScalarGridSpec(
            num_scalar_prefetch=1,
            grid=(NX,),
            in_specs=[
                block,
                pl.BlockSpec((1,) + w_up.shape[1:], lambda i, c: (c[0], 0, 0)),
                pl.BlockSpec((1,) + w_down.shape[1:], lambda i, c: (c[0], 0, 0)),
                pl.BlockSpec(up_sib.shape, lambda i, c: (0, 0)),
                pl.BlockSpec(dn_sib.shape, lambda i, c: (0, 0)),
            ],
            out_specs=block,
        ),
        compiler_params=pltpu.CompilerParams(vmem_limit_bytes=40 << 20),
        name="expert",
    )(core, routed, w_up, w_down, up_sib, dn_sib)


def combine_kernel(
    part,
    hits,
    gates,
    second,
    block_out,
    out,
    rel_r,
    rel_l,
    in_l,
    in_r,
    sum_r,
    sum_l,
    total,
    picked,
    inbox,
    send_sem,
    recv_sem,
    local_sem,
):
    me = Place()
    x, y, z = me.x, me.y, me.z
    xr, xl = me.at(dx=1), me.at(dx=-1)
    right, left, across = (x + 1) % NX, (x + NX - 1) % NX, (x + 2) % NX
    sib = me.at(other=True)
    greet(plane_peers(me) + [xr, xl, sib])
    sends = Sends(send_sem, recv_sem)
    start = sends.start
    order = (4, 3, 5, 2, 6, 1, 7, 0)
    low, high = pl.ds(0, 2), pl.ds(2, 2)
    begun, summed, final = [], [], []

    def begin(i):
        g = (z + order[i]) % NZ
        begun.append(
            (
                start(part.at[across, g, low], rel_r.at[g], xr),
                start(part.at[across, g, high], rel_l.at[g], xl),
                start(part.at[right, g, high], in_l.at[g, high], xr),
                start(part.at[left, g, low], in_r.at[g, low], xl),
            )
        )

    def add(i):
        g = (z + order[i]) % NZ
        begun[i][0].wait_recv()
        sum_r[g] = (part[right, g, low].astype(F32) + rel_r[g].astype(F32)).astype(BF)
        one = start(sum_r.at[g], in_l.at[g, low], xr)
        begun[i][1].wait_recv()
        sum_l[g] = (part[left, g, high].astype(F32) + rel_l[g].astype(F32)).astype(BF)
        two = start(sum_l.at[g], in_r.at[g, high], xl)
        summed.append((one, two))

    def close(i):
        g = (z + order[i]) % NZ
        begun[i][2].wait_recv()
        begun[i][3].wait_recv()
        summed[i][0].wait_recv()
        summed[i][1].wait_recv()
        total[g] = (
            part[x, g].astype(F32) + in_l[g].astype(F32) + in_r[g].astype(F32)
        ).astype(BF)
        for dy in range(NY):
            src = total.at[g, (y + dy) % NY]
            if (dy, order[i]) == (0, 0):
                keep = pltpu.make_async_copy(src, out.at[y, z], local_sem.at[0])
                keep.start()
                final.append(keep)
            else:
                start(src, out.at[y, z], me.at(dy=dy, dz=order[i]))
                final.append(sends.copies[-1])

    ahead = 3
    for i in range(ahead):
        begin(i)
    for i in range(NZ):
        if i + ahead < NZ:
            begin(i + ahead)
        add(i)
        if i >= 1:
            close(i - 1)
    close(NZ - 1)
    for copy in final[:-NY]:
        copy.wait_recv()
    final[-NY].wait()
    for copy in final[-NY + 1 :]:
        copy.wait_recv()

    rows = out[...].reshape(PLACES * 8, 128).reshape(PLACES, 8, 128).reshape(PLACES, D)
    given = []
    for k in range(TOP):
        taken = lax.dot_general(
            hits[k], rows, (((0,), (0,)), ((), ())), preferred_element_type=F32
        )
        picked[k] = taken.astype(BF).reshape(2, ROWS, D)
        given.append(start(picked.at[k, 1 - me.c], inbox.at[k], sib))
    result = second[...].astype(F32)
    for k in range(TOP):
        given[k].wait_recv()
        value = picked[k, me.c].astype(F32) + inbox[k].astype(F32)
        result = result + gates[:, k : k + 1] * value
    block_out[...] = result.astype(BF)
    sends.finish()


def combine(part, hits, gates, second):
    count = 31 + 6 * NZ + TOP
    cell = (SUB, 128)
    return pl.pallas_call(
        combine_kernel,
        out_shape=jax.ShapeDtypeStruct(second.shape, BF),
        in_specs=[VMEM] * 4,
        out_specs=VMEM,
        scratch_shapes=[
            pltpu.VMEM((NY, NZ) + cell, BF),
            pltpu.VMEM((NZ, 2) + cell, BF),
            pltpu.VMEM((NZ, 2) + cell, BF),
            pltpu.VMEM((NZ, NY) + cell, BF),
            pltpu.VMEM((NZ, NY) + cell, BF),
            pltpu.VMEM((NZ, 2) + cell, BF),
            pltpu.VMEM((NZ, 2) + cell, BF),
            pltpu.VMEM((NZ, NY) + cell, BF),
            pltpu.VMEM((TOP, 2, ROWS, D), BF),
            pltpu.VMEM((TOP, ROWS, D), BF),
            pltpu.SemaphoreType.DMA((count,)),
            pltpu.SemaphoreType.DMA((count,)),
            pltpu.SemaphoreType.DMA((1,)),
        ],
        compiler_params=pltpu.CompilerParams(
            collective_id=3, has_side_effects=True, vmem_limit_bytes=32 << 20
        ),
        name="combine",
    )(part, hits, gates, second)


def local(frames, lengths, w_qkv, w_out, conv_w, w_router, expert_ids, w_up, w_down):
    xg, ng, wg, up_sib, dn_sib = gather_all(
        frames, lengths, expert_ids, w_qkv, w_out, w_up, w_down
    )
    mixed, wo = heads_back(attention(xg, ng, wg), wg)
    second, hidden, gates, hits = middle(
        frames, mixed, wo.reshape(D, D), ng, conv_w, w_router, expert_ids
    )
    routed = dispatch(hidden, hits)
    core = (lax.axis_index("dp") % 2).reshape(1)
    part = expert(core, routed.reshape(NX, -1, 128), w_up, w_down, up_sib, dn_sib)
    return combine(part.reshape(routed.shape), hits, gates, second)


def solution(mesh):
    in_specs = (
        P(("dp", "expert"), None),
        P(("dp", "expert"), None),
        P("expert", None),
        P("expert", None),
        P(),
        P(),
        P(("dp", "expert"), None),
        P("expert", None, "dp"),
        P("expert", "dp", None),
    )
    out_specs = P(("dp", "expert"), None)
    return jax.shard_map(local, mesh=mesh, in_specs=in_specs, out_specs=out_specs, check_vma=False)
```

time: 250 us -> 156 us (0.62)
  Pallas kernels: 189 us -> 144 us
  matrix products: 18.6 us -> 0 us
  other arithmetic: 13.7 us -> 0 us
  local copies, waits for them, and re-layouts: 17.2 us -> 9.13 us
  starting transfers between devices: 8.05 us -> 0 us
    pallas_call x1, Pallas kernels: 34 us -> 12 us  [heads_back(): pl.pallas_call(heads_kernel, out_shape=(jax.ShapeDtypeStruct((8, ROWS, 12...]
    dot_general x8 -> x0, matrix products: 18.6 us -> none  [the longest x2 14.7 us: local(): result = result + jnp.dot(activated, dn2[piece], preferred_element_type=F32)]
    pallas_call x3 -> x5, Pallas kernels: 115 us -> 96.4 us  [the longest x1 42.9 us: combine(): pl.pallas_call(combine_kernel, out_shape=jax.ShapeDtypeStruct(second.shap...]
    reshape x5 -> x0, local copies, waits for them, and re-layouts: 9.38 us -> none  [the longest x2 4.95 us: local(): routed = dispatch(cells.reshape(NY, NZ, SUB, 128)).reshape(-1, D)]
    ppermute x2 -> x0, starting transfers between devices: 8.05 us -> none  [swap_cores(): return lax.ppermute(values, 'dp', [(d, d ^ 1) for d in range(8)])]
    reduce_sum x8 -> x0, other arithmetic: 7.75 us -> none  [the longest x2 5.27 us: normalize(): mean_value = jnp.mean(values, axis=-1, keepdims=True)]
    unnamed x19 -> x23, local copies, waits for them, and re-layouts: 4.07 us -> 9.13 us
    convert_element_type x10 -> x0, other arithmetic: 3.81 us -> none  [the longest x1 1.16 us: local(): normed_in = normalize(frames.astype(F32)).astype(BF)]
  transfers between devices with their start and end apart: 2 -> 0, of which waited for: 1 -> 0; matrix products, arithmetic and copies ran while one was open for 1% -> 0% of each run, Pallas kernels for 0% -> 0%
where the time goes in v2:
time: 156 us; the launch traced here: 154 us
  Pallas kernels  144 us (92%)
  local copies, waits for them, and re-layouts  9.13 us (6%)
    pallas_call x1, Pallas kernels, combine(): pl.pallas_call(combine_kernel, out_shape=jax.ShapeDtypeStruct(second.shap...  42.9 us
    pallas_call x1, Pallas kernels, dispatch(): pl.pallas_call(dispatch_kernel, out_shape=jax.ShapeDtypeStruct((NX, NZ, N...  36 us
    pallas_call x1, Pallas kernels, gather_all(): pl.pallas_call(gather_kernel, out_shape=(jax.ShapeDtypeStruct((8, ROWS, D...  35 us
    pallas_call x1, Pallas kernels, heads_back(): pl.pallas_call(heads_kernel, out_shape=(jax.ShapeDtypeStruct((8, ROWS, 12...  12 us
    unnamed x23, local copies, waits for them, and re-layouts  9.13 us
    pallas_call x1, Pallas kernels, expert(): pl.pallas_call(expert_kernel, out_shape=jax.ShapeDtypeStruct(routed.shape...  7.98 us
    pallas_call x1, Pallas kernels, attention(): pl.pallas_call(attention_kernel, grid=(1,), out_shape=jax.ShapeDtypeStruc...  6.15 us
    pallas_call x1, Pallas kernels, middle(): pl.pallas_call(middle_kernel, out_shape=(jax.ShapeDtypeStruct((ROWS, D),...  4.37 us

profile of v2, /device:TPU:7, one launch (start us, length us, event | category | flops | bytes accessed | tf_op | source)
XLA Modules:
  0.0 153.7 jit_solution(15147302650883520356)
XLA Ops:
  0.0 0.8 copy.10.ids
  0.8 1.1 copy.11.w_router
  1.9 0.0 copy-start
  1.9 1.6 %copy-done = bf16[2,1024,512]{2,1,0:T(8,128)(2,1)S(1)} copy-done((bf16[2,1024,512]{2,1,0:T(8,128)(2,1)S(1)}, bf16[2,1024,512]{2,1,0:T(8,128)(2,1)}, u32[]{:S(2)}) %copy-start) | copy-done | bytes 2097176
  3.5 0.0 copy-start.2
  3.5 1.6 %copy-done.2 = bf16[2,512,1024]{2,1,0:T(8,128)(2,1)S(1)} copy-done((bf16[2,512,1024]{2,1,0:T(8,128)(2,1)S(1)}, bf16[2,512,1024]{2,1,0:T(8,128)(2,1)}, u32[]{:S(2)}) %copy-start.2) | copy-done | bytes 2097176
  5.1 0.0 copy-start.4
  5.1 0.9 copy-done.4
  6.0 0.0 copy-start.6
  6.0 0.9 copy-done.6
  6.9 0.0 copy-start.8
  6.9 0.8 copy-done.8
  7.8 0.0 copy-start.9
  7.8 0.7 copy-done.9
  8.4 35.0 %gather.1 = (bf16[8,128,1024]{2,1,0:T(8,128)(2,1)S(1)}, bf16[8,16,128]{2,1,0:T(8,128)(2,1)S(1)}, bf16[4,8,32,896]{3,2,1,0:T(8,128)(2,1)S(1)}, bf16[1024,512]{1,0:T(8,128)(2,1)S(1)}, bf16[512,1024]{1,0:T(8,128)(2,1)S(1)}) custom-call(bf16[128,1024]{1,0:T(8,128)(2,1)S(1)} %copy-done.4, s32[1,4]{1,0:T(1,128)S(1)} %copy-done.9, s32[128,2]{1,0:T(8,128)S(1)} %copy.10.ids, ...), custom_call_target="tpu_custom_call" | custom-call | tf_op jit(solution)/shard_map/gather/pallas_call | solution.py:278
  43.4 6.2 %attention.1.mixed = bf16[8,128,128]{2,1,0:T(8,128)(2,1)S(1)} custom-call(bf16[8,128,1024]{2,1,0:T(8,128)(2,1)S(1)} %get-tuple-element.16.x_ref, bf16[8,16,128]{2,1,0:T(8,128)(2,1)S(1)} %get-tuple-element.17.notes_ref.notes, bf16[1024,896]{1,0:T(8,128)(2,1)S(1)} %bitcast.7), custom_call_target="tpu_custom_call" | custom-call | tf_op jit(solution)/shard_map/attention/pallas_call | solution.py:328
  49.6 0.0 copy-start.5
  49.6 0.0 copy-start.7
  49.6 12.0 %heads_back.1 = (bf16[8,128,128]{2,1,0:T(8,128)(2,1)S(1)}, bf16[4,8,32,1024]{3,2,1,0:T(8,128)(2,1)S(1)}) custom-call(bf16[8,128,128]{2,1,0:T(8,128)(2,1)S(1)} %attention.1.mixed, bf16[4,8,32,896]{3,2,1,0:T(8,128)(2,1)S(1)} %get-tuple-element.18.wg), custom_call_target="tpu_custom_call" | custom-call | tf_op jit(solution)/shard_map/heads_back/pallas_call | solution.py:368
  61.6 0.0 copy-done.5
  61.6 0.0 copy-done.7
  61.7 0.0 copy-start.3
  61.7 4.4 %middle.1 = (bf16[128,1024]{1,0:T(8,128)(2,1)S(1)}, bf16[128,1024]{1,0:T(8,128)(2,1)S(1)}, f32[128,2]{1,0:T(8,128)S(1)}, bf16[2,320,256]{2,1,0:T(8,128)(2,1)S(1)}) custom-call(bf16[128,1024]{1,0:T(8,128)(2,1)S(1)} %copy-done.5, bf16[8,128,128]{2,1,0:T(8,128)(2,1)S(1)} %get-tuple-element.19.mixed, bf16[1024,1024]{1,0:T(8,128)(2,1)S(1)} %bitcast.8, ...), custom_call_target="tpu_custom_call" | custom-call | tf_op jit(solution)/shard_map/middle/pallas_call | solution.py:457
  66.0 0.0 copy-start.1
  66.1 36.0 %dispatch.1 = bf16[4,8,4,80,128]{4,3,2,1,0:T(8,128)(2,1)S(1)} custom-call(bf16[128,1024]{1,0:T(8,128)(2,1)S(1)} %get-tuple-element.21.hidden, bf16[2,320,256]{2,1,0:T(8,128)(2,1)S(1)} %get-tuple-element.22.hits), custom_call_target="tpu_custom_call" | custom-call | tf_op jit(solution)/shard_map/dispatch/pallas_call | solution.py:542
  102.1 0.0 copy-done.3
  102.1 0.0 copy-done.1
  102.1 8.0 %expert.1 = bf16[4,2560,128]{2,1,0:T(8,128)(2,1)S(1)} custom-call(s32[1]{0:T(128)} %bitcast.core_ref, bf16[4,2560,128]{2,1,0:T(8,128)(2,1)S(1)} %bitcast.6, bf16[2,1024,512]{2,1,0:T(8,128)(2,1)S(1)} %copy-done.1, bf16[2,512,1024]{2,1,0:T(8,128)(2,1)S(1)} %copy-done.3, bf16[1024,512]{1,0:T(8,128)(2,1)S(1)} %get-tuple-element.23.up_sib, ...), custom_call_target="tpu_custom_call" | custom-call | tf_op jit(solution)/shard_map/expert/pallas_call | solution.py:574
  110.1 42.9 %combine.1 = bf16[128,1024]{1,0:T(8,128)(2,1)S(1)} custom-call(bf16[4,8,4,80,128]{4,3,2,1,0:T(8,128)(2,1)S(1)} %bitcast.5, bf16[2,320,256]{2,1,0:T(8,128)(2,1)S(1)} %get-tuple-element.22.hits, f32[128,2]{1,0:T(8,128)S(1)} %get-tuple-element.25.gates, bf16[128,1024]{1,0:T(8,128)(2,1)S(1)} %get-tuple-element.26.second), custom_call_target="tpu_custom_call" | custom-call | tf_op jit(solution)/shard_map/combine/pallas_call | solution.py:702
  153.0 0.7 copy.14
Async XLA Ops:
  1.9 1.6 %copy-start = (bf16[2,1024,512]{2,1,0:T(8,128)(2,1)S(1)}, bf16[2,1024,512]{2,1,0:T(8,128)(2,1)}, u32[]{:S(2)}) copy-start(bf16[2,1024,512]{2,1,0:T(8,128)(2,1)} %up_own.1) | copy-start | bytes 6291460
  3.5 1.6 %copy-start.2 = (bf16[2,512,1024]{2,1,0:T(8,128)(2,1)S(1)}, bf16[2,512,1024]{2,1,0:T(8,128)(2,1)}, u32[]{:S(2)}) copy-start(bf16[2,512,1024]{2,1,0:T(8,128)(2,1)} %dn_own.1) | copy-start | bytes 6291460
  5.1 0.9 copy-start.4
  6.0 0.9 copy-start.6
  6.9 0.8 copy-start.8
  7.8 0.7 copy-start.9
  49.6 12.1 %copy-start.5 = (bf16[128,1024]{1,0:T(8,128)(2,1)S(1)}, bf16[128,1024]{1,0:T(8,128)(2,1)}, u32[]{:S(2)}) copy-start(bf16[128,1024]{1,0:T(8,128)(2,1)} %frames.3) | copy-start | bytes 786436
  49.6 12.0 %copy-start.7 = (f32[31,1024]{1,0:T(8,128)S(1)}, f32[31,1024]{1,0:T(8,128)}, u32[]{:S(2)}) copy-start(f32[31,1024]{1,0:T(8,128)} %conv_w.1) | copy-start | bytes 380932
  61.7 40.5 %copy-start.3 = (bf16[2,512,1024]{2,1,0:T(8,128)(2,1)S(1)}, bf16[2,512,1024]{2,1,0:T(8,128)(2,1)}, u32[]{:S(2)}) copy-start(bf16[2,512,1024]{2,1,0:T(8,128)(2,1)} %dn_own.1) | copy-start | bytes 6291460
  66.0 36.1 %copy-start.1 = (bf16[2,1024,512]{2,1,0:T(8,128)(2,1)S(1)}, bf16[2,1024,512]{2,1,0:T(8,128)(2,1)}, u32[]{:S(2)}) copy-start(bf16[2,1024,512]{2,1,0:T(8,128)(2,1)} %up_own.1) | copy-start | bytes 6291460

commit v3 on v2

--- a/solution.py
+++ b/solution.py
@@ -21,7 +21,7 @@
 NOTES = 16
 PLACES = EXPERT_DEVS * CELL
 MESH = pl.DeviceIdType.MESH
-ANY = pl.BlockSpec(memory_space=pl.ANY)
+ANY = pl.BlockSpec(memory_space=pltpu.HBM)
 VMEM = pl.BlockSpec(memory_space=pltpu.VMEM)
 SMEM = pl.BlockSpec(memory_space=pltpu.SMEM)
 BF = jnp.bfloat16
@@ -480,124 +480,26 @@
     return [me.at(dy=dy, dz=dz) for dy, dz in PLANE]
 
 
-def dispatch_kernel(hidden, hits, out, both, cells, send_sem, recv_sem, local_sem):
-    me = Place()
-    x, y, z = me.x, me.y, me.z
-    xr, xl, sib = me.at(dx=1), me.at(dx=-1), me.at(other=True)
-    greet(plane_peers(me) + [xr, xl, sib])
-    sends = Sends(send_sem, recv_sem)
-    start = sends.start
-    theirs = start(hidden, both.at[me.c], sib)
-    both[me.c] = hidden[...]
-    pick = hits[0] + hits[1]
-    theirs.wait_recv()
-    rows = jnp.dot(pick, both[...].reshape(2 * ROWS, D), preferred_element_type=F32)
-    cells[...] = rows.astype(BF).reshape(PLACES, 8, 128).reshape(NY, NZ, SUB, 128)
-    keep = pltpu.make_async_copy(cells.at[y, z], out.at[x, z, y], local_sem.at[0])
-    keep.start()
-    order = (0, 1, 7, 2, 6, 3, 5, 4)
-    direct = {}
-
-    def issue(dz):
-        for dy in range(NY):
-            if (dy, dz) != (0, 0):
-                src = cells.at[(y + dy) % NY, (z + dz) % NZ]
-                direct[dy, dz] = start(src, out.at[x, z, y], me.at(dy=dy, dz=dz))
-
-    ahead = 2
-    for dz in order[:ahead]:
-        issue(dz)
-    keep.wait()
-    right, left = (x + 1) % NX, (x + NX - 1) % NX
-    sideways, last = [], []
-
-    def relay(i):
-        group = (z - order[i] + NZ) % NZ
-        to_r, to_l = sideways[i]
-        to_r.wait_recv()
-        low = out.at[left, group, pl.ds(0, 2)]
-        last.append(start(low, low, xr))
-        to_l.wait_recv()
-        high = out.at[right, group, pl.ds(2, 2)]
-        last.append(start(high, high, xl))
-
-    for i, dz in enumerate(order):
-        if i + ahead < NZ:
-            issue(order[i + ahead])
-        for dy in range(NY):
-            if (dy, dz) != (0, 0):
-                direct[dy, dz].wait_recv()
-        block = out.at[x, (z - dz + NZ) % NZ]
-        sideways.append((start(block, block, xr), start(block, block, xl)))
-        if i >= 1:
-            relay(i - 1)
-    relay(NZ - 1)
-    for copy in last:
-        copy.wait_recv()
-    sends.finish()
-
-
-def dispatch(hidden, hits):
-    count = 32 + 4 * NZ
-    return pl.pallas_call(
-        dispatch_kernel,
-        out_shape=jax.ShapeDtypeStruct((NX, NZ, NY, SUB, 128), BF),
-        in_specs=[VMEM, VMEM],
-        out_specs=ANY,
-        scratch_shapes=[
-            pltpu.VMEM((2, ROWS, D), BF),
-            pltpu.VMEM((NY, NZ, SUB, 128), BF),
-            pltpu.SemaphoreType.DMA((count,)),
-            pltpu.SemaphoreType.DMA((count,)),
-            pltpu.SemaphoreType.DMA((1,)),
-        ],
-        compiler_params=pltpu.CompilerParams(
-            collective_id=2, has_side_effects=True, vmem_limit_bytes=24 << 20
-        ),
-        name="dispatch",
-    )(hidden, hits)
-
-
-def expert_kernel(core_ref, x_ref, up_own, dn_own, up_sib, dn_sib, out_ref):
-    rows = x_ref[0].reshape(PLACES, 8, 128).reshape(PLACES, D)
-    result = None
-    for up, down in ((up_own.at[0], dn_own.at[0]), (up_sib, dn_sib)):
-        upward = jnp.dot(rows, up[...], preferred_element_type=F32)
-        activated = (upward / (1.0 + jnp.exp(-upward))).astype(BF)
-        term = jnp.dot(activated, down[...], preferred_element_type=F32)
-        result = term if result is None else result + term
-    out_ref[0] = result.astype(BF).reshape(PLACES, 8, 128).reshape(PLACES * 8, 128)
-
-
-def expert(core, routed, w_up, w_down, up_sib, dn_sib):
-    block = pl.BlockSpec((1, PLACES * 8, 128), lambda i, c: (i, 0, 0))
-    return pl.pallas_call(
-        expert_kernel,
-        out_shape=jax.ShapeDtypeStruct(routed.shape, BF),
-        grid_spec=pltpu.PrefetchScalarGridSpec(
-            num_scalar_prefetch=1,
-            grid=(NX,),
-            in_specs=[
-                block,
-                pl.BlockSpec((1,) + w_up.shape[1:], lambda i, c: (c[0], 0, 0)),
-                pl.BlockSpec((1,) + w_down.shape[1:], lambda i, c: (c[0], 0, 0)),
-                pl.BlockSpec(up_sib.shape, lambda i, c: (0, 0)),
-                pl.BlockSpec(dn_sib.shape, lambda i, c: (0, 0)),
-            ],
-            out_specs=block,
-        ),
-        compiler_params=pltpu.CompilerParams(vmem_limit_bytes=40 << 20),
-        name="expert",
-    )(core, routed, w_up, w_down, up_sib, dn_sib)
-
-
-def combine_kernel(
-    part,
+ORDER = (0, 1, 7, 2, 6, 3, 5, 4)
+
+
+def experts_kernel(
+    hidden,
     hits,
     gates,
     second,
+    wup,
+    wdn,
+    up_sib,
+    dn_sib,
     block_out,
-    out,
+    both,
+    cells,
+    routed,
+    part,
+    up_own,
+    dn_own,
+    back,
     rel_r,
     rel_l,
     in_l,
@@ -612,99 +514,161 @@
     local_sem,
 ):
     me = Place()
-    x, y, z = me.x, me.y, me.z
-    xr, xl = me.at(dx=1), me.at(dx=-1)
+    x, y, z, c = me.x, me.y, me.z, me.c
+    xr, xl, sib = me.at(dx=1), me.at(dx=-1), me.at(other=True)
     right, left, across = (x + 1) % NX, (x + NX - 1) % NX, (x + 2) % NX
-    sib = me.at(other=True)
+    low, high = pl.ds(0, 2), pl.ds(2, 2)
+    load_up = pltpu.make_async_copy(wup.at[c], up_own, local_sem.at[0])
+    load_up.start()
+    load_dn = pltpu.make_async_copy(wdn.at[c], dn_own, local_sem.at[1])
+    load_dn.start()
     greet(plane_peers(me) + [xr, xl, sib])
     sends = Sends(send_sem, recv_sem)
     start = sends.start
-    order = (4, 3, 5, 2, 6, 1, 7, 0)
-    low, high = pl.ds(0, 2), pl.ds(2, 2)
-    begun, summed, final = [], [], []
-
-    def begin(i):
-        g = (z + order[i]) % NZ
+
+    theirs = start(hidden, both.at[c], sib)
+    both[c] = hidden[...]
+    pick = hits[0] + hits[1]
+    theirs.wait_recv()
+    rows = jnp.dot(pick, both[...].reshape(2 * ROWS, D), preferred_element_type=F32)
+    cells[...] = rows.astype(BF).reshape(PLACES, 8, 128).reshape(NY, NZ, SUB, 128)
+    keep = pltpu.make_async_copy(cells.at[y, z], routed.at[z, x, y], local_sem.at[2])
+    keep.start()
+
+    direct, sideways, relays, begun, summed, final = {}, [], [], [], [], []
+
+    def group(i):
+        return (z - ORDER[i] + NZ) % NZ
+
+    def issue(i):
+        dz = ORDER[i]
+        for dy in range(NY):
+            if (dy, dz) != (0, 0):
+                src = cells.at[(y + dy) % NY, (z + dz) % NZ]
+                direct[dy, dz] = start(src, routed.at[z, x, y], me.at(dy=dy, dz=dz))
+
+    def spread(i):
+        for dy in range(NY):
+            if (dy, ORDER[i]) == (0, 0):
+                keep.wait()
+            else:
+                direct[dy, ORDER[i]].wait_recv()
+        block = routed.at[group(i), x]
+        sideways.append((start(block, block, xr), start(block, block, xl)))
+
+    def relay(i):
+        g = group(i)
+        sideways[i][0].wait_recv()
+        one = routed.at[g, left, low]
+        to_r = start(one, one, xr)
+        sideways[i][1].wait_recv()
+        two = routed.at[g, right, high]
+        relays.append((to_r, start(two, two, xl)))
+
+    def compute(i):
+        g = group(i)
+        relays[i][0].wait_recv()
+        relays[i][1].wait_recv()
+        count = NX * NY * CELL
+        rows = routed[g].reshape(count * 8, 128).reshape(count, 8, 128).reshape(count, D)
+        result = None
+        for up, down in ((up_own, dn_own), (up_sib, dn_sib)):
+            upward = jnp.dot(rows, up[...], preferred_element_type=F32)
+            activated = (upward / (1.0 + jnp.exp(-upward))).astype(BF)
+            term = jnp.dot(activated, down[...], preferred_element_type=F32)
+            result = term if result is None else result + term
+        part[g] = result.astype(BF).reshape(count, 8, 128).reshape(NX, NY, SUB, 128)
         begun.append(
             (
-                start(part.at[across, g, low], rel_r.at[g], xr),
-                start(part.at[across, g, high], rel_l.at[g], xl),
-                start(part.at[right, g, high], in_l.at[g, high], xr),
-                start(part.at[left, g, low], in_r.at[g, low], xl),
+                start(part.at[g, across, low], rel_r.at[g], xr),
+                start(part.at[g, across, high], rel_l.at[g], xl),
+                start(part.at[g, right, high], in_l.at[g, high], xr),
+                start(part.at[g, left, low], in_r.at[g, low], xl),
             )
         )
 
     def add(i):
-        g = (z + order[i]) % NZ
+        g = group(i)
         begun[i][0].wait_recv()
-        sum_r[g] = (part[right, g, low].astype(F32) + rel_r[g].astype(F32)).astype(BF)
+        sum_r[g] = (part[g, right, low].astype(F32) + rel_r[g].astype(F32)).astype(BF)
         one = start(sum_r.at[g], in_l.at[g, low], xr)
         begun[i][1].wait_recv()
-        sum_l[g] = (part[left, g, high].astype(F32) + rel_l[g].astype(F32)).astype(BF)
-        two = start(sum_l.at[g], in_r.at[g, high], xl)
-        summed.append((one, two))
+        sum_l[g] = (part[g, left, high].astype(F32) + rel_l[g].astype(F32)).astype(BF)
+        summed.append((one, start(sum_l.at[g], in_r.at[g, high], xl)))
 
     def close(i):
-        g = (z + order[i]) % NZ
+        g = group(i)
         begun[i][2].wait_recv()
         begun[i][3].wait_recv()
         summed[i][0].wait_recv()
         summed[i][1].wait_recv()
         total[g] = (
-            part[x, g].astype(F32) + in_l[g].astype(F32) + in_r[g].astype(F32)
+            part[g, x].astype(F32) + in_l[g].astype(F32) + in_r[g].astype(F32)
         ).astype(BF)
         for dy in range(NY):
             src = total.at[g, (y + dy) % NY]
-            if (dy, order[i]) == (0, 0):
-                keep = pltpu.make_async_copy(src, out.at[y, z], local_sem.at[0])
-                keep.start()
-                final.append(keep)
+            if (dy, ORDER[i]) == (0, 0):
+                home = pltpu.make_async_copy(src, back.at[y, z], local_sem.at[3])
+                home.start()
+                final.append(home.wait)
             else:
-                start(src, out.at[y, z], me.at(dy=dy, dz=order[i]))
-                final.append(sends.copies[-1])
-
-    ahead = 3
+                copy = start(src, back.at[y, z], me.at(dy=dy, dz=-ORDER[i]))
+                final.append(copy.wait_recv)
+
+    ahead = 2
     for i in range(ahead):
-        begin(i)
-    for i in range(NZ):
-        if i + ahead < NZ:
-            begin(i + ahead)
-        add(i)
-        if i >= 1:
-            close(i - 1)
-    close(NZ - 1)
-    for copy in final[:-NY]:
-        copy.wait_recv()
-    final[-NY].wait()
-    for copy in final[-NY + 1 :]:
-        copy.wait_recv()
-
-    rows = out[...].reshape(PLACES * 8, 128).reshape(PLACES, 8, 128).reshape(PLACES, D)
+        issue(i)
+    for t in range(NZ + 4):
+        if t + ahead < NZ:
+            issue(t + ahead)
+        if t < NZ:
+            spread(t)
+        if 1 <= t <= NZ:
+            relay(t - 1)
+        if t == 2:
+            load_up.wait()
+            load_dn.wait()
+        if 2 <= t <= NZ + 1:
+            compute(t - 2)
+        if 3 <= t <= NZ + 2:
+            add(t - 3)
+        if 4 <= t:
+            close(t - 4)
+    for wait in final:
+        wait()
+
+    rows = back[...].reshape(PLACES * 8, 128).reshape(PLACES, 8, 128).reshape(PLACES, D)
     given = []
     for k in range(TOP):
         taken = lax.dot_general(
             hits[k], rows, (((0,), (0,)), ((), ())), preferred_element_type=F32
         )
         picked[k] = taken.astype(BF).reshape(2, ROWS, D)
-        given.append(start(picked.at[k, 1 - me.c], inbox.at[k], sib))
+        given.append(start(picked.at[k, 1 - c], inbox.at[k], sib))
     result = second[...].astype(F32)
     for k in range(TOP):
         given[k].wait_recv()
-        value = picked[k, me.c].astype(F32) + inbox[k].astype(F32)
+        value = picked[k, c].astype(F32) + inbox[k].astype(F32)
         result = result + gates[:, k : k + 1] * value
     block_out[...] = result.astype(BF)
     sends.finish()
 
 
-def combine(part, hits, gates, second):
-    count = 31 + 6 * NZ + TOP
+def experts(hidden, hits, gates, second, w_up, w_down, up_sib, dn_sib):
+    count = 1 + 31 + 4 * NZ + 6 * NZ + 31 + TOP
     cell = (SUB, 128)
     return pl.pallas_call(
-        combine_kernel,
+        experts_kernel,
         out_shape=jax.ShapeDtypeStruct(second.shape, BF),
-        in_specs=[VMEM] * 4,
+        in_specs=[VMEM] * 4 + [ANY] * 2 + [VMEM] * 2,
         out_specs=VMEM,
         scratch_shapes=[
+            pltpu.VMEM((2, ROWS, D), BF),
+            pltpu.VMEM((NY, NZ) + cell, BF),
+            pltpu.VMEM((NZ, NX, NY) + cell, BF),
+            pltpu.VMEM((NZ, NX, NY) + cell, BF),
+            pltpu.VMEM(up_sib.shape, BF),
+            pltpu.VMEM(dn_sib.shape, BF),
             pltpu.VMEM((NY, NZ) + cell, BF),
             pltpu.VMEM((NZ, 2) + cell, BF),
             pltpu.VMEM((NZ, 2) + cell, BF),
@@ -717,13 +681,13 @@
             pltpu.VMEM((TOP, ROWS, D), BF),
             pltpu.SemaphoreType.DMA((count,)),
             pltpu.SemaphoreType.DMA((count,)),
-            pltpu.SemaphoreType.DMA((1,)),
+            pltpu.SemaphoreType.DMA((4,)),
         ],
         compiler_params=pltpu.CompilerParams(
-            collective_id=3, has_side_effects=True, vmem_limit_bytes=32 << 20
+            collective_id=2, has_side_effects=True, vmem_limit_bytes=48 << 20
         ),
-        name="combine",
-    )(part, hits, gates, second)
+        name="experts",
+    )(hidden, hits, gates, second, w_up, w_down, up_sib, dn_sib)
 
 
 def local(frames, lengths, w_qkv, w_out, conv_w, w_router, expert_ids, w_up, w_down):
@@ -734,10 +698,7 @@
     second, hidden, gates, hits = middle(
         frames, mixed, wo.reshape(D, D), ng, conv_w, w_router, expert_ids
     )
-    routed = dispatch(hidden, hits)
-    core = (lax.axis_index("dp") % 2).reshape(1)
-    part = expert(core, routed.reshape(NX, -1, 128), w_up, w_down, up_sib, dn_sib)
-    return combine(part.reshape(routed.shape), hits, gates, second)
+    return experts(hidden, hits, gates, second, w_up, w_down, up_sib, dn_sib)
 
 
 def solution(mesh):

time: 156 us -> 151 us (0.968)
  Pallas kernels: 144 us -> 130 us
  local copies, waits for them, and re-layouts: 9.13 us -> 17.3 us
    pallas_call x3 -> x1, Pallas kernels: 86.9 us -> 72.9 us  [experts(): pl.pallas_call(experts_kernel, out_shape=jax.ShapeDtypeStruct(second.shap...]
    unnamed x23 -> x35, local copies, waits for them, and re-layouts: 9.13 us -> 17.3 us
where the time goes in v3:
time: 151 us; the launch traced here: 148 us
  Pallas kernels  130 us (86%)
  local copies, waits for them, and re-layouts  17.3 us (11%)
    pallas_call x1, Pallas kernels, experts(): pl.pallas_call(experts_kernel, out_shape=jax.ShapeDtypeStruct(second.shap...  72.9 us
    pallas_call x1, Pallas kernels, gather_all(): pl.pallas_call(gather_kernel, out_shape=(jax.ShapeDtypeStruct((8, ROWS, D...  35 us
    unnamed x35, local copies, waits for them, and re-layouts  17.3 us
    pallas_call x1, Pallas kernels, heads_back(): pl.pallas_call(heads_kernel, out_shape=(jax.ShapeDtypeStruct((8, ROWS, 12...  12 us
    pallas_call x1, Pallas kernels, attention(): pl.pallas_call(attention_kernel, grid=(1,), out_shape=jax.ShapeDtypeStruc...  6.15 us
    pallas_call x1, Pallas kernels, middle(): pl.pallas_call(middle_kernel, out_shape=(jax.ShapeDtypeStruct((ROWS, D),...  4.37 us

profile of v3, /device:TPU:7, one launch (start us, length us, event | category | flops | bytes accessed | tf_op | source)
XLA Modules:
  0.0 147.9 jit_solution(9265545659405570041)
XLA Ops:
  0.0 0.8 copy.10.ids
  0.8 0.0 copy-start
  0.8 1.6 %copy-done = bf16[2,1024,512]{2,1,0:T(8,128)(2,1)S(1)} copy-done((bf16[2,1024,512]{2,1,0:T(8,128)(2,1)S(1)}, bf16[2,1024,512]{2,1,0:T(8,128)(2,1)}, u32[]{:S(2)}) %copy-start) | copy-done | bytes 2097176
  2.4 0.0 copy-start.2
  2.4 1.6 %copy-done.2 = bf16[2,512,1024]{2,1,0:T(8,128)(2,1)S(1)} copy-done((bf16[2,512,1024]{2,1,0:T(8,128)(2,1)S(1)}, bf16[2,512,1024]{2,1,0:T(8,128)(2,1)}, u32[]{:S(2)}) %copy-start.2) | copy-done | bytes 2097176
  4.0 0.0 copy-start.7
  4.0 0.9 copy-done.7
  4.9 0.0 copy-start.12
  4.9 0.9 copy-done.12
  5.8 0.0 copy-start.14
  5.8 0.8 copy-done.14
  6.7 0.0 copy-start.15
  6.7 0.7 copy-done.15
  7.3 35.0 %gather.1 = (bf16[8,128,1024]{2,1,0:T(8,128)(2,1)S(1)}, bf16[8,16,128]{2,1,0:T(8,128)(2,1)S(1)}, bf16[4,8,32,896]{3,2,1,0:T(8,128)(2,1)S(1)}, bf16[1024,512]{1,0:T(8,128)(2,1)S(1)}, bf16[512,1024]{1,0:T(8,128)(2,1)S(1)}) custom-call(bf16[128,1024]{1,0:T(8,128)(2,1)S(1)} %copy-done.7, s32[1,4]{1,0:T(1,128)S(1)} %copy-done.15, s32[128,2]{1,0:T(8,128)S(1)} %copy.10.ids, ...), custom_call_target="tpu_custom_call" | custom-call | tf_op jit(solution)/shard_map/gather/pallas_call | solution.py:278
  42.3 0.0 copy-start.5
  42.4 1.0 copy-done.5
  43.3 6.2 %attention.1.mixed = bf16[8,128,128]{2,1,0:T(8,128)(2,1)S(1)} custom-call(bf16[8,128,1024]{2,1,0:T(8,128)(2,1)S(1)} %get-tuple-element.16.x_ref, bf16[8,16,128]{2,1,0:T(8,128)(2,1)S(1)} %get-tuple-element.17.notes_ref.notes, bf16[1024,896]{1,0:T(8,128)(2,1)S(1)} %bitcast.2), custom_call_target="tpu_custom_call" | custom-call | tf_op jit(solution)/shard_map/attention/pallas_call | solution.py:328
  49.5 0.0 copy-start.8
  49.5 12.0 %heads_back.1 = (bf16[8,128,128]{2,1,0:T(8,128)(2,1)S(1)}, bf16[4,8,32,1024]{3,2,1,0:T(8,128)(2,1)S(1)}) custom-call(bf16[8,128,128]{2,1,0:T(8,128)(2,1)S(1)} %attention.1.mixed, bf16[4,8,32,896]{3,2,1,0:T(8,128)(2,1)S(1)} %get-tuple-element.18.wg), custom_call_target="tpu_custom_call" | custom-call | tf_op jit(solution)/shard_map/heads_back/pallas_call | solution.py:368
  61.5 0.0 copy-start.3
  61.5 1.3 copy-done.3
  62.9 0.0 copy-start.10
  62.9 0.7 copy-done.10
  63.6 0.0 copy-start.1
  63.6 1.9 %copy.11.w_router = bf16[1024,64]{1,0:T(8,128)(2,1)} copy(bf16[1024,64]{0,1:T(8,128)(2,1)} %param.14) | data formatting | bytes 262144 | tf_op args[5]
  65.5 0.0 copy-done.8
  65.5 0.0 copy-start.4
  65.5 1.6 %copy-done.4 = bf16[4,8,32,1024]{3,2,1,0:T(8,128)(2,1)S(1)} copy-done((bf16[4,8,32,1024]{3,2,1,0:T(8,128)(2,1)S(1)}, bf16[4,8,32,1024]{3,2,1,0:T(8,128)(2,1)}, u32[]{:S(2)}) %copy-start.4) | copy-done | bytes 2097176
  67.1 0.0 copy-start.9
  67.1 0.9 copy-done.9
  68.0 0.0 copy-start.11
  68.0 0.9 copy-done.11
  69.0 0.0 copy-start.13
  69.0 0.9 copy-done.13
  69.9 0.0 copy-start.6
  69.9 4.4 %middle.1 = (bf16[128,1024]{1,0:T(8,128)(2,1)S(1)}, bf16[128,1024]{1,0:T(8,128)(2,1)S(1)}, f32[128,2]{1,0:T(8,128)S(1)}, bf16[2,320,256]{2,1,0:T(8,128)(2,1)S(1)}) custom-call(bf16[128,1024]{1,0:T(8,128)(2,1)S(1)} %copy-done.8, bf16[8,128,128]{2,1,0:T(8,128)(2,1)S(1)} %copy-done.11, bf16[1024,1024]{1,0:T(8,128)(2,1)S(1)} %bitcast.3, ...), custom_call_target="tpu_custom_call" | custom-call | tf_op jit(solution)/shard_map/middle/pallas_call | solution.py:457
  74.2 0.0 copy-done.1
  74.3 0.0 copy-done.6
  74.3 72.9 %experts.1 = bf16[128,1024]{1,0:T(8,128)(2,1)S(1)} custom-call(bf16[128,1024]{1,0:T(8,128)(2,1)S(1)} %get-tuple-element.21.hidden, bf16[2,320,256]{2,1,0:T(8,128)(2,1)S(1)} %get-tuple-element.22.hits, f32[128,2]{1,0:T(8,128)S(1)} %get-tuple-element.23.gates, bf16[128,1024]{1,0:T(8,128)(2,1)S(1)} %get-tuple-element.24.second, ...), custom_call_target="tpu_custom_call" | custom-call | tf_op jit(solution)/shard_map/experts/pallas_call | solution.py:660
  147.2 0.7 copy.14
Async XLA Ops:
  0.8 1.6 %copy-start = (bf16[2,1024,512]{2,1,0:T(8,128)(2,1)S(1)}, bf16[2,1024,512]{2,1,0:T(8,128)(2,1)}, u32[]{:S(2)}) copy-start(bf16[2,1024,512]{2,1,0:T(8,128)(2,1)} %wup.3) | copy-start | bytes 6291460
  2.4 1.6 %copy-start.2 = (bf16[2,512,1024]{2,1,0:T(8,128)(2,1)S(1)}, bf16[2,512,1024]{2,1,0:T(8,128)(2,1)}, u32[]{:S(2)}) copy-start(bf16[2,512,1024]{2,1,0:T(8,128)(2,1)} %wdn.3) | copy-start | bytes 6291460
  4.0 0.9 copy-start.7
  4.9 0.9 copy-start.12
  5.8 0.8 copy-start.14
  6.7 0.7 copy-start.15
  42.3 1.0 copy-start.5
  49.5 16.0 %copy-start.8 = (bf16[128,1024]{1,0:T(8,128)(2,1)S(1)}, bf16[128,1024]{1,0:T(8,128)(2,1)}, u32[]{:S(2)}) copy-start(bf16[128,1024]{1,0:T(8,128)(2,1)} %frames.3) | copy-start | bytes 786436
  61.5 1.3 copy-start.3
  62.9 0.7 copy-start.10
  63.6 10.7 %copy-start.1 = (bf16[2,1024,512]{2,1,0:T(8,128)(2,1)S(1)}, bf16[2,1024,512]{2,1,0:T(8,128)(2,1)}, u32[]{:S(2)}) copy-start(bf16[2,1024,512]{2,1,0:T(8,128)(2,1)} %wup.3) | copy-start | bytes 6291460
  65.5 1.6 %copy-start.4 = (bf16[4,8,32,1024]{3,2,1,0:T(8,128)(2,1)S(1)}, bf16[4,8,32,1024]{3,2,1,0:T(8,128)(2,1)}, u32[]{:S(2)}) copy-start(bf16[4,8,32,1024]{3,2,1,0:T(8,128)(2,1)} %copy-done.3) | copy-start | bytes 6291460
  67.1 0.9 copy-start.9
  68.0 0.9 copy-start.11
  69.0 0.9 copy-start.13
  69.9 4.4 %copy-start.6 = (bf16[512,1024]{1,0:T(8,128)(2,1)S(1)}, bf16[512,1024]{1,0:T(8,128)(2,1)}, u32[]{:S(2)}) copy-start(bf16[512,1024]{1,0:T(8,128)(2,1)} %copy-done.5) | copy-start | bytes 3145732

commit v4 on v0

v4 whole, which is shorter than its diff:
```python
import types

import jax
import jax.numpy as jnp
from jax import lax
from jax.experimental import pallas as pl
from jax.experimental.pallas import tpu as pltpu
from jax.sharding import PartitionSpec as P

HEAD_DIM = 64
ROWS = 128
D = 1024
TOP = 2
NX, NY, NZ = 4, 4, 8
EXPERT_DEVS = NY * NZ
CAP = 5
CELL = 2 * CAP
SUB = CELL * D // 128
QCOLS = 384
OCOLS = 512
NOTES = 16
PLACES = EXPERT_DEVS * CELL
MESH = pl.DeviceIdType.MESH
HBM = pl.BlockSpec(memory_space=pltpu.HBM)
VMEM = pl.BlockSpec(memory_space=pltpu.VMEM)
SMEM = pl.BlockSpec(memory_space=pltpu.SMEM)
BF = jnp.bfloat16
F32 = jnp.float32


def normalize(values):
    mean_value = jnp.mean(values, axis=-1, keepdims=True)
    centred = values - mean_value
    variance = jnp.mean(centred * centred, axis=-1, keepdims=True)
    return centred * lax.rsqrt(variance + 1e-05)


class Place:
    def __init__(self):
        dp, ex = lax.axis_index("dp"), lax.axis_index("expert")
        self.dp, self.ex = dp, ex
        self.x, self.c = dp // 2, dp % 2
        self.y, self.z = ex // NZ, ex % NZ

    def at(self, dx=0, dy=0, dz=0, other=False):
        x, y, z = (self.x + dx + NX) % NX, (self.y + dy + NY) % NY, (self.z + dz + NZ) % NZ
        c = 1 - self.c if other else self.c
        return (x * 2 + c, y * NZ + z)


class Sends:
    def __init__(self, send_sem, recv_sem):
        self.send_sem, self.recv_sem, self.copies = send_sem, recv_sem, []

    def start(self, src, dst, device):
        at = len(self.copies)
        copy = pltpu.make_async_remote_copy(
            src_ref=src,
            dst_ref=dst,
            send_sem=self.send_sem.at[at],
            recv_sem=self.recv_sem.at[at],
            device_id=device,
            device_id_type=MESH,
        )
        copy.start()
        self.copies.append(copy)
        return copy

    def finish(self):
        for copy in self.copies:
            copy.wait_send()


def greet(devices):
    barrier = pltpu.get_barrier_semaphore()
    for device in devices:
        pl.semaphore_signal(barrier, inc=1, device_id=device, device_id_type=MESH)
    pl.semaphore_wait(barrier, len(devices))


def run_tasks(tasks):
    waiting = [(next(task, None), task) for task in tasks]
    waiting = [entry for entry in waiting if entry[0] is not None]
    while waiting:
        first = min(range(len(waiting)), key=lambda n: waiting[n][0][0])
        (_, copy), task = waiting.pop(first)
        if copy is not None:
            copy.wait_recv()
        following = next(task, None)
        if following is not None:
            waiting.append((following, task))


def write_notes(lengths, ids, notes):
    rows = lax.broadcasted_iota(jnp.int32, (8, ROWS), 0)
    lanes = lax.broadcasted_iota(jnp.int32, (8, ROWS), 1)
    marks = jnp.zeros((8, ROWS), F32)
    begin = jnp.int32(0)
    for u in range(4):
        end = begin + lengths[0, u]
        inside = (rows == u) & (lanes >= begin) & (lanes < end)
        marks = jnp.where(inside, 1.0, marks)
        begin = end
    for k in range(TOP):
        marks = jnp.where(rows == 4 + k, ids[k : k + 1, :].astype(F32), marks)
    full = jnp.concatenate([marks, jnp.zeros((NOTES - 8, ROWS), F32)], axis=0)
    notes[...] = full.astype(BF)


def attend(qkv, marks):
    first_head = lax.broadcasted_iota(jnp.int32, (ROWS, 128), 1) < HEAD_DIM
    same = lax.dot_general(marks, marks, (((0,), (0,)), ((), ())), preferred_element_type=F32)
    allowed = same > 0.5
    q, k, v = (qkv[:, 128 * i : 128 * i + 128] for i in range(3))
    mixed = []
    for h in range(2):
        mine = jnp.where(first_head == (h == 0), q, jnp.zeros_like(q))
        scores = lax.dot_general(mine, k, (((1,), (1,)), ((), ())), preferred_element_type=F32)
        scores = jnp.where(allowed, scores * HEAD_DIM ** (-0.5), -1e30)
        highest = jnp.max(scores, axis=-1, keepdims=True)
        expo = jnp.exp(scores - highest)
        probs = (expo / jnp.sum(expo, axis=-1, keepdims=True)).astype(BF)
        mixed.append(jnp.dot(probs, v, preferred_element_type=F32))
    return jnp.where(first_head, mixed[0], mixed[1]).astype(BF)


def middle(
    dp, frames, rows, wo, notes, conv_w, w_router, ids, second, hidden, gates, hits, shifted, masks
):
    core = dp % 2
    added = jnp.dot(rows, wo, preferred_element_type=F32)
    first = (frames[...].astype(F32) + added).astype(BF).astype(F32)
    conv_in = normalize(first)

    square = (ROWS, ROWS)
    at_row = lax.broadcasted_iota(jnp.int32, square, 0)
    at_lane = lax.broadcasted_iota(jnp.int32, square, 1)
    marks = notes[dp, :4, :].astype(F32)
    same = lax.dot_general(marks, marks, (((0,), (0,)), ((), ())), preferred_element_type=F32)
    begin = jnp.min(jnp.where(same > 0.5, at_lane, ROWS), axis=1, keepdims=True)
    end = jnp.max(jnp.where(same > 0.5, at_lane + 1, 0), axis=1, keepdims=True)
    low = jnp.broadcast_to(begin, square) - at_row + 15
    high = jnp.broadcast_to(end, square) - at_row + 15
    for j in range(31):
        masks[j] = jnp.where((low <= j) & (j < high), 1.0, 0.0)

    edge = jnp.zeros((16, D), F32)
    padded = jnp.concatenate([edge, conv_in, edge], axis=0)
    for s in range(8):
        shifted[s] = padded[s : s + 152]

    def columns(i, carry):
        lanes = pl.ds(pl.multiple_of(i * 128, 128), 128)
        total = jnp.zeros((ROWS, 128), F32)
        for j in range(31):
            window = shifted[(j + 1) % 8, pl.ds((j + 1) // 8 * 8, ROWS), lanes]
            total = total + (conv_w[pl.ds(j, 1), lanes] * window) * masks[j]
        shifted[0, pl.ds(0, ROWS), lanes] = total
        return carry

    lax.fori_loop(0, D // 128, columns, 0)
    conv_out = shifted[0, pl.ds(0, ROWS), :]
    after = (first + conv_out / (1.0 + jnp.exp(-conv_out))).astype(BF)
    second[...] = after
    normed = normalize(after.astype(F32)).astype(BF)
    hidden[...] = normed

    logits = lax.dot_general(
        w_router[...], normed, (((1,), (1,)), ((), ())), preferred_element_type=F32
    )
    each = lax.broadcasted_iota(jnp.int32, (2 * EXPERT_DEVS, ROWS), 0)
    for k in range(TOP):
        chosen = jnp.where(ids[k : k + 1, :] == each, logits, 0.0)
        gate = 1.0 / (1.0 + jnp.exp(-jnp.sum(chosen, axis=0, keepdims=True)))
        turned = jnp.where(at_row == at_lane, jnp.broadcast_to(gate, square), 0.0)
        gates[:, k : k + 1] = jnp.sum(turned, axis=1, keepdims=True)

    before = (at_row < at_lane).astype(BF)
    place = lax.broadcasted_iota(jnp.int32, (PLACES, ROWS), 0)
    for s in range(2):
        names = notes[dp // 2 * 2 + s, 4:8, :].astype(F32).astype(jnp.int32)
        held = jnp.zeros((2 * EXPERT_DEVS, 1), F32)
        for k in range(TOP):
            name = names[k : k + 1]
            ones = jnp.where(name == each, 1.0, 0.0)
            earlier = jnp.dot(ones.astype(BF), before, preferred_element_type=F32) + held
            rank = jnp.sum(ones * earlier, axis=0, keepdims=True).astype(jnp.int32)
            held = held + jnp.sum(ones, axis=1, keepdims=True)
            slot = name // 2 * CELL + s * CAP + rank
            slot = jnp.where(name % 2 == core, slot, -1)
            hits[k, :, pl.ds(s * ROWS, ROWS)] = jnp.where(place == slot, 1.0, 0.0).astype(BF)


SCRATCH = dict(
    second=((ROWS, D), BF),
    hidden=((ROWS, D), BF),
    gates=((ROWS, TOP), F32),
    hits=((TOP, PLACES, 2 * ROWS), BF),
    up_sib=((D, 512), BF),
    dn_sib=((512, D), BF),
    up_own=((D, 512), BF),
    dn_own=((512, D), BF),
    xc=((ROWS, D), BF),
    xg=((8, ROWS, D), BF),
    notes=((NOTES, ROWS), BF),
    ng=((8, NOTES, ROWS), BF),
    wq=((NY, NZ, 32, QCOLS), BF),
    wo=((NY, NZ, 32, D), BF),
    mixed=((8, ROWS, 128), BF),
    heads=((8, ROWS, 128), BF),
    shifted=((8, 152, D), F32),
    masks=((31, ROWS, ROWS), F32),
    both=((2, ROWS, D), BF),
    cells=((NY, NZ, SUB, 128), BF),
    routed=((NZ, NX, NY, SUB, 128), BF),
    part=((NZ, NX, NY, SUB, 128), BF),
    back=((NY, NZ, SUB, 128), BF),
    rel_r=((NZ, 2, SUB, 128), BF),
    rel_l=((NZ, 2, SUB, 128), BF),
    in_l=((NZ, NY, SUB, 128), BF),
    in_r=((NZ, NY, SUB, 128), BF),
    sum_r=((NZ, 2, SUB, 128), BF),
    sum_l=((NZ, 2, SUB, 128), BF),
    total=((NZ, NY, SUB, 128), BF),
    picked=((TOP, 2, ROWS, D), BF),
    inbox=((TOP, ROWS, D), BF),
)
COPIES = 256


def block_kernel(
    frames, lengths, ids, conv_w, w_router, wqkv, wout, wup, wdn, block_out, *scratch
):
    send_sem, recv_sem, local_sem = scratch[len(SCRATCH) :]
    ref = types.SimpleNamespace(**dict(zip(SCRATCH, scratch)))
    me = Place()
    sib = me.at(other=True)
    others = [((me.dp + o) % 8, me.ex) for o in range(1, 8)]
    half = pl.ds(pl.multiple_of(me.c * OCOLS, 128), OCOLS)
    loads = [
        (wout.at[:, half], ref.wo.at[me.y, me.z, :, half]),
        (wup.at[me.c], ref.up_own),
        (wdn.at[me.c], ref.dn_own),
    ]
    for part in range(3):
        columns = pl.ds(pl.multiple_of(part * D + me.dp * 128, 128), 128)
        loads.append((wqkv.at[:, columns], ref.wq.at[me.y, me.z, :, pl.ds(part * 128, 128)]))
    loads = [
        pltpu.make_async_copy(src, dst, local_sem.at[n]) for n, (src, dst) in enumerate(loads)
    ]
    for copy in loads:
        copy.start()
    greet(plane_peers(me) + others)
    sends = Sends(send_sem, recv_sem)
    for copy in loads:
        copy.wait()
    front(me, sends, others, frames, lengths, ids, conv_w, w_router, wup, wdn, ref)
    experts(me, sends, block_out, ref, local_sem)
    sends.finish()


def front(me, sends, others, frames, lengths, ids, conv_w, w_router, wup, wdn, ref):
    start = sends.start
    xc, xg, notes, ng, wq, wo = ref.xc, ref.xg, ref.notes, ref.ng, ref.wq, ref.wo
    mixed, heads = ref.mixed, ref.heads
    x, c, y, z, dp = me.x, me.c, me.y, me.z, me.dp
    sib = me.at(other=True)
    xr, xl = me.at(dx=1), me.at(dx=-1)
    yu, yd = me.at(dy=1), me.at(dy=-1)
    zu, zd = me.at(dz=1), me.at(dz=-1)
    half = pl.ds(pl.multiple_of(c * OCOLS, 128), OCOLS)

    def yy(d):
        return (y + d + NY) % NY

    def zz(d):
        return (z + d + NZ) % NZ

    swaps, noted, given, ready = [], [], [], set()

    def out_weights():
        def block(dy):
            return wo.at[yy(dy), z, :, half]

        def bundle(dz, first=0, count=NY):
            return wo.at[pl.ds(first, count), zz(dz), :, half]

        def share(dz):
            given.append(start(bundle(dz), bundle(dz), sib))

        to_u = start(block(0), block(0), yu)
        to_d = start(block(0), block(0), yd)
        yield 1.5, to_u
        over = start(block(-1), block(-1), yu)
        yield 1.5, to_d
        yield 3.0, over
        up = start(bundle(0), bundle(0), zu)
        down = start(bundle(0), bundle(0), zd)
        share(0)
        for s in range(1, 4):
            yield 3.0 + 3.4 * s, up
            if s < 3:
                up = start(bundle(-s), bundle(-s), zu)
            else:
                up = start(bundle(-s, 0, 2), bundle(-s, 0, 2), zu)
            share(-s)
            yield 3.0 + 3.4 * s, down
            if s < 3:
                down = start(bundle(s), bundle(s), zd)
            else:
                down = start(bundle(s, 2, 2), bundle(s, 2, 2), zd)
            share(s)
        yield 15.0, up
        yield 15.0, down
        share(4)

    def qkv_weights():
        def block(dy, dz):
            return wq.at[yy(dy), zz(dz)]

        def available(dz):
            one = block(0, dz)
            spread.append((dz, start(one, one, yu), start(one, one, yd)))

        def pass_on(n, time):
            dz, to_u, to_d = spread[n]
            yield time, to_u
            yield time, to_d
            one = block(-1, dz) if dz in (0, 1, 2, 3) else block(1, dz)
            last.append(start(one, one, yu if dz in (0, 1, 2, 3) else yd))

        spread, last = [], []
        up = start(block(0, 0), block(0, 0), zu)
        down = start(block(0, 0), block(0, 0), zd)
        available(0)
        for s in range(1, 4):
            yield 1.2 * s, up
            up = start(block(0, -s), block(0, -s), zu)
            available(-s)
            yield 1.2 * s, down
            if s < 3:
                down = start(block(0, s), block(0, s), zd)
            available(s)
            yield from pass_on(2 * s - 2, 1.2 * s + 0.1)
            if s > 1:
                yield from pass_on(2 * s - 3, 1.2 * s + 0.1)
        yield 4.8, up
        available(4)
        for n in (5, 6, 7):
            yield from pass_on(n, 5.0 + 0.4 * n)
        for copy in last:
            yield 8.4, copy
        ready.add("w")

    def row_blocks():
        xc[...] = normalize(frames[...].astype(F32)).astype(BF)
        xg[dp] = xc[...]
        low, high = pl.ds(0, 64), pl.ds(64, 64)
        left = xg.at[((x + NX - 1) % NX) * 2 + c]
        right = xg.at[((x + 1) % NX) * 2 + c]
        across = xg.at[((x + 2) % NX) * 2 + c]
        r_low = start(xc.at[low], xg.at[dp, low], xr)
        l_high = start(xc.at[high], xg.at[dp, high], xl)
        to_sib = start(xc, xg.at[dp], sib)
        r_high = start(xc.at[high], xg.at[dp, high], xr)
        l_low = start(xc.at[low], xg.at[dp, low], xl)
        write_notes(lengths, ids, notes)
        ng[dp] = notes[...]
        for device in others:
            noted.append(start(notes, ng.at[dp], device))
        swaps.append(start(wup.at[1 - c], ref.up_sib, sib))
        swaps.append(start(wdn.at[1 - c], ref.dn_sib, sib))
        yield 4.5, r_low
        over_r = start(left.at[low], left.at[low], xr)
        yield 4.5, l_high
        over_l = start(right.at[high], right.at[high], xl)
        yield 8.0, r_high
        left_sib = start(left, left, sib)
        yield 8.0, l_low
        right_sib = start(right, right, sib)
        yield 8.45, to_sib
        for copy in noted:
            yield 8.45, copy
        ready.add(0)
        ready.add(1)
        yield 9.5, over_r
        yield 9.5, over_l
        across_sib = start(across, across, sib)
        yield 10.5, left_sib
        yield 10.5, right_sib
        ready.add(2)
        yield 11.5, across_sib
        ready.add(3)

    def attention():
        pairs = (
            (dp, x * 2 + 1 - c),
            ((x + NX - 1) % NX * 2 + c, (x + 1) % NX * 2 + c),
            ((x + NX - 1) % NX * 2 + 1 - c, (x + 1) % NX * 2 + 1 - c),
            ((x + 2) % NX * 2 + c, (x + 2) % NX * 2 + 1 - c),
        )
        for n, pair in enumerate(pairs):
            yield 8.6 + n, None
            assert "w" in ready and n in ready
            rows = jnp.concatenate([xg[b] for b in pair], axis=0)
            qkv = jnp.dot(rows, wq[...].reshape(D, QCOLS), preferred_element_type=F32).astype(BF)
            for m, b in enumerate(pair):
                marks = ng[b, :4, :].astype(F32)
                result = attend(qkv[m * ROWS : (m + 1) * ROWS], marks)
                if (n, m) == (0, 0):
                    heads[dp] = result
                else:
                    mixed[b] = result
                    back.append(start(mixed.at[b], heads.at[dp], (b, me.ex)))

    back = []
    run_tasks([qkv_weights(), out_weights(), row_blocks(), attention()])
    for copy in given + back + swaps:
        copy.wait_recv()
    rows = jnp.concatenate([heads[b] for b in range(8)], axis=1)
    middle(
        dp,
        frames,
        rows,
        wo[...].reshape(D, D),
        ng,
        conv_w,
        w_router,
        ids,
        ref.second,
        ref.hidden,
        ref.gates,
        ref.hits,
        ref.shifted,
        ref.masks,
    )


PLANE = [(dy, dz) for dz in range(NZ) for dy in range(NY) if (dy, dz) != (0, 0)]


def plane_peers(me):
    return [me.at(dy=dy, dz=dz) for dy, dz in PLANE]


ORDER = (0, 1, 7, 2, 6, 3, 5, 4)


def experts(me, sends, block_out, ref, local_sem):
    start = sends.start
    hidden, hits, gates, second = ref.hidden, ref.hits, ref.gates, ref.second
    both, cells, routed, part, back = ref.both, ref.cells, ref.routed, ref.part, ref.back
    rel_r, rel_l, in_l, in_r = ref.rel_r, ref.rel_l, ref.in_l, ref.in_r
    sum_r, sum_l, total, picked, inbox = ref.sum_r, ref.sum_l, ref.total, ref.picked, ref.inbox
    x, y, z, c = me.x, me.y, me.z, me.c
    xr, xl, sib = me.at(dx=1), me.at(dx=-1), me.at(other=True)
    right, left, across = (x + 1) % NX, (x + NX - 1) % NX, (x + 2) % NX
    low, high = pl.ds(0, 2), pl.ds(2, 2)

    theirs = start(hidden, both.at[c], sib)
    both[c] = hidden[...]
    pick = hits[0] + hits[1]
    theirs.wait_recv()
    rows = jnp.dot(pick, both[...].reshape(2 * ROWS, D), preferred_element_type=F32)
    cells[...] = rows.astype(BF).reshape(PLACES, 8, 128).reshape(NY, NZ, SUB, 128)
    keep = pltpu.make_async_copy(cells.at[y, z], routed.at[z, x, y], local_sem.at[6])
    keep.start()

    direct, sideways, relays, begun, summed, final = {}, [], [], [], [], []

    def group(i):
        return (z - ORDER[i] + NZ) % NZ

    def issue(i):
        dz = ORDER[i]
        for dy in range(NY):
            if (dy, dz) != (0, 0):
                src = cells.at[(y + dy) % NY, (z + dz) % NZ]
                direct[dy, dz] = start(src, routed.at[z, x, y], me.at(dy=dy, dz=dz))

    def spread(i):
        for dy in range(NY):
            if (dy, ORDER[i]) == (0, 0):
                keep.wait()
            else:
                direct[dy, ORDER[i]].wait_recv()
        block = routed.at[group(i), x]
        sideways.append((start(block, block, xr), start(block, block, xl)))

    def relay(i):
        g = group(i)
        sideways[i][0].wait_recv()
        one = routed.at[g, left, low]
        to_r = start(one, one, xr)
        sideways[i][1].wait_recv()
        two = routed.at[g, right, high]
        relays.append((to_r, start(two, two, xl)))

    def compute(i):
        g = group(i)
        relays[i][0].wait_recv()
        relays[i][1].wait_recv()
        count = NX * NY * CELL
        rows = routed[g].reshape(count * 8, 128).reshape(count, 8, 128).reshape(count, D)
        result = None
        for up, down in ((ref.up_own, ref.dn_own), (ref.up_sib, ref.dn_sib)):
            upward = jnp.dot(rows, up[...], preferred_element_type=F32)
            activated = (upward / (1.0 + jnp.exp(-upward))).astype(BF)
            term = jnp.dot(activated, down[...], preferred_element_type=F32)
            result = term if result is None else result + term
        part[g] = result.astype(BF).reshape(count, 8, 128).reshape(NX, NY, SUB, 128)
        begun.append(
            (
                start(part.at[g, across, low], rel_r.at[g], xr),
                start(part.at[g, across, high], rel_l.at[g], xl),
                start(part.at[g, right, high], in_l.at[g, high], xr),
                start(part.at[g, left, low], in_r.at[g, low], xl),
            )
        )

    def add(i):
        g = group(i)
        begun[i][0].wait_recv()
        sum_r[g] = (part[g, right, low].astype(F32) + rel_r[g].astype(F32)).astype(BF)
        one = start(sum_r.at[g], in_l.at[g, low], xr)
        begun[i][1].wait_recv()
        sum_l[g] = (part[g, left, high].astype(F32) + rel_l[g].astype(F32)).astype(BF)
        summed.append((one, start(sum_l.at[g], in_r.at[g, high], xl)))

    def close(i):
        g = group(i)
        begun[i][2].wait_recv()
        begun[i][3].wait_recv()
        summed[i][0].wait_recv()
        summed[i][1].wait_recv()
        total[g] = (
            part[g, x].astype(F32) + in_l[g].astype(F32) + in_r[g].astype(F32)
        ).astype(BF)
        for dy in range(NY):
            src = total.at[g, (y + dy) % NY]
            if (dy, ORDER[i]) == (0, 0):
                home = pltpu.make_async_copy(src, back.at[y, z], local_sem.at[7])
                home.start()
                final.append(home.wait)
            else:
                copy = start(src, back.at[y, z], me.at(dy=dy, dz=-ORDER[i]))
                final.append(copy.wait_recv)

    ahead = 2
    for i in range(ahead):
        issue(i)
    for t in range(NZ + 4):
        if t + ahead < NZ:
            issue(t + ahead)
        if t < NZ:
            spread(t)
        if 1 <= t <= NZ:
            relay(t - 1)
        if 2 <= t <= NZ + 1:
            compute(t - 2)
        if 3 <= t <= NZ + 2:
            add(t - 3)
        if 4 <= t:
            close(t - 4)
    for wait in final:
        wait()

    rows = back[...].reshape(PLACES * 8, 128).reshape(PLACES, 8, 128).reshape(PLACES, D)
    given = []
    for k in range(TOP):
        taken = lax.dot_general(
            hits[k], rows, (((0,), (0,)), ((), ())), preferred_element_type=F32
        )
        picked[k] = taken.astype(BF).reshape(2, ROWS, D)
        given.append(start(picked.at[k, 1 - c], inbox.at[k], sib))
    result = second[...].astype(F32)
    for k in range(TOP):
        given[k].wait_recv()
        value = picked[k, c].astype(F32) + inbox[k].astype(F32)
        result = result + gates[:, k : k + 1] * value
    block_out[...] = result


def local(frames, lengths, w_qkv, w_out, conv_w, w_router, expert_ids, w_up, w_down):
    result = pl.pallas_call(
        block_kernel,
        out_shape=jax.ShapeDtypeStruct((ROWS, D), F32),
        in_specs=[VMEM, SMEM, VMEM, VMEM, VMEM] + [HBM] * 4,
        out_specs=VMEM,
        scratch_shapes=[pltpu.VMEM(*shape) for shape in SCRATCH.values()]
        + [
            pltpu.SemaphoreType.DMA((COPIES,)),
            pltpu.SemaphoreType.DMA((COPIES,)),
            pltpu.SemaphoreType.DMA((8,)),
        ],
        compiler_params=pltpu.CompilerParams(
            collective_id=0, has_side_effects=True, vmem_limit_bytes=60 << 20
        ),
        name="block",
    )(frames, lengths, expert_ids.T, conv_w, w_router.T, w_qkv, w_out, w_up, w_down)
    return result.astype(BF)


def solution(mesh):
    in_specs = (
        P(("dp", "expert"), None),
        P(("dp", "expert"), None),
        P("expert", None),
        P("expert", None),
        P(),
        P(),
        P(("dp", "expert"), None),
        P("expert", None, "dp"),
        P("expert", "dp", None),
    )
    out_specs = P(("dp", "expert"), None)
    return jax.shard_map(local, mesh=mesh, in_specs=in_specs, out_specs=out_specs, check_vma=False)
```

time: 346 us -> 122 us (0.35)
  waiting for transfers between devices: 237 us -> 0 us
  Pallas kernels: 0 us -> 118 us
  local copies, waits for them, and re-layouts: 32.4 us -> 0 us
  matrix products: 22 us -> 0 us
  blocking collectives: 18.3 us -> 0 us
  between operations: 13.4 us -> 0.01 us
  starting transfers between devices: 9.87 us -> 0 us
  other arithmetic: 11.4 us -> 1.78 us
    all_gather x3 -> x0, waiting for transfers between devices: 176 us -> none  [the longest x1 72.4 us: local(): lax.all_gather(w_qkv, 'expert', axis=0, tiled=True)]
    pallas_call x0 -> x1, Pallas kernels: none -> 118 us  [local(): pl.pallas_call(block_kernel, out_shape=jax.ShapeDtypeStruct((ROWS, D), F3...]
    reduce_scatter x1 -> x0, waiting for transfers between devices: 43.2 us -> none  [local(): lax.psum_scatter(jnp.einsum('nef,efd->ned', activated, w_down, preferred_...]
    dot_general x6 -> x0, matrix products: 20.4 us -> none  [the longest x1 9.73 us: local(): jnp.einsum('nef,efd->ned', activated, w_down, preferred_element_type=jnp....]
    all_to_all x1 -> x0, blocking collectives: 18.3 us -> none  [local(): lax.all_to_all(outgoing, 'expert', split_axis=0, concat_axis=0, tiled=True)]
    all_to_all x1 -> x0, waiting for transfers between devices: 16.3 us -> none  [local(): lax.all_to_all(summed, 'expert', split_axis=0, concat_axis=0, tiled=True)]
    scatter x1 -> x0, local copies, waits for them, and re-layouts: 12.2 us -> none  [local(): table = jnp.full((group_size * capacity, EXP_DEV), count_rows, jnp.int32)...]
    all_to_all x1 -> x0, starting transfers between devices: 9.57 us -> none  [local(): lax.all_to_all(summed, 'expert', split_axis=0, concat_axis=0, tiled=True)]
  transfers between devices with their start and end apart: 5 -> 0, of which waited for: 5 -> 0; matrix products, arithmetic and copies ran while one was open for 10% -> 0% of each run, Pallas kernels for 0% -> 0%
where the time goes in v4:
time: 122 us; the launch traced here: 120 us
  Pallas kernels  118 us (97%)
  other arithmetic  1.78 us (1%)
    pallas_call x1, Pallas kernels, local(): pl.pallas_call(block_kernel, out_shape=jax.ShapeDtypeStruct((ROWS, D), F3...  118 us

profile of v4, /device:TPU:7, one launch (start us, length us, event | category | flops | bytes accessed | tf_op | source)
XLA Modules:
  0.0 119.8 jit_solution(16275981399793816772)
XLA Ops:
  0.0 118.0 %block.1 = f32[128,1024]{1,0:T(8,128)} custom-call(bf16[128,1024]{1,0:T(8,128)(2,1)} %frames.1, s32[1,4]{1,0:T(1,128)} %lengths.1, s32[2,128]{1,0:T(2,128)} %bitcast.3, f32[31,1024]{1,0:T(8,128)} %conv_w.1, bf16[64,1024]{1,0:T(8,128)(2,1)} %bitcast.2, bf16[32,3072]{1,0:T(8,128)(2,1)} %wqkv.1, bf16[32,1024]{1,0:T(8,128)(2,1)} %wout.1, ...), custom_call_target="tpu_custom_call" | custom-call | tf_op jit(solution)/shard_map/block/pallas_call | solution.py:585
  118.1 1.8 %convert_element_type.3 = bf16[128,1024]{1,0:T(8,128)(2,1)} convert(f32[128,1024]{1,0:T(8,128)} %block.1) | non-fusion elementwise | flops 131072 | bytes 786432 | tf_op jit(solution)/shard_map/convert_element_type | solution.py:601

commit v5 on v4

--- a/solution.py
+++ b/solution.py
@@ -1,3 +1,4 @@
+import math
 import types
 
 import jax
@@ -49,26 +50,42 @@
 
 
 class Sends:
-    def __init__(self, send_sem, recv_sem):
-        self.send_sem, self.recv_sem, self.copies = send_sem, recv_sem, []
-
-    def start(self, src, dst, device):
-        at = len(self.copies)
+    def __init__(self, send_sem, recv_sem, ruler):
+        self.send_sem, self.recv_sem, self.ruler = send_sem, recv_sem, ruler
+        self.slots, self.sent = 0, [0]
+
+    def slot(self):
+        self.slots += 1
+        assert self.slots <= self.recv_sem.shape[0]
+        return self.slots - 1
+
+    def start(self, src, dst, device, slot=None):
+        slot = self.slot() if slot is None else slot
+        length = math.prod(src.shape) // 128
+        if self.sent[-1] + length > self.ruler.shape[0]:
+            self.sent.append(0)
+        self.sent[-1] += length
         copy = pltpu.make_async_remote_copy(
             src_ref=src,
             dst_ref=dst,
-            send_sem=self.send_sem.at[at],
-            recv_sem=self.recv_sem.at[at],
+            send_sem=self.send_sem.at[len(self.sent) - 1],
+            recv_sem=self.recv_sem.at[slot],
             device_id=device,
             device_id_type=MESH,
         )
         copy.start()
-        self.copies.append(copy)
         return copy
 
+    def measure(self, length, sem):
+        piece = self.ruler.at[pl.ds(0, length)]
+        pltpu.make_async_copy(piece, piece, sem).wait()
+
+    def arrive(self, slot, length):
+        self.measure(length, self.recv_sem.at[slot])
+
     def finish(self):
-        for copy in self.copies:
-            copy.wait_send()
+        for n, length in enumerate(self.sent):
+            self.measure(length, self.send_sem.at[n])
 
 
 def greet(devices):
@@ -124,14 +141,9 @@
     return jnp.where(first_head, mixed[0], mixed[1]).astype(BF)
 
 
-def middle(
-    dp, frames, rows, wo, notes, conv_w, w_router, ids, second, hidden, gates, hits, shifted, masks
-):
+def plan(dp, notes, hits, masks):
     core = dp % 2
-    added = jnp.dot(rows, wo, preferred_element_type=F32)
-    first = (frames[...].astype(F32) + added).astype(BF).astype(F32)
-    conv_in = normalize(first)
-
+    each = lax.broadcasted_iota(jnp.int32, (2 * EXPERT_DEVS, ROWS), 0)
     square = (ROWS, ROWS)
     at_row = lax.broadcasted_iota(jnp.int32, square, 0)
     at_lane = lax.broadcasted_iota(jnp.int32, square, 1)
@@ -143,37 +155,6 @@
     high = jnp.broadcast_to(end, square) - at_row + 15
     for j in range(31):
         masks[j] = jnp.where((low <= j) & (j < high), 1.0, 0.0)
-
-    edge = jnp.zeros((16, D), F32)
-    padded = jnp.concatenate([edge, conv_in, edge], axis=0)
-    for s in range(8):
-        shifted[s] = padded[s : s + 152]
-
-    def columns(i, carry):
-        lanes = pl.ds(pl.multiple_of(i * 128, 128), 128)
-        total = jnp.zeros((ROWS, 128), F32)
-        for j in range(31):
-            window = shifted[(j + 1) % 8, pl.ds((j + 1) // 8 * 8, ROWS), lanes]
-            total = total + (conv_w[pl.ds(j, 1), lanes] * window) * masks[j]
-        shifted[0, pl.ds(0, ROWS), lanes] = total
-        return carry
-
-    lax.fori_loop(0, D // 128, columns, 0)
-    conv_out = shifted[0, pl.ds(0, ROWS), :]
-    after = (first + conv_out / (1.0 + jnp.exp(-conv_out))).astype(BF)
-    second[...] = after
-    normed = normalize(after.astype(F32)).astype(BF)
-    hidden[...] = normed
-
-    logits = lax.dot_general(
-        w_router[...], normed, (((1,), (1,)), ((), ())), preferred_element_type=F32
-    )
-    each = lax.broadcasted_iota(jnp.int32, (2 * EXPERT_DEVS, ROWS), 0)
-    for k in range(TOP):
-        chosen = jnp.where(ids[k : k + 1, :] == each, logits, 0.0)
-        gate = 1.0 / (1.0 + jnp.exp(-jnp.sum(chosen, axis=0, keepdims=True)))
-        turned = jnp.where(at_row == at_lane, jnp.broadcast_to(gate, square), 0.0)
-        gates[:, k : k + 1] = jnp.sum(turned, axis=1, keepdims=True)
 
     before = (at_row < at_lane).astype(BF)
     place = lax.broadcasted_iota(jnp.int32, (PLACES, ROWS), 0)
@@ -191,6 +172,51 @@
             hits[k, :, pl.ds(s * ROWS, ROWS)] = jnp.where(place == slot, 1.0, 0.0).astype(BF)
 
 
+def middle(
+    frames, rows, wo, conv_w, w_router, ids, second, hidden, gates, shifted, masks
+):
+    square = (ROWS, ROWS)
+    at_row = lax.broadcasted_iota(jnp.int32, square, 0)
+    at_lane = lax.broadcasted_iota(jnp.int32, square, 1)
+    halves = [
+        jnp.dot(rows, wo[n].reshape(D, OCOLS), preferred_element_type=F32) for n in range(2)
+    ]
+    added = jnp.concatenate(halves, axis=1)
+    first = (frames[...].astype(F32) + added).astype(BF).astype(F32)
+    conv_in = normalize(first)
+
+    edge = jnp.zeros((16, D), F32)
+    padded = jnp.concatenate([edge, conv_in, edge], axis=0)
+    for s in range(8):
+        shifted[s] = padded[s : s + 152]
+
+    def columns(i, carry):
+        lanes = pl.ds(pl.multiple_of(i * 128, 128), 128)
+        total = jnp.zeros((ROWS, 128), F32)
+        for j in range(31):
+            window = shifted[(j + 1) % 8, pl.ds((j + 1) // 8 * 8, ROWS), lanes]
+            total = total + (conv_w[pl.ds(j, 1), lanes] * window) * masks[j]
+        shifted[0, pl.ds(0, ROWS), lanes] = total
+        return carry
+
+    lax.fori_loop(0, D // 128, columns, 0)
+    conv_out = shifted[0, pl.ds(0, ROWS), :]
+    after = (first + conv_out / (1.0 + jnp.exp(-conv_out))).astype(BF)
+    second[...] = after
+    normed = normalize(after.astype(F32)).astype(BF)
+    hidden[...] = normed
+
+    logits = lax.dot_general(
+        w_router[...], normed, (((1,), (1,)), ((), ())), preferred_element_type=F32
+    )
+    each = lax.broadcasted_iota(jnp.int32, (2 * EXPERT_DEVS, ROWS), 0)
+    for k in range(TOP):
+        chosen = jnp.where(ids[k : k + 1, :] == each, logits, 0.0)
+        gate = 1.0 / (1.0 + jnp.exp(-jnp.sum(chosen, axis=0, keepdims=True)))
+        turned = jnp.where(at_row == at_lane, jnp.broadcast_to(gate, square), 0.0)
+        gates[:, k : k + 1] = jnp.sum(turned, axis=1, keepdims=True)
+
+
 SCRATCH = dict(
     second=((ROWS, D), BF),
     hidden=((ROWS, D), BF),
@@ -205,7 +231,7 @@
     notes=((NOTES, ROWS), BF),
     ng=((8, NOTES, ROWS), BF),
     wq=((NY, NZ, 32, QCOLS), BF),
-    wo=((NY, NZ, 32, D), BF),
+    wo=((2, NY, NZ, 32, OCOLS), BF),
     mixed=((8, ROWS, 128), BF),
     heads=((8, ROWS, 128), BF),
     shifted=((8, 152, D), F32),
@@ -224,8 +250,9 @@
     total=((NZ, NY, SUB, 128), BF),
     picked=((TOP, 2, ROWS, D), BF),
     inbox=((TOP, ROWS, D), BF),
+    ruler=((20480, 128), BF),
 )
-COPIES = 256
+SEND_SLOTS, RECV_SLOTS = 3, 121
 
 
 def block_kernel(
@@ -238,7 +265,7 @@
     others = [((me.dp + o) % 8, me.ex) for o in range(1, 8)]
     half = pl.ds(pl.multiple_of(me.c * OCOLS, 128), OCOLS)
     loads = [
-        (wout.at[:, half], ref.wo.at[me.y, me.z, :, half]),
+        (wout.at[:, half], ref.wo.at[me.c, me.y, me.z]),
         (wup.at[me.c], ref.up_own),
         (wdn.at[me.c], ref.dn_own),
     ]
@@ -251,10 +278,12 @@
     for copy in loads:
         copy.start()
     greet(plane_peers(me) + others)
-    sends = Sends(send_sem, recv_sem)
-    for copy in loads:
+    sends = Sends(send_sem, recv_sem, ref.ruler)
+    for copy in loads[:1] + loads[3:]:
         copy.wait()
     front(me, sends, others, frames, lengths, ids, conv_w, w_router, wup, wdn, ref)
+    for copy in loads[1:3]:
+        copy.wait()
     experts(me, sends, block_out, ref, local_sem)
     sends.finish()
 
@@ -268,88 +297,89 @@
     xr, xl = me.at(dx=1), me.at(dx=-1)
     yu, yd = me.at(dy=1), me.at(dy=-1)
     zu, zd = me.at(dz=1), me.at(dz=-1)
-    half = pl.ds(pl.multiple_of(c * OCOLS, 128), OCOLS)
-
     def yy(d):
         return (y + d + NY) % NY
 
     def zz(d):
         return (z + d + NZ) % NZ
 
-    swaps, noted, given, ready = [], [], [], set()
+    swaps, noted, given, heard, ready = *(sends.slot() for _ in range(4)), set()
 
     def out_weights():
-        def block(dy):
-            return wo.at[yy(dy), z, :, half]
-
-        def bundle(dz, first=0, count=NY):
-            return wo.at[pl.ds(first, count), zz(dz), :, half]
-
-        def share(dz):
-            given.append(start(bundle(dz), bundle(dz), sib))
-
-        to_u = start(block(0), block(0), yu)
-        to_d = start(block(0), block(0), yd)
-        yield 1.5, to_u
-        over = start(block(-1), block(-1), yu)
-        yield 1.5, to_d
-        yield 3.0, over
-        up = start(bundle(0), bundle(0), zu)
-        down = start(bundle(0), bundle(0), zd)
-        share(0)
-        for s in range(1, 4):
-            yield 3.0 + 3.4 * s, up
-            if s < 3:
-                up = start(bundle(-s), bundle(-s), zu)
-            else:
-                up = start(bundle(-s, 0, 2), bundle(-s, 0, 2), zu)
-            share(-s)
-            yield 3.0 + 3.4 * s, down
-            if s < 3:
-                down = start(bundle(s), bundle(s), zd)
-            else:
-                down = start(bundle(s, 2, 2), bundle(s, 2, 2), zd)
-            share(s)
-        yield 15.0, up
-        yield 15.0, down
-        share(4)
+        def block(dy, dz):
+            return wo.at[c, yy(dy), zz(dz)]
+
+        def share(dy, dz):
+            start(block(dy, dz), block(dy, dz), sib, given)
+
+        def along_z(dy, time):
+            up = start(block(dy, 0), block(dy, 0), zu)
+            down = start(block(dy, 0), block(dy, 0), zd)
+            share(dy, 0)
+            for s in range(1, 4):
+                yield time + 2.6 * s, up
+                if s < 3 or dy in (0, 2):
+                    up = start(block(dy, -s), block(dy, -s), zu)
+                share(dy, -s)
+                yield time + 2.6 * s + 0.1, down
+                if s < 3 or dy in (1, -1):
+                    down = start(block(dy, s), block(dy, s), zd)
+                share(dy, s)
+            yield time + 10.4, up if dy in (0, 2) else down
+            share(dy, 4)
+
+        def from_above():
+            yield 1.9, to_d
+            yield from along_z(1, 2.0)
+
+        def from_across():
+            yield 2.0, None
+            yield 4.1, overs[0]
+            yield from along_z(2, 4.2)
+
+        to_u = start(block(0, 0), block(0, 0), yu)
+        to_d = start(block(0, 0), block(0, 0), yd)
+        overs = []
+
+        def from_below():
+            yield 1.9, to_u
+            overs.append(start(block(-1, 0), block(-1, 0), yu))
+            yield from along_z(-1, 2.0)
+
+        return [along_z(0, 0.0), from_below(), from_above(), from_across()]
 
     def qkv_weights():
         def block(dy, dz):
             return wq.at[yy(dy), zz(dz)]
 
         def available(dz):
-            one = block(0, dz)
-            spread.append((dz, start(one, one, yu), start(one, one, yd)))
+            one, slot = block(0, dz), sends.slot()
+            start(one, one, yu, slot)
+            start(one, one, yd, slot)
+            spread.append((dz, slot))
 
         def pass_on(n, time):
-            dz, to_u, to_d = spread[n]
-            yield time, to_u
-            yield time, to_d
-            one = block(-1, dz) if dz in (0, 1, 2, 3) else block(1, dz)
-            last.append(start(one, one, yu if dz in (0, 1, 2, 3) else yd))
-
-        spread, last = [], []
-        up = start(block(0, 0), block(0, 0), zu)
-        down = start(block(0, 0), block(0, 0), zd)
+            dz, slot = spread[n]
+            yield time, None
+            sends.arrive(slot, 2 * 32 * QCOLS // 128)
+            one = block(-1, dz) if dz in (0, 1, 2, -3) else block(1, dz)
+            start(one, one, yu if dz in (0, 1, 2, -3) else yd, last)
+
+        spread, last = [], sends.slot()
+        order = (1, -1, 2, -2, 3, -3, 4)
+        direct = [
+            start(block(0, 0), block(0, 0), me.at(dz=dz)) for dz in order
+        ]
         available(0)
-        for s in range(1, 4):
-            yield 1.2 * s, up
-            up = start(block(0, -s), block(0, -s), zu)
-            available(-s)
-            yield 1.2 * s, down
-            if s < 3:
-                down = start(block(0, s), block(0, s), zd)
-            available(s)
-            yield from pass_on(2 * s - 2, 1.2 * s + 0.1)
-            if s > 1:
-                yield from pass_on(2 * s - 3, 1.2 * s + 0.1)
-        yield 4.8, up
-        available(4)
-        for n in (5, 6, 7):
-            yield from pass_on(n, 5.0 + 0.4 * n)
-        for copy in last:
-            yield 8.4, copy
+        for n, dz in enumerate(order):
+            yield 2.0 + 0.5 * n, direct[n]
+            available(-dz)
+            if n >= 3:
+                yield from pass_on(n - 3, 2.1 + 0.5 * n)
+        for n in range(4, 8):
+            yield from pass_on(n, 4.2 + 0.6 * n)
+        yield 10.2, None
+        sends.arrive(last, NZ * 32 * QCOLS // 128)
         ready.add("w")
 
     def row_blocks():
@@ -367,29 +397,30 @@
         write_notes(lengths, ids, notes)
         ng[dp] = notes[...]
         for device in others:
-            noted.append(start(notes, ng.at[dp], device))
-        swaps.append(start(wup.at[1 - c], ref.up_sib, sib))
-        swaps.append(start(wdn.at[1 - c], ref.dn_sib, sib))
-        yield 4.5, r_low
+            start(notes, ng.at[dp], device, noted)
+        start(wup.at[1 - c], ref.up_sib, sib, swaps)
+        start(wdn.at[1 - c], ref.dn_sib, sib, swaps)
+        yield 5.5, r_low
         over_r = start(left.at[low], left.at[low], xr)
-        yield 4.5, l_high
+        yield 5.5, l_high
         over_l = start(right.at[high], right.at[high], xl)
-        yield 8.0, r_high
+        yield 8.5, r_high
         left_sib = start(left, left, sib)
-        yield 8.0, l_low
+        yield 8.5, l_low
         right_sib = start(right, right, sib)
-        yield 8.45, to_sib
-        for copy in noted:
-            yield 8.45, copy
+        yield 8.6, to_sib
+        yield 8.6, None
+        sends.arrive(noted, 7 * NOTES)
         ready.add(0)
         ready.add(1)
-        yield 9.5, over_r
-        yield 9.5, over_l
+        plan(dp, ng, ref.hits, ref.masks)
+        yield 10.0, over_r
+        yield 10.0, over_l
         across_sib = start(across, across, sib)
         yield 10.5, left_sib
         yield 10.5, right_sib
         ready.add(2)
-        yield 11.5, across_sib
+        yield 12.0, across_sib
         ready.add(3)
 
     def attention():
@@ -400,7 +431,7 @@
             ((x + 2) % NX * 2 + c, (x + 2) % NX * 2 + 1 - c),
         )
         for n, pair in enumerate(pairs):
-            yield 8.6 + n, None
+            yield 10.3 + n, None
             assert "w" in ready and n in ready
             rows = jnp.concatenate([xg[b] for b in pair], axis=0)
             qkv = jnp.dot(rows, wq[...].reshape(D, QCOLS), preferred_element_type=F32).astype(BF)
@@ -411,26 +442,23 @@
                     heads[dp] = result
                 else:
                     mixed[b] = result
-                    back.append(start(mixed.at[b], heads.at[dp], (b, me.ex)))
-
-    back = []
-    run_tasks([qkv_weights(), out_weights(), row_blocks(), attention()])
-    for copy in given + back + swaps:
-        copy.wait_recv()
+                    start(mixed.at[b], heads.at[dp], (b, me.ex), heard)
+
+    run_tasks([qkv_weights(), *out_weights(), row_blocks(), attention()])
+    sends.arrive(given, D * OCOLS // 128)
+    sends.arrive(heard, 7 * ROWS)
+    sends.arrive(swaps, 2 * D * 512 // 128)
     rows = jnp.concatenate([heads[b] for b in range(8)], axis=1)
     middle(
-        dp,
         frames,
         rows,
-        wo[...].reshape(D, D),
-        ng,
+        wo,
         conv_w,
         w_router,
         ids,
         ref.second,
         ref.hidden,
         ref.gates,
-        ref.hits,
         ref.shifted,
         ref.masks,
     )
@@ -443,7 +471,7 @@
     return [me.at(dy=dy, dz=dz) for dy, dz in PLANE]
 
 
-ORDER = (0, 1, 7, 2, 6, 3, 5, 4)
+ORDER = (0, 2, 6, 4, 3, 5, 1, 7)
 
 
 def experts(me, sends, block_out, ref, local_sem):
@@ -466,40 +494,40 @@
     keep = pltpu.make_async_copy(cells.at[y, z], routed.at[z, x, y], local_sem.at[6])
     keep.start()
 
-    direct, sideways, relays, begun, summed, final = {}, [], [], [], [], []
+    direct, sideways, relays, begun, closing = [], [], [], [], []
+    returned = sends.slot()
 
     def group(i):
         return (z - ORDER[i] + NZ) % NZ
 
     def issue(i):
         dz = ORDER[i]
+        direct.append(sends.slot())
         for dy in range(NY):
             if (dy, dz) != (0, 0):
                 src = cells.at[(y + dy) % NY, (z + dz) % NZ]
-                direct[dy, dz] = start(src, routed.at[z, x, y], me.at(dy=dy, dz=dz))
+                start(src, routed.at[z, x, y], me.at(dy=dy, dz=dz), direct[i])
 
     def spread(i):
-        for dy in range(NY):
-            if (dy, ORDER[i]) == (0, 0):
-                keep.wait()
-            else:
-                direct[dy, ORDER[i]].wait_recv()
+        if ORDER[i] == 0:
+            keep.wait()
+        sends.arrive(direct[i], (NY - (ORDER[i] == 0)) * SUB)
         block = routed.at[group(i), x]
         sideways.append((start(block, block, xr), start(block, block, xl)))
 
     def relay(i):
         g = group(i)
+        relays.append(sends.slot())
         sideways[i][0].wait_recv()
         one = routed.at[g, left, low]
-        to_r = start(one, one, xr)
+        start(one, one, xr, relays[i])
         sideways[i][1].wait_recv()
         two = routed.at[g, right, high]
-        relays.append((to_r, start(two, two, xl)))
+        start(two, two, xl, relays[i])
 
     def compute(i):
         g = group(i)
-        relays[i][0].wait_recv()
-        relays[i][1].wait_recv()
+        sends.arrive(relays[i], NY * SUB)
         count = NX * NY * CELL
         rows = routed[g].reshape(count * 8, 128).reshape(count, 8, 128).reshape(count, D)
         result = None
@@ -513,38 +541,33 @@
             (
                 start(part.at[g, across, low], rel_r.at[g], xr),
                 start(part.at[g, across, high], rel_l.at[g], xl),
-                start(part.at[g, right, high], in_l.at[g, high], xr),
-                start(part.at[g, left, low], in_r.at[g, low], xl),
             )
         )
+        closing.append(sends.slot())
+        start(part.at[g, right, high], in_l.at[g, high], xr, closing[i])
+        start(part.at[g, left, low], in_r.at[g, low], xl, closing[i])
 
     def add(i):
         g = group(i)
         begun[i][0].wait_recv()
         sum_r[g] = (part[g, right, low].astype(F32) + rel_r[g].astype(F32)).astype(BF)
-        one = start(sum_r.at[g], in_l.at[g, low], xr)
+        start(sum_r.at[g], in_l.at[g, low], xr, closing[i])
         begun[i][1].wait_recv()
         sum_l[g] = (part[g, left, high].astype(F32) + rel_l[g].astype(F32)).astype(BF)
-        summed.append((one, start(sum_l.at[g], in_r.at[g, high], xl)))
+        start(sum_l.at[g], in_r.at[g, high], xl, closing[i])
 
     def close(i):
         g = group(i)
-        begun[i][2].wait_recv()
-        begun[i][3].wait_recv()
-        summed[i][0].wait_recv()
-        summed[i][1].wait_recv()
+        sends.arrive(closing[i], 2 * NY * SUB)
         total[g] = (
             part[g, x].astype(F32) + in_l[g].astype(F32) + in_r[g].astype(F32)
         ).astype(BF)
         for dy in range(NY):
             src = total.at[g, (y + dy) % NY]
             if (dy, ORDER[i]) == (0, 0):
-                home = pltpu.make_async_copy(src, back.at[y, z], local_sem.at[7])
-                home.start()
-                final.append(home.wait)
+                back[y, z] = total[g, y]
             else:
-                copy = start(src, back.at[y, z], me.at(dy=dy, dz=-ORDER[i]))
-                final.append(copy.wait_recv)
+                start(src, back.at[y, z], me.at(dy=dy, dz=-ORDER[i]), returned)
 
     ahead = 2
     for i in range(ahead):
@@ -562,8 +585,7 @@
             add(t - 3)
         if 4 <= t:
             close(t - 4)
-    for wait in final:
-        wait()
+    sends.arrive(returned, (NY * NZ - 1) * SUB)
 
     rows = back[...].reshape(PLACES * 8, 128).reshape(PLACES, 8, 128).reshape(PLACES, D)
     given = []
@@ -589,8 +611,8 @@
         out_specs=VMEM,
         scratch_shapes=[pltpu.VMEM(*shape) for shape in SCRATCH.values()]
         + [
-            pltpu.SemaphoreType.DMA((COPIES,)),
-            pltpu.SemaphoreType.DMA((COPIES,)),
+            pltpu.SemaphoreType.DMA((SEND_SLOTS,)),
+            pltpu.SemaphoreType.DMA((RECV_SLOTS,)),
             pltpu.SemaphoreType.DMA((8,)),
         ],
         compiler_params=pltpu.CompilerParams(

time: 122 us -> 112 us (0.918)
  Pallas kernels: 118 us -> 108 us
    pallas_call x1, Pallas kernels: 118 us -> 108 us  [local(): pl.pallas_call(block_kernel, out_shape=jax.ShapeDtypeStruct((ROWS, D), F3...]
where the time goes in v5:
time: 112 us; the launch traced here: 110 us
  Pallas kernels  108 us (96%)
  other arithmetic  1.78 us (2%)
    pallas_call x1, Pallas kernels, local(): pl.pallas_call(block_kernel, out_shape=jax.ShapeDtypeStruct((ROWS, D), F3...  108 us

profile of v5, /device:TPU:7, one launch (start us, length us, event | category | flops | bytes accessed | tf_op | source)
XLA Modules:
  0.0 109.6 jit_solution(5109533984488935507)
XLA Ops:
  0.0 107.8 %block.1 = f32[128,1024]{1,0:T(8,128)} custom-call(bf16[128,1024]{1,0:T(8,128)(2,1)} %frames.1, s32[1,4]{1,0:T(1,128)} %lengths.1, s32[2,128]{1,0:T(2,128)} %bitcast.3, f32[31,1024]{1,0:T(8,128)} %conv_w.1, bf16[64,1024]{1,0:T(8,128)(2,1)} %bitcast.2, bf16[32,3072]{1,0:T(8,128)(2,1)} %wqkv.1, bf16[32,1024]{1,0:T(8,128)(2,1)} %wout.1, ...), custom_call_target="tpu_custom_call" | custom-call | tf_op jit(solution)/shard_map/block/pallas_call | solution.py:607
  107.8 1.8 %convert_element_type.3 = bf16[128,1024]{1,0:T(8,128)(2,1)} convert(f32[128,1024]{1,0:T(8,128)} %block.1) | non-fusion elementwise | flops 131072 | bytes 786432 | tf_op jit(solution)/shard_map/convert_element_type | solution.py:623

commit v6 on v5

--- a/solution.py
+++ b/solution.py
@@ -129,16 +129,23 @@
     same = lax.dot_general(marks, marks, (((0,), (0,)), ((), ())), preferred_element_type=F32)
     allowed = same > 0.5
     q, k, v = (qkv[:, 128 * i : 128 * i + 128] for i in range(3))
+    q = q * jnp.asarray(HEAD_DIM ** (-0.5), BF)
     mixed = []
     for h in range(2):
-        mine = jnp.where(first_head == (h == 0), q, jnp.zeros_like(q))
-        scores = lax.dot_general(mine, k, (((1,), (1,)), ((), ())), preferred_element_type=F32)
-        scores = jnp.where(allowed, scores * HEAD_DIM ** (-0.5), -1e30)
-        highest = jnp.max(scores, axis=-1, keepdims=True)
-        expo = jnp.exp(scores - highest)
-        probs = (expo / jnp.sum(expo, axis=-1, keepdims=True)).astype(BF)
-        mixed.append(jnp.dot(probs, v, preferred_element_type=F32))
-    return jnp.where(first_head, mixed[0], mixed[1]).astype(BF)
+        own = first_head == (h == 0)
+        scores = lax.dot_general(
+            jnp.where(own, q, jnp.zeros_like(q)),
+            k,
+            (((1,), (1,)), ((), ())),
+            preferred_element_type=F32,
+        )
+        scores = jnp.where(allowed, scores, -1e30)
+        expo = jnp.exp(scores - jnp.max(scores, axis=-1, keepdims=True)).astype(BF)
+        mixed.append(
+            jnp.dot(expo, jnp.where(own, v, jnp.ones_like(v)), preferred_element_type=F32)
+        )
+    sums = jnp.where(first_head, mixed[1], mixed[0])
+    return (jnp.where(first_head, mixed[0], mixed[1]) / pltpu.roll(sums, 64, 1)).astype(BF)
 
 
 def plan(dp, notes, hits, masks):
@@ -218,6 +225,9 @@
 
 
 SCRATCH = dict(
+    frames=((ROWS, D), BF),
+    conv_w=((31, D), F32),
+    w_router=((2 * EXPERT_DEVS, D), BF),
     second=((ROWS, D), BF),
     hidden=((ROWS, D), BF),
     gates=((ROWS, TOP), F32),
@@ -252,11 +262,11 @@
     inbox=((TOP, ROWS, D), BF),
     ruler=((20480, 128), BF),
 )
-SEND_SLOTS, RECV_SLOTS = 3, 121
+SEND_SLOTS, RECV_SLOTS = 3, 119
 
 
 def block_kernel(
-    frames, lengths, ids, conv_w, w_router, wqkv, wout, wup, wdn, block_out, *scratch
+    lengths, ids, frames, conv_w, w_router, wqkv, wout, wup, wdn, block_out, *scratch
 ):
     send_sem, recv_sem, local_sem = scratch[len(SCRATCH) :]
     ref = types.SimpleNamespace(**dict(zip(SCRATCH, scratch)))
@@ -265,9 +275,12 @@
     others = [((me.dp + o) % 8, me.ex) for o in range(1, 8)]
     half = pl.ds(pl.multiple_of(me.c * OCOLS, 128), OCOLS)
     loads = [
+        (frames, ref.frames),
         (wout.at[:, half], ref.wo.at[me.c, me.y, me.z]),
         (wup.at[me.c], ref.up_own),
         (wdn.at[me.c], ref.dn_own),
+        (conv_w, ref.conv_w),
+        (w_router, ref.w_router),
     ]
     for part in range(3):
         columns = pl.ds(pl.multiple_of(part * D + me.dp * 128, 128), 128)
@@ -279,16 +292,16 @@
         copy.start()
     greet(plane_peers(me) + others)
     sends = Sends(send_sem, recv_sem, ref.ruler)
-    for copy in loads[:1] + loads[3:]:
+    for copy in loads[1:2] + loads[6:]:
         copy.wait()
-    front(me, sends, others, frames, lengths, ids, conv_w, w_router, wup, wdn, ref)
-    for copy in loads[1:3]:
+    front(me, sends, others, loads, lengths, ids, wup, wdn, ref)
+    for copy in loads[2:4]:
         copy.wait()
     experts(me, sends, block_out, ref, local_sem)
     sends.finish()
 
 
-def front(me, sends, others, frames, lengths, ids, conv_w, w_router, wup, wdn, ref):
+def front(me, sends, others, loads, lengths, ids, wup, wdn, ref):
     start = sends.start
     xc, xg, notes, ng, wq, wo = ref.xc, ref.xg, ref.notes, ref.ng, ref.wq, ref.wo
     mixed, heads = ref.mixed, ref.heads
@@ -333,17 +346,15 @@
             yield from along_z(1, 2.0)
 
         def from_across():
-            yield 2.0, None
-            yield 4.1, overs[0]
-            yield from along_z(2, 4.2)
+            yield 2.4, over
+            yield from along_z(2, 2.5)
 
         to_u = start(block(0, 0), block(0, 0), yu)
         to_d = start(block(0, 0), block(0, 0), yd)
-        overs = []
+        over = start(block(0, 0), block(0, 0), me.at(dy=2))
 
         def from_below():
             yield 1.9, to_u
-            overs.append(start(block(-1, 0), block(-1, 0), yu))
             yield from along_z(-1, 2.0)
 
         return [along_z(0, 0.0), from_below(), from_above(), from_across()]
@@ -356,12 +367,16 @@
             one, slot = block(0, dz), sends.slot()
             start(one, one, yu, slot)
             start(one, one, yd, slot)
+            if len(spread) >= 5:
+                start(one, one, me.at(dy=2), last)
             spread.append((dz, slot))
 
         def pass_on(n, time):
             dz, slot = spread[n]
             yield time, None
             sends.arrive(slot, 2 * 32 * QCOLS // 128)
+            if n >= 5:
+                return
             one = block(-1, dz) if dz in (0, 1, 2, -3) else block(1, dz)
             start(one, one, yu if dz in (0, 1, 2, -3) else yd, last)
 
@@ -377,13 +392,14 @@
             if n >= 3:
                 yield from pass_on(n - 3, 2.1 + 0.5 * n)
         for n in range(4, 8):
-            yield from pass_on(n, 4.2 + 0.6 * n)
-        yield 10.2, None
+            yield from pass_on(n, 4.6 + 0.5 * n)
+        yield 8.8, None
         sends.arrive(last, NZ * 32 * QCOLS // 128)
         ready.add("w")
 
     def row_blocks():
-        xc[...] = normalize(frames[...].astype(F32)).astype(BF)
+        loads[0].wait()
+        xc[...] = normalize(ref.frames[...].astype(F32)).astype(BF)
         xg[dp] = xc[...]
         low, high = pl.ds(0, 64), pl.ds(64, 64)
         left = xg.at[((x + NX - 1) % NX) * 2 + c]
@@ -431,7 +447,7 @@
             ((x + 2) % NX * 2 + c, (x + 2) % NX * 2 + 1 - c),
         )
         for n, pair in enumerate(pairs):
-            yield 10.3 + n, None
+            yield (9.0, 9.6, 10.6, 12.1)[n], None
             assert "w" in ready and n in ready
             rows = jnp.concatenate([xg[b] for b in pair], axis=0)
             qkv = jnp.dot(rows, wq[...].reshape(D, QCOLS), preferred_element_type=F32).astype(BF)
@@ -449,12 +465,14 @@
     sends.arrive(heard, 7 * ROWS)
     sends.arrive(swaps, 2 * D * 512 // 128)
     rows = jnp.concatenate([heads[b] for b in range(8)], axis=1)
+    loads[4].wait()
+    loads[5].wait()
     middle(
-        frames,
+        ref.frames,
         rows,
         wo,
-        conv_w,
-        w_router,
+        ref.conv_w,
+        ref.w_router,
         ids,
         ref.second,
         ref.hidden,
@@ -472,6 +490,7 @@
 
 
 ORDER = (0, 2, 6, 4, 3, 5, 1, 7)
+STRAIGHT = 7
 
 
 def experts(me, sends, block_out, ref, local_sem):
@@ -491,7 +510,7 @@
     theirs.wait_recv()
     rows = jnp.dot(pick, both[...].reshape(2 * ROWS, D), preferred_element_type=F32)
     cells[...] = rows.astype(BF).reshape(PLACES, 8, 128).reshape(NY, NZ, SUB, 128)
-    keep = pltpu.make_async_copy(cells.at[y, z], routed.at[z, x, y], local_sem.at[6])
+    keep = pltpu.make_async_copy(cells.at[y, z], routed.at[z, x, y], local_sem.at[9])
     keep.start()
 
     direct, sideways, relays, begun, closing = [], [], [], [], []
@@ -537,18 +556,26 @@
             term = jnp.dot(activated, down[...], preferred_element_type=F32)
             result = term if result is None else result + term
         part[g] = result.astype(BF).reshape(count, 8, 128).reshape(NX, NY, SUB, 128)
+        closing.append(sends.slot())
+        if i >= STRAIGHT:
+            start(part.at[g, across, low], rel_r.at[g], me.at(dx=2), closing[i])
+            start(part.at[g, across, high], rel_l.at[g], me.at(dx=2), closing[i])
+            start(part.at[g, right], in_l.at[g], xr, closing[i])
+            start(part.at[g, left], in_r.at[g], xl, closing[i])
+            return
         begun.append(
             (
                 start(part.at[g, across, low], rel_r.at[g], xr),
                 start(part.at[g, across, high], rel_l.at[g], xl),
             )
         )
-        closing.append(sends.slot())
         start(part.at[g, right, high], in_l.at[g, high], xr, closing[i])
         start(part.at[g, left, low], in_r.at[g, low], xl, closing[i])
 
     def add(i):
         g = group(i)
+        if i >= STRAIGHT:
+            return
         begun[i][0].wait_recv()
         sum_r[g] = (part[g, right, low].astype(F32) + rel_r[g].astype(F32)).astype(BF)
         start(sum_r.at[g], in_l.at[g, low], xr, closing[i])
@@ -558,10 +585,11 @@
 
     def close(i):
         g = group(i)
-        sends.arrive(closing[i], 2 * NY * SUB)
-        total[g] = (
-            part[g, x].astype(F32) + in_l[g].astype(F32) + in_r[g].astype(F32)
-        ).astype(BF)
+        sends.arrive(closing[i], (2 + (i >= STRAIGHT)) * NY * SUB)
+        added = part[g, x].astype(F32) + in_l[g].astype(F32) + in_r[g].astype(F32)
+        if i >= STRAIGHT:
+            added = added + jnp.concatenate([rel_r[g], rel_l[g]], axis=0).astype(F32)
+        total[g] = added.astype(BF)
         for dy in range(NY):
             src = total.at[g, (y + dy) % NY]
             if (dy, ORDER[i]) == (0, 0):
@@ -572,7 +600,7 @@
     ahead = 2
     for i in range(ahead):
         issue(i)
-    for t in range(NZ + 4):
+    for t in range(NZ + 3):
         if t + ahead < NZ:
             issue(t + ahead)
         if t < NZ:
@@ -585,6 +613,7 @@
             add(t - 3)
         if 4 <= t:
             close(t - 4)
+    close(NZ - 1)
     sends.arrive(returned, (NY * NZ - 1) * SUB)
 
     rows = back[...].reshape(PLACES * 8, 128).reshape(PLACES, 8, 128).reshape(PLACES, D)
@@ -600,27 +629,27 @@
         given[k].wait_recv()
         value = picked[k, c].astype(F32) + inbox[k].astype(F32)
         result = result + gates[:, k : k + 1] * value
-    block_out[...] = result
+    block_out[...] = result.astype(BF)
 
 
 def local(frames, lengths, w_qkv, w_out, conv_w, w_router, expert_ids, w_up, w_down):
     result = pl.pallas_call(
         block_kernel,
-        out_shape=jax.ShapeDtypeStruct((ROWS, D), F32),
-        in_specs=[VMEM, SMEM, VMEM, VMEM, VMEM] + [HBM] * 4,
+        out_shape=jax.ShapeDtypeStruct((ROWS, D), BF),
+        in_specs=[SMEM, VMEM] + [HBM] * 7,
         out_specs=VMEM,
         scratch_shapes=[pltpu.VMEM(*shape) for shape in SCRATCH.values()]
         + [
             pltpu.SemaphoreType.DMA((SEND_SLOTS,)),
             pltpu.SemaphoreType.DMA((RECV_SLOTS,)),
-            pltpu.SemaphoreType.DMA((8,)),
+            pltpu.SemaphoreType.DMA((10,)),
         ],
         compiler_params=pltpu.CompilerParams(
             collective_id=0, has_side_effects=True, vmem_limit_bytes=60 << 20
         ),
         name="block",
-    )(frames, lengths, expert_ids.T, conv_w, w_router.T, w_qkv, w_out, w_up, w_down)
-    return result.astype(BF)
+    )(lengths, expert_ids.T, frames, conv_w, w_router.T, w_qkv, w_out, w_up, w_down)
+    return jnp.maximum(result, jnp.finfo(BF).min)
 
 
 def solution(mesh):

time: 112 us -> 108 us (0.964)
  Pallas kernels: 108 us -> 105 us
    pallas_call x1, Pallas kernels: 108 us -> 105 us  [local(): pl.pallas_call(block_kernel, out_shape=jax.ShapeDtypeStruct((ROWS, D), BF...]
    convert_element_type x1 -> x0, other arithmetic: 1.78 us -> none  [local(): return result.astype(BF)]
    max x0 -> x1, other arithmetic: none -> 1.68 us  [local(): return jnp.maximum(result, jnp.finfo(BF).min)]
where the time goes in v6:
time: 108 us; the launch traced here: 106 us
  Pallas kernels  105 us (97%)
  other arithmetic  1.68 us (2%)
    pallas_call x1, Pallas kernels, local(): pl.pallas_call(block_kernel, out_shape=jax.ShapeDtypeStruct((ROWS, D), BF...  105 us

profile of v6, /device:TPU:7, one launch (start us, length us, event | category | flops | bytes accessed | tf_op | source)
XLA Modules:
  0.0 106.4 jit_solution(2574923055043903646)
XLA Ops:
  0.0 104.7 %block.1 = bf16[128,1024]{1,0:T(8,128)(2,1)} custom-call(s32[1,4]{1,0:T(1,128)} %lengths.1, s32[2,128]{1,0:T(2,128)} %bitcast.3, bf16[128,1024]{1,0:T(8,128)(2,1)} %frames.1, f32[31,1024]{1,0:T(8,128)} %conv_w.1, bf16[64,1024]{1,0:T(8,128)(2,1)} %bitcast.2, bf16[32,3072]{1,0:T(8,128)(2,1)} %wqkv.1, bf16[32,1024]{1,0:T(8,128)(2,1)} %wout.1, ...), custom_call_target="tpu_custom_call" | custom-call | tf_op jit(solution)/shard_map/block/pallas_call | solution.py:636
  104.7 1.7 %broadcast_maximum_fusion = bf16[128,1024]{1,0:T(8,128)(2,1)} fusion(bf16[128,1024]{1,0:T(8,128)(2,1)} %block.1), kind=kLoop, calls=%fused_computation | loop fusion | flops 131072 | bytes 524288 | tf_op jit(solution)/shard_map/max | solution.py:652

commit v7 on v6

--- a/solution.py
+++ b/solution.py
@@ -180,7 +180,7 @@
 
 
 def middle(
-    frames, rows, wo, conv_w, w_router, ids, second, hidden, gates, shifted, masks
+    frames, rows, wo, conv_w, w_router, ids, second, hidden, gates, shifted, masks, swap
 ):
     square = (ROWS, ROWS)
     at_row = lax.broadcasted_iota(jnp.int32, square, 0)
@@ -212,6 +212,7 @@
     second[...] = after
     normed = normalize(after.astype(F32)).astype(BF)
     hidden[...] = normed
+    swap()
 
     logits = lax.dot_general(
         w_router[...], normed, (((1,), (1,)), ((), ())), preferred_element_type=F32
@@ -258,7 +259,7 @@
     sum_r=((NZ, 2, SUB, 128), BF),
     sum_l=((NZ, 2, SUB, 128), BF),
     total=((NZ, NY, SUB, 128), BF),
-    picked=((TOP, 2, ROWS, D), BF),
+    picked=((TOP, ROWS, D), BF),
     inbox=((TOP, ROWS, D), BF),
     ruler=((20480, 128), BF),
 )
@@ -294,10 +295,10 @@
     sends = Sends(send_sem, recv_sem, ref.ruler)
     for copy in loads[1:2] + loads[6:]:
         copy.wait()
-    front(me, sends, others, loads, lengths, ids, wup, wdn, ref)
+    theirs = front(me, sends, others, loads, lengths, ids, wup, wdn, ref)
     for copy in loads[2:4]:
         copy.wait()
-    experts(me, sends, block_out, ref, local_sem)
+    experts(me, sends, theirs, block_out, ref)
     sends.finish()
 
 
@@ -330,15 +331,15 @@
             down = start(block(dy, 0), block(dy, 0), zd)
             share(dy, 0)
             for s in range(1, 4):
-                yield time + 2.6 * s, up
+                yield time + 3.6 * s, up
                 if s < 3 or dy in (0, 2):
                     up = start(block(dy, -s), block(dy, -s), zu)
                 share(dy, -s)
-                yield time + 2.6 * s + 0.1, down
+                yield time + 3.6 * s + 0.1, down
                 if s < 3 or dy in (1, -1):
                     down = start(block(dy, s), block(dy, s), zd)
                 share(dy, s)
-            yield time + 10.4, up if dy in (0, 2) else down
+            yield time + 14.4, up if dy in (0, 2) else down
             share(dy, 4)
 
         def from_above():
@@ -465,6 +466,7 @@
     sends.arrive(heard, 7 * ROWS)
     sends.arrive(swaps, 2 * D * 512 // 128)
     rows = jnp.concatenate([heads[b] for b in range(8)], axis=1)
+    swapped = []
     loads[4].wait()
     loads[5].wait()
     middle(
@@ -479,7 +481,9 @@
         ref.gates,
         ref.shifted,
         ref.masks,
+        lambda: swapped.append(start(ref.hidden, ref.both.at[c], sib)),
     )
+    return swapped[0]
 
 
 PLANE = [(dy, dz) for dz in range(NZ) for dy in range(NY) if (dy, dz) != (0, 0)]
@@ -493,7 +497,7 @@
 STRAIGHT = 7
 
 
-def experts(me, sends, block_out, ref, local_sem):
+def experts(me, sends, theirs, block_out, ref):
     start = sends.start
     hidden, hits, gates, second = ref.hidden, ref.hits, ref.gates, ref.second
     both, cells, routed, part, back = ref.both, ref.cells, ref.routed, ref.part, ref.back
@@ -504,14 +508,12 @@
     right, left, across = (x + 1) % NX, (x + NX - 1) % NX, (x + 2) % NX
     low, high = pl.ds(0, 2), pl.ds(2, 2)
 
-    theirs = start(hidden, both.at[c], sib)
     both[c] = hidden[...]
     pick = hits[0] + hits[1]
     theirs.wait_recv()
     rows = jnp.dot(pick, both[...].reshape(2 * ROWS, D), preferred_element_type=F32)
     cells[...] = rows.astype(BF).reshape(PLACES, 8, 128).reshape(NY, NZ, SUB, 128)
-    keep = pltpu.make_async_copy(cells.at[y, z], routed.at[z, x, y], local_sem.at[9])
-    keep.start()
+    routed[z, x, y] = cells[y, z]
 
     direct, sideways, relays, begun, closing = [], [], [], [], []
     returned = sends.slot()
@@ -528,8 +530,6 @@
                 start(src, routed.at[z, x, y], me.at(dy=dy, dz=dz), direct[i])
 
     def spread(i):
-        if ORDER[i] == 0:
-            keep.wait()
         sends.arrive(direct[i], (NY - (ORDER[i] == 0)) * SUB)
         block = routed.at[group(i), x]
         sideways.append((start(block, block, xr), start(block, block, xl)))
@@ -617,18 +617,22 @@
     sends.arrive(returned, (NY * NZ - 1) * SUB)
 
     rows = back[...].reshape(PLACES * 8, 128).reshape(PLACES, 8, 128).reshape(PLACES, D)
+
+    def take(k, core):
+        columns = pl.ds(pl.multiple_of(core * ROWS, ROWS), ROWS)
+        return lax.dot_general(
+            hits[k, :, columns], rows, (((0,), (0,)), ((), ())), preferred_element_type=F32
+        )
+
     given = []
     for k in range(TOP):
-        taken = lax.dot_general(
-            hits[k], rows, (((0,), (0,)), ((), ())), preferred_element_type=F32
-        )
-        picked[k] = taken.astype(BF).reshape(2, ROWS, D)
-        given.append(start(picked.at[k, 1 - c], inbox.at[k], sib))
+        picked[k] = take(k, 1 - c).astype(BF)
+        given.append(start(picked.at[k], inbox.at[k], sib))
     result = second[...].astype(F32)
+    mine = [take(k, c) for k in range(TOP)]
     for k in range(TOP):
         given[k].wait_recv()
-        value = picked[k, c].astype(F32) + inbox[k].astype(F32)
-        result = result + gates[:, k : k + 1] * value
+        result = result + gates[:, k : k + 1] * (mine[k] + inbox[k].astype(F32))
     block_out[...] = result.astype(BF)
 
 
@@ -642,7 +646,7 @@
         + [
             pltpu.SemaphoreType.DMA((SEND_SLOTS,)),
             pltpu.SemaphoreType.DMA((RECV_SLOTS,)),
-            pltpu.SemaphoreType.DMA((10,)),
+            pltpu.SemaphoreType.DMA((9,)),
         ],
         compiler_params=pltpu.CompilerParams(
             collective_id=0, has_side_effects=True, vmem_limit_bytes=60 << 20

time: 108 us -> 108 us (level)
  no operation moved by 1% of the time
where the time goes in v7:
time: 108 us; the launch traced here: 106 us
  Pallas kernels  104 us (96%)
  other arithmetic  1.68 us (2%)
    pallas_call x1, Pallas kernels, local(): pl.pallas_call(block_kernel, out_shape=jax.ShapeDtypeStruct((ROWS, D), BF...  104 us

profile of v7, /device:TPU:7, one launch (start us, length us, event | category | flops | bytes accessed | tf_op | source)
XLA Modules:
  0.0 105.7 jit_solution(7845229286575913575)
XLA Ops:
  0.0 104.1 %block.1 = bf16[128,1024]{1,0:T(8,128)(2,1)} custom-call(s32[1,4]{1,0:T(1,128)} %lengths.1, s32[2,128]{1,0:T(2,128)} %bitcast.3, bf16[128,1024]{1,0:T(8,128)(2,1)} %frames.1, f32[31,1024]{1,0:T(8,128)} %conv_w.1, bf16[64,1024]{1,0:T(8,128)(2,1)} %bitcast.2, bf16[32,3072]{1,0:T(8,128)(2,1)} %wqkv.1, bf16[32,1024]{1,0:T(8,128)(2,1)} %wout.1, ...), custom_call_target="tpu_custom_call" | custom-call | tf_op jit(solution)/shard_map/block/pallas_call | solution.py:640
  104.1 1.7 %broadcast_maximum_fusion = bf16[128,1024]{1,0:T(8,128)(2,1)} fusion(bf16[128,1024]{1,0:T(8,128)(2,1)} %block.1), kind=kLoop, calls=%fused_computation | loop fusion | flops 131072 | bytes 524288 | tf_op jit(solution)/shard_map/max | solution.py:656

commit v8 on v7

--- a/solution.py
+++ b/solution.py
@@ -289,12 +289,14 @@
     loads = [
         pltpu.make_async_copy(src, dst, local_sem.at[n]) for n, (src, dst) in enumerate(loads)
     ]
-    for copy in loads:
-        copy.start()
+    for n in (6, 7, 8, 1, 0):
+        loads[n].start()
     greet(plane_peers(me) + others)
     sends = Sends(send_sem, recv_sem, ref.ruler)
     for copy in loads[1:2] + loads[6:]:
         copy.wait()
+    for copy in loads[2:6]:
+        copy.start()
     theirs = front(me, sends, others, loads, lengths, ids, wup, wdn, ref)
     for copy in loads[2:4]:
         copy.wait()

time: 108 us -> 107 us (level)
  no operation moved by 1% of the time
where the time goes in v8:
time: 107 us; the launch traced here: 106 us
  Pallas kernels  104 us (97%)
  other arithmetic  1.68 us (2%)
    pallas_call x1, Pallas kernels, local(): pl.pallas_call(block_kernel, out_shape=jax.ShapeDtypeStruct((ROWS, D), BF...  104 us

profile of v8, /device:TPU:7, one launch (start us, length us, event | category | flops | bytes accessed | tf_op | source)
XLA Modules:
  0.0 105.8 jit_solution(1571092754534104469)
XLA Ops:
  0.0 104.1 %block.1 = bf16[128,1024]{1,0:T(8,128)(2,1)} custom-call(s32[1,4]{1,0:T(1,128)} %lengths.1, s32[2,128]{1,0:T(2,128)} %bitcast.3, bf16[128,1024]{1,0:T(8,128)(2,1)} %frames.1, f32[31,1024]{1,0:T(8,128)} %conv_w.1, bf16[64,1024]{1,0:T(8,128)(2,1)} %bitcast.2, bf16[32,3072]{1,0:T(8,128)(2,1)} %wqkv.1, bf16[32,1024]{1,0:T(8,128)(2,1)} %wout.1, ...), custom_call_target="tpu_custom_call" | custom-call | tf_op jit(solution)/shard_map/block/pallas_call | solution.py:642
  104.1 1.7 %broadcast_maximum_fusion = bf16[128,1024]{1,0:T(8,128)(2,1)} fusion(bf16[128,1024]{1,0:T(8,128)(2,1)} %block.1), kind=kLoop, calls=%fused_computation | loop fusion | flops 131072 | bytes 524288 | tf_op jit(solution)/shard_map/max | solution.py:658
